TPU v7x, 128 devices: a whole 4x4x4 slice. The times are simulated.
128 devices in a mesh: tm: 16 (over x, y), rows: 8 (over z, core).
Axes of the slice: x: 4, y: 4, z: 4, core: 2. Of those that a mesh axis runs over, the one named last changes fastest.
Arguments:
- inputs: bfloat16 [32, 32, 128, 256], P('tm', 'rows'), may hold values from -6 to 6
- in_weight: bfloat16 [3, 3, 256, 256], replicated, may hold values from -0.125 to 0.125
- out_weight: bfloat16 [3, 3, 256, 256], replicated, may hold values from -0.0625 to 0.0625
- skip_gain: float32 [256], replicated, may hold values from 0.5 to 1.5
- rates: float32 [256], replicated, may hold values from 0.002 to 1
- step_sizes: float32 [32], P('tm'), may hold values from 0.25 to 4
- cotangent: bfloat16 [32, 32, 128, 256], P('tm', 'rows'), may hold values from -6 to 6
Outputs:
- outputs: bfloat16 [32, 32, 128, 256], P('tm', 'rows')
- grad_inputs: bfloat16 [32, 32, 128, 256], P('tm', 'rows')
- grad_in_weight: float32 [3, 3, 256, 256], replicated
- grad_out_weight: float32 [3, 3, 256, 256], replicated
- grad_skip: float32 [256], replicated
- grad_rates: float32 [256], replicated
- grad_steps: float32 [32], P('tm')
All inputs are finite; a program needn't handle non-finite values.
Results may differ from a plain program's by a relative error of at most 0.015.
Values may be sent and summed in bfloat16 or wider, within the bound.
No kernel may reach another device: no remote copies, remote signals or barrier semaphores. Data moves between devices by JAX's collectives and lax.ppermute only.
A program may use at most 128 MiB of HBM per device.

v0:
```python
import math

import jax
import jax.numpy as jnp
from jax import lax
from jax.sharding import PartitionSpec as P


def extended(shard, sides, width):
    for axis, dim in sides:
        count, length = (lax.axis_size(axis), shard.shape[dim])
        up = [(i, (i + 1) % count) for i in range(count - 1)]
        down = [(j, i) for i, j in up]
        last = lax.slice_in_dim(shard, length - width, length, axis=dim)
        initial = lax.slice_in_dim(shard, 0, width, axis=dim)
        before = lax.ppermute(last, axis, up)
        after = lax.ppermute(initial, axis, down)
        shard = jnp.concatenate([before, shard, after], axis=dim)
    return shard


def prefix(shard, axis, combine, identity, reverse):
    count, place = (lax.axis_size(axis), lax.axis_index(axis))
    everything = jax.tree.map(lambda part: lax.all_gather(part, axis), shard)
    start = jax.tree.map(
        lambda part, zero: jnp.broadcast_to(jnp.asarray(zero, part.dtype), part.shape),
        shard,
        identity,
    )

    def turn(k, before):
        at = count - 1 - k if reverse else k
        reached = at > place if reverse else at < place
        new = combine(before, jax.tree.map(lambda part: part[at], everything))
        return jax.tree.map(lambda a, b: jnp.where(reached, a, b), new, before)

    return lax.fori_loop(0, count, turn, start)


def shifted(padded, row_tap, col_tap, height, width):
    return padded[:, row_tap : row_tap + height, col_tap : col_tap + width, :]


def with_rims(field):
    banded = extended(field, (("rows", 1),), 1)
    return jnp.pad(banded, ((0, 0), (0, 0), (1, 1), (0, 0)))


def conv_taps(padded, weight, flipped):
    frames, rows_pad, cols_pad, chans = padded.shape
    height = rows_pad - 2
    width = cols_pad - 2
    result = None
    for row_tap in range(3):
        for col_tap in range(3):
            if flipped:
                window = shifted(padded, 2 - row_tap, 2 - col_tap, height, width)
                matrix = weight[row_tap, col_tap].T
            else:
                window = shifted(padded, row_tap, col_tap, height, width)
                matrix = weight[row_tap, col_tap]
            term = jnp.dot(window.reshape(-1, chans), matrix, preferred_element_type=jnp.float32)
            result = term if result is None else result + term
    return result.reshape(frames, height, width, -1)


def weight_taps(plain, padded_out):
    frames, height, width, chans = plain.shape
    flat = plain.reshape(-1, chans)
    grid_rows = []
    for row_tap in range(3):
        grid_cols = []
        for col_tap in range(3):
            window = shifted(padded_out, 2 - row_tap, 2 - col_tap, height, width).reshape(
                -1, padded_out.shape[3]
            )
            grid_cols.append(
                lax.dot_general(
                    flat, window, (((0,), (0,)), ((), ())), preferred_element_type=jnp.float32
                )
            )
        grid_rows.append(jnp.stack(grid_cols))
    return jnp.stack(grid_rows)


def combine(earlier, later):
    return (earlier[0] * later[0], later[0] * earlier[1] + later[1])


def on_device(inputs, in_weight, out_weight, skip_gain, rates, step_sizes, cotangent):
    frames, height, width, chans = inputs.shape
    states_ch = in_weight.shape[3]
    frames_all = frames * lax.axis_size("tm")
    band_count = lax.axis_size("rows")
    rows_all = height * band_count
    scale = 1.0 / math.sqrt(frames_all * rows_all * width)
    identity = (
        jnp.ones((states_ch,), jnp.float32),
        jnp.zeros((height, width, states_ch), jnp.float32),
    )
    driven = conv_taps(with_rims(inputs), in_weight, False)
    decays = jnp.exp(-rates[None, :] * step_sizes[:, None])
    running = jnp.zeros((height, width, states_ch), jnp.float32)
    local_states = []
    for frame in range(frames):
        running = decays[frame] * running + driven[frame]
        local_states.append(running)
    block_decay = jnp.prod(decays, axis=0)
    carry_decay, carry_state = prefix((block_decay, running), "tm", combine, identity, False)
    cumulative = jnp.cumprod(decays, axis=0)
    states = jnp.stack(local_states) + cumulative[:, None, None, :] * carry_state[None]
    earlier = jnp.concatenate([carry_state[None], states[:-1]], axis=0)
    state_bf = states.astype(jnp.bfloat16)
    pre_act = conv_taps(with_rims(state_bf), out_weight, False) + skip_gain * inputs.astype(
        jnp.float32
    )
    outputs = jax.nn.gelu(pre_act).astype(jnp.bfloat16)
    grad_z = jax.vjp(jax.nn.gelu, pre_act)[1](cotangent.astype(jnp.float32))[0]
    gz_pad = with_rims(grad_z.astype(jnp.bfloat16))
    out_part = weight_taps(state_bf, gz_pad) * scale
    grad_state = conv_taps(gz_pad, out_weight, True)
    local_adjoint = [None] * frames
    running = grad_state[frames - 1]
    local_adjoint[frames - 1] = running
    frame = 0
    running = grad_state[frame] + decays[frame + 1] * running
    local_adjoint[frame] = running
    sent_back = decays[0] * local_adjoint[0]
    later_decay, incoming = prefix((block_decay, sent_back), "tm", combine, identity, True)
    tail_products = [None] * frames
    product_now = jnp.ones((states_ch,), jnp.float32)
    tail_products[frames - 1] = product_now
    frame = 0
    product_now = product_now * decays[frame + 1]
    tail_products[frame] = product_now
    adjoint = jnp.stack(local_adjoint) + jnp.stack(tail_products)[:, None, None, :] * incoming[None]
    adj_pad = with_rims(adjoint.astype(jnp.bfloat16))
    grad_inputs = (conv_taps(adj_pad, in_weight, True) + skip_gain * grad_z).astype(jnp.bfloat16)
    in_part = weight_taps(inputs, adj_pad) * scale
    skip_part = jnp.sum(grad_z * inputs.astype(jnp.float32), axis=(0, 1, 2)) * scale
    coupling = jnp.sum(adjoint * earlier, axis=(1, 2))
    rate_part = -jnp.sum(coupling * step_sizes[:, None] * decays, axis=0) * scale
    step_part = -jnp.sum(coupling * rates[None, :] * decays, axis=1) / math.sqrt(
        rows_all * width * states_ch
    )
    offset = lax.axis_index("tm") * frames
    step_vector = lax.dynamic_update_slice(
        jnp.zeros((frames_all,), jnp.float32), step_part, (offset,)
    )
    grad_in_weight, grad_out_weight, grad_skip, grad_rates, step_total = lax.psum(
        (in_part, out_part, skip_part, rate_part, step_vector), ("tm", "rows")
    )
    grad_steps = lax.dynamic_slice(step_total, (offset,), (frames,))
    return (
        outputs,
        grad_inputs,
        grad_in_weight,
        grad_out_weight,
        grad_skip,
        grad_rates,
        grad_steps,
    )


def solution(mesh):
    placed = (P("tm", "rows", None, None), P(), P(), P(), P(), P("tm"), P("tm", "rows", None, None))
    return jax.shard_map(
        on_device,
        mesh=mesh,
        in_specs=placed,
        out_specs=(
            P("tm", "rows", None, None),
            P("tm", "rows", None, None),
            P(),
            P(),
            P(),
            P(),
            P("tm"),
        ),
        check_vma=False,
    )
```

profile of v0, /device:TPU:1, one launch (start us, length us, event | category | flops | bytes accessed | tf_op | source)
XLA Modules:
  0.0 542.5 jit_solution(8414759142955961919)
XLA Ops:
  8.2 4.9 collective-permute-start
  13.2 1.9 collective-permute-start.1
  16.5 2.9 collective-permute-done.1
  27.0 18.9 %all-gather.1 = f32[16,1,256]{2,1,0:T(1,128)S(1)} all-gather(f32[1,1,256]{2,1,0:T(1,128)S(1)} %bitcast.385), channel_id=2, replica_groups=mesh['tm'=16,'rows'=8] {'tm'}, dimensions={0}, use_global_device_ids=true | all-gather | bytes 17408 | tf_op jit(solution)/shard_map/all_gather | solution.py:24
  45.9 53.2 %all-gather.5.cloned.1.call-done = f32[16,4,128,256]{3,2,1,0:T(8,128)} async-done(((f32[1,4,128,256]{3,2,1,0:T(8,128)}), f32[16,4,128,256]{3,2,1,0:T(8,128)}) %all-gather.5.cloned.1.call-update) | async-done | bytes 8388624 | tf_op jit(solution)/shard_map/all_gather | solution.py:24
  99.1 24.3 %while.30 = (s32[]{:T(128)}, f32[4,128,256]{2,1,0:T(8,128)S(1)}, s32[]{:T(128)}, f32[16,256]{1,0:T(8,128)S(1)}, f32[16,4,128,256]{3,2,1,0:T(8,128)}, /*index=5*/s32[]{:T(128)}, s32[]{:T(128)}) while((s32[]{:T(128)}, f32[4,128,256]{2,1,0:T(8,128)S(1)}, s32[]{:T(128)}, f32[16,256]{1,0:T(8,128)S(1)}, f32[16,4,128,256]{3,2,1,0:T(8,128)}, ...), condition=%wide.region_3.4_spmd.clone, body=%wide.region_2.3_spmd.clone.sunk | while | flops 524292 | bytes 1576049 | solution.py:37
  100.6 1.5 fusion.195
  102.1 1.5 fusion.195
  103.7 1.5 fusion.195
  105.2 1.5 fusion.195
  106.7 1.5 fusion.195
  108.2 1.5 fusion.195
  109.7 1.5 fusion.195
  111.3 1.5 fusion.195
  112.8 1.5 fusion.195
  114.3 1.5 fusion.195
  115.8 1.5 fusion.195
  117.3 1.5 fusion.195
  118.9 1.5 fusion.195
  120.4 1.5 fusion.195
  121.9 1.5 fusion.195
  124.8 3.7 collective-permute-start.2
  128.6 1.9 collective-permute-start.3
  131.5 3.4 collective-permute-done.3
  137.8 1.8 fusion.125
  139.5 2.0 copy.86
  143.6 2.1 copy.81
  153.8 1.8 fusion.8
  155.7 1.9 collective-permute-start.4
  157.6 2.6 collective-permute-start.5
  160.3 3.7 collective-permute-done.5
  172.1 2.0 copy.90
  174.2 1.9 slice.363
  180.1 1.6 maximum_multiply_fusion.1
  181.8 62.1 %all-gather.7.cloned.1.call-done = f32[16,4,128,256]{3,2,1,0:T(8,128)} async-done(((f32[1,4,128,256]{3,2,1,0:T(8,128)}), f32[16,4,128,256]{3,2,1,0:T(8,128)}) %all-gather.7.cloned.1.call-update) | async-done | bytes 8388624 | tf_op jit(solution)/shard_map/all_gather | solution.py:24
  243.8 24.5 %while.31 = (s32[]{:T(128)}, f32[4,128,256]{2,1,0:T(8,128)S(1)}, s32[]{:T(128)}, f32[16,256]{1,0:T(8,128)S(1)}, f32[16,4,128,256]{3,2,1,0:T(8,128)}, /*index=5*/s32[]{:T(128)}, s32[]{:T(128)}, s32[]{:T(128)}, s32[]{:T(128)}) while((s32[]{:T(128)}, f32[4,128,256]{2,1,0:T(8,128)S(1)}, s32[]{:T(128)}, f32[16,256]{1,0:T(8,128)S(1)}, ...), condition=%wide.region_5.6_spmd.clone, body=%wide.region_4.5_spmd.clone.sunk | while | flops 524296 | bytes 1576111 | solution.py:37
  243.8 1.6 fusion.196
  245.4 1.5 fusion.196
  247.0 1.5 fusion.196
  248.5 1.5 fusion.196
  250.0 1.5 fusion.196
  251.5 1.5 fusion.196
  253.1 1.5 fusion.196
  254.6 1.5 fusion.196
  256.1 1.5 fusion.196
  259.2 1.5 fusion.196
  266.8 1.5 fusion.196
  269.3 1.6 fusion.18
  272.2 64.7 %all-reduce.5 = (f32[256]{0:T(256)}, f32[256]{0:T(256)}, f32[32]{0:T(128)S(1)}) all-reduce(f32[256]{0:T(256)S(1)} %get-tuple-element.403, f32[256]{0:T(256)S(1)} %get-tuple-element.402, f32[32]{0:T(128)S(1)} %multiply_dynamic-update-slice_fusion), channel_id=1, replica_groups=mesh['tm'=16,'rows'=8] {'tm','rows'}, use_global_device_ids=true, to_apply=%region_9.10 | all-reduce | flops 544 | bytes 4352 | tf_op jit(solution)/shard_map/psum | solution.py:150
  337.6 3.4 collective-permute-start.6
  340.9 2.1 collective-permute-start.7
  343.4 3.8 collective-permute-done.7
  354.2 2.4 fusion.124
  360.2 2.1 copy.100
  362.3 2.1 copy.98
  364.4 2.1 copy.97
  366.5 2.1 copy.95
  368.5 2.0 copy.94
  370.6 2.0 copy.92
  372.6 2.4 fusion.67
  376.7 1.6 maximum_multiply_fusion
  386.5 144.3 %all-reduce.9.cloned.1.call-done = (f32[3,3,256,256]{2,3,1,0:T(8,128)}, f32[3,3,256,256]{2,3,1,0:T(8,128)}) async-done(((f32[3,3,256,256]{2,3,1,0:T(8,128)}, f32[3,3,256,256]{2,3,1,0:T(8,128)}), (f32[3,3,256,256]{2,3,1,0:T(8,128)}, f32[3,3,256,256]{2,3,1,0:T(8,128)})) %all-reduce.9.cloned.1.call-update) | async-done | bytes 4718608 | tf_op jit(solution)/shard_map/psum | solution.py:150
  530.8 3.2 copy.111
  534.0 1.9 copy.112
  (243 shorter events, 69.8 us)
Async XLA Ops:
  7.2 91.9 %all-gather.5.cloned.1.call-start = ((), (), s32[]{:S(2)}) async-start(), calls=%async_computation | async-start | bytes 8912896 | tf_op jit(solution)/shard_map/all_gather | solution.py:24
  8.2 8.3 %collective-permute-start = (bf16[2,1,128,256]{3,2,1,0:T(8,128)(2,1)S(1)}, bf16[2,1,128,256]{3,2,1,0:T(8,128)(2,1)S(1)}, u32[]{:S(2)}, u32[]{:S(2)}) collective-permute-start(bf16[2,1,128,256]{3,2,1,0:T(8,128)(2,1)S(1)} %get-tuple-element.392), channel_id=1, source_target_pairs={{0,1},{1,2},{2,3},{3,4},{4,5},{5,6},{6,7},{8,9},{9,10},{10,11},{11... | collective-permute-start | bytes 393224 | tf_op jit(solution)/shard_map/ppermute | solution.py:16
  13.2 6.3 %collective-permute-start.1 = (bf16[2,1,128,256]{3,2,1,0:T(8,128)(2,1)S(1)}, bf16[2,1,128,256]{3,2,1,0:T(8,128)(2,1)S(1)}, u32[]{:S(2)}, u32[]{:S(2)}) collective-permute-start(bf16[2,1,128,256]{3,2,1,0:T(8,128)(2,1)S(1)} %get-tuple-element.393), channel_id=1, source_target_pairs={{1,0},{2,1},{3,2},{4,3},{5,4},{6,5},{7,6},{9,8},{10,9},{11,10},{12... | collective-permute-start | bytes 393224 | tf_op jit(solution)/shard_map/ppermute | solution.py:17
  20.7 1.3 copy-start.11
  22.0 1.0 copy-start
  26.9 216.9 %all-gather.7.cloned.1.call-start = ((), (), s32[]{:S(2)}) async-start(), calls=%async_computation.1 | async-start | bytes 8912896 | tf_op jit(solution)/shard_map/all_gather | solution.py:24
  123.6 1.2 copy-start.5
  124.8 6.7 %collective-permute-start.2 = (bf16[2,1,128,256]{2,3,1,0:T(8,128)(2,1)S(1)}, bf16[2,1,128,256]{2,3,1,0:T(8,128)(2,1)S(1)}, u32[]{:S(2)}, u32[]{:S(2)}) collective-permute-start(bf16[2,1,128,256]{2,3,1,0:T(8,128)(2,1)S(1)} %get-tuple-element.388), channel_id=1, source_target_pairs={{0,1},{1,2},{2,3},{3,4},{4,5},{5,6},{6,7},{8,9},{9,10},{10,11},{11... | collective-permute-start | bytes 393224 | tf_op jit(solution)/shard_map/ppermute | solution.py:16
  128.6 6.3 %collective-permute-start.3 = (bf16[2,1,128,256]{2,3,1,0:T(8,128)(2,1)S(1)}, bf16[2,1,128,256]{2,3,1,0:T(8,128)(2,1)S(1)}, u32[]{:S(2)}, u32[]{:S(2)}) collective-permute-start(bf16[2,1,128,256]{2,3,1,0:T(8,128)(2,1)S(1)} %get-tuple-element.389), channel_id=1, source_target_pairs={{1,0},{2,1},{3,2},{4,3},{5,4},{6,5},{7,6},{9,8},{10,9},{11,10},{12... | collective-permute-start | bytes 393224 | tf_op jit(solution)/shard_map/ppermute | solution.py:17
  143.6 3.4 copy-start.9
  147.0 1.7 copy-start.28
  148.7 1.0 copy-start.27
  149.0 1.1 copy-start.21
  150.0 1.1 copy-start.26
  150.4 1.1 copy-start.25
  151.4 1.1 copy-start.22
  151.8 1.1 copy-start.24
  152.8 1.1 copy-start.39
  152.8 1.1 copy-start.40
  155.6 4.6 copy-start.1
  155.7 4.5 collective-permute-start.4
  157.6 6.3 %collective-permute-start.5 = (bf16[2,1,128,256]{3,2,1,0:T(8,128)(2,1)S(1)}, bf16[2,1,128,256]{3,2,1,0:T(8,128)(2,1)S(1)}, u32[]{:S(2)}, u32[]{:S(2)}) collective-permute-start(bf16[2,1,128,256]{3,2,1,0:T(8,128)(2,1)S(1)} %get-tuple-element.385), channel_id=1, source_target_pairs={{1,0},{2,1},{3,2},{4,3},{5,4},{6,5},{7,6},{9,8},{10,9},{11,10},{12... | collective-permute-start | bytes 393224 | tf_op jit(solution)/shard_map/ppermute | solution.py:17
  164.2 1.3 copy-start.10
  166.2 0.8 copy-start.3
  166.2 2.1 copy-start.7
  174.1 356.7 %all-reduce.9.cloned.1.call-start = ((), (), s32[]{:S(2)}) async-start(), calls=%async_computation.2 | async-start | bytes 9437184 | tf_op jit(solution)/shard_map/psum | solution.py:150
  174.2 2.3 copy-start.8
  177.2 1.0 copy-start.4
  243.8 25.5 %copy-start.6 = (f32[4,128,256]{1,2,0:T(8,128)S(1)}, f32[4,128,256]{1,2,0:T(8,128)}, u32[]{:S(2)}) copy-start(f32[4,128,256]{1,2,0:T(8,128)} %copy-done.5) | copy-start | bytes 1572868
  243.8 25.5 %copy-start.15 = (f32[1,4,128,256]{2,3,1,0:T(8,128)S(1)}, f32[1,4,128,256]{2,3,1,0:T(8,128)}, u32[]{:S(2)}) copy-start(f32[1,4,128,256]{2,3,1,0:T(8,128)} %get-tuple-element.342) | copy-start | bytes 1572868
  270.9 1.1 copy-start.41
  270.9 1.1 copy-start.42
  337.6 5.8 %collective-permute-start.6 = (bf16[2,1,128,256]{2,3,1,0:T(8,128)(2,1)S(1)}, bf16[2,1,128,256]{2,3,1,0:T(8,128)(2,1)S(1)}, u32[]{:S(2)}, u32[]{:S(2)}) collective-permute-start(bf16[2,1,128,256]{2,3,1,0:T(8,128)(2,1)S(1)} %get-tuple-element.380), channel_id=1, source_target_pairs={{0,1},{1,2},{2,3},{3,4},{4,5},{5,6},{6,7},{8,9},{9,10},{10,11},{11... | collective-permute-start | bytes 393224 | tf_op jit(solution)/shard_map/ppermute | solution.py:16
  340.9 6.3 %collective-permute-start.7 = (bf16[2,1,128,256]{2,3,1,0:T(8,128)(2,1)S(1)}, bf16[2,1,128,256]{2,3,1,0:T(8,128)(2,1)S(1)}, u32[]{:S(2)}, u32[]{:S(2)}) collective-permute-start(bf16[2,1,128,256]{2,3,1,0:T(8,128)(2,1)S(1)} %get-tuple-element.381), channel_id=1, source_target_pairs={{1,0},{2,1},{3,2},{4,3},{5,4},{6,5},{7,6},{9,8},{10,9},{11,10},{12... | collective-permute-start | bytes 393224 | tf_op jit(solution)/shard_map/ppermute | solution.py:17
  343.4 13.3 %copy-start.37 = (bf16[2,1,128,256]{2,3,1,0:T(8,128)(2,1)}, bf16[2,1,128,256]{2,3,1,0:T(8,128)(2,1)S(1)}, u32[]{:S(2)}) copy-start(bf16[2,1,128,256]{2,3,1,0:T(8,128)(2,1)S(1)} %collective-permute-done.6) | copy-start | bytes 393220
  347.2 9.5 %copy-start.35 = (bf16[2,1,128,256]{2,3,1,0:T(8,128)(2,1)}, bf16[2,1,128,256]{2,3,1,0:T(8,128)(2,1)S(1)}, u32[]{:S(2)}) copy-start(bf16[2,1,128,256]{2,3,1,0:T(8,128)(2,1)S(1)} %collective-permute-done.7) | copy-start | bytes 393220
  356.7 2.1 copy-start.12
  372.6 2.4 copy-start.38
  372.6 2.8 copy-start.33
  372.6 2.8 copy-start.34
  375.1 0.9 copy-start.36
  375.4 1.0 copy-start.29
  375.4 1.0 copy-start.30
  375.4 1.1 copy-start.31
  375.4 1.2 copy-start.32
  378.3 1.2 copy-start.13
  379.6 1.5 copy-start.23
  381.0 1.0 copy-start.16
  381.4 1.1 copy-start.20
  382.4 1.1 copy-start.19
  382.8 1.2 copy-start.17
  383.8 1.1 copy-start.18
  384.3 1.3 copy-start.2
  530.8 3.2 copy-start.14
Sparse Core Ops, SparseCore 0:
  27.0 72.0 all-gather.4
  174.2 69.5 all-gather.6
  378.5 152.2 all-reduce.8
where the time goes:
time: 545 us; the launch traced here: 542 us
  waiting for transfers between devices  273 us (50%)
  blocking collectives  83.6 us (15%)
  other arithmetic  62.9 us (12%)
  local copies, waits for them, and re-layouts  57.4 us (11%)
  matrix products  26.8 us (5%)
  starting transfers between devices  22.7 us (4%)
  between operations  14.7 us (3%)
    psum x1, waiting for transfers between devices, on_device(): lax.psum((in_part, out_part, skip_part, rate_part, step_vector), ('tm', '...  144 us
    all_gather x2, waiting for transfers between devices, prefix(): everything = jax.tree.map(lambda part: lax.all_gather(part, axis), shard)  115 us
    psum x1, blocking collectives, on_device(): lax.psum((in_part, out_part, skip_part, rate_part, step_vector), ('tm', '...  64.7 us
    select_n x32, other arithmetic, turn(): return jax.tree.map(lambda a, b: jnp.where(reached, a, b), new, before)  47.5 us
    slice x20, local copies, waits for them, and re-layouts, shifted(): return padded[:, row_tap:row_tap + height, col_tap:col_tap + width, :]  29 us
    all_gather x1, blocking collectives, prefix(): everything = jax.tree.map(lambda part: lax.all_gather(part, axis), shard)  18.9 us
    dot_general x36, matrix products, conv_taps(): jnp.dot(window.reshape(-1, chans), matrix, preferred_element_type=jnp.flo...  16.6 us
    unnamed x89, local copies, waits for them, and re-layouts  15.5 us
  transfers between devices with their start and end apart: 11, of which 7 were waited for; matrix products, arithmetic and copies ran while one was open for 3% of the time, Pallas kernels for 0%

commit v1 on v0

v1 whole, which is shorter than its diff:
```python
import functools
import math

import jax
import jax.numpy as jnp
from jax import lax
from jax.experimental import pallas as pl
from jax.experimental.pallas import tpu as pltpu
from jax.sharding import Mesh, PartitionSpec as P

BF, F32 = jnp.bfloat16, jnp.float32
VM = pl.BlockSpec(memory_space=pltpu.VMEM)
SM = pl.BlockSpec(memory_space=pltpu.SMEM)
FRAMES, HEIGHT, WIDTH, CHANS = 2, 4, 128, 256
BLOCKS = 16
PLACES = HEIGHT * WIDTH // BLOCKS
CHIPS = 64


def sds(shape, dtype):
    return jax.ShapeDtypeStruct(shape, dtype)


def call(body, outs, ins, flops=0):
    nbytes = sum(math.prod(o.shape) * o.dtype.itemsize for o in outs)
    nbytes += sum(math.prod(i.shape) * i.dtype.itemsize for i in ins)
    specs = [SM if i.ndim == 1 else VM for i in ins]
    return pl.pallas_call(
        body,
        out_shape=outs,
        in_specs=specs,
        out_specs=[VM] * len(outs),
        compiler_params=pltpu.CompilerParams(vmem_limit_bytes=40 << 20),
        cost_estimate=pl.CostEstimate(flops=flops, bytes_accessed=nbytes, transcendentals=0),
    )(*ins)


CONV_FLOPS = 2 * 9 * FRAMES * HEIGHT * WIDTH * CHANS * CHANS


def col_shift(v, by):
    turned = pltpu.roll(v, by % WIDTH, 1)
    at = lax.broadcasted_iota(jnp.int32, v.shape, 1)
    return jnp.where(at == (0 if by == 1 else WIDTH - 1), 0.0, turned)


def padded(t, above, mid, below):
    return jnp.concatenate([above[t], mid[t], below[t]], axis=0)


def conv(rows, weight, flipped):
    lhs = jnp.concatenate([rows[a : a + HEIGHT] for a in range(3)], axis=-1)
    lhs = lhs.reshape(HEIGHT * WIDTH, 3 * CHANS)
    parts = []
    for b in range(3):
        if flipped:
            rhs = jnp.concatenate([weight[2 - a, 2 - b] for a in range(3)], axis=1)
            y = lax.dot_general(lhs, rhs, (((1,), (1,)), ((), ())), preferred_element_type=F32)
        else:
            rhs = jnp.concatenate([weight[a, b] for a in range(3)], axis=0)
            y = jnp.dot(lhs, rhs, preferred_element_type=F32)
        parts.append(y.reshape(HEIGHT, WIDTH, CHANS))
    return parts[1] + col_shift(parts[0], 1) + col_shift(parts[2], -1)


def transposed_body(v_ref, out_ref):
    lane = lax.broadcasted_iota(jnp.int32, (CHANS, WIDTH), 1)
    for t in range(FRAMES):
        for h in range(HEIGHT):
            flat = v_ref[t, h].astype(F32).T
            at = pl.ds((t * HEIGHT + h) * WIDTH, WIDTH)
            left = jnp.where(lane == 0, 0.0, pltpu.roll(flat, 1, 1))
            right = jnp.where(lane == WIDTH - 1, 0.0, pltpu.roll(flat, WIDTH - 1, 1))
            out_ref[0:CHANS, at] = left.astype(BF)
            out_ref[CHANS : 2 * CHANS, at] = flat.astype(BF)
            out_ref[2 * CHANS : 3 * CHANS, at] = right.astype(BF)


def transposed(v):
    return call(transposed_body, [sds((3 * CHANS, FRAMES * HEIGHT * WIDTH), BF)], [v])[0]


def decay(rates_ref, step):
    return jnp.exp(-rates_ref[...] * step)


def drive_body(steps, x, above, below, weight, rates, local, send):
    d1 = decay(rates, steps[1])
    first = conv(padded(0, above, x, below), weight, False)
    local[0] = first
    last = d1 * first + conv(padded(1, above, x, below), weight, False)
    local[1] = last
    send[:, 0:PLACES, :] = last.reshape(BLOCKS, PLACES, CHANS).astype(BF)
    total = jnp.full((BLOCKS, 16, CHANS), steps[0] + steps[1], F32)
    row = lax.broadcasted_iota(jnp.int32, total.shape, 1)
    one = total.astype(BF).astype(F32)
    two = (total - one).astype(BF).astype(F32)
    three = total - one - two
    send[:, PLACES : PLACES + 16, :] = jnp.where(
        row == 0, one, jnp.where(row == 1, two, jnp.where(row == 2, three, 0.0))
    ).astype(BF)


def forward_scan_body(got, rates, send, block_decays):
    carry = jnp.zeros((PLACES, CHANS), F32)
    for k in range(BLOCKS):
        send[k] = carry.astype(BF)
        span = jnp.sum(got[k, PLACES : PLACES + 16, :].astype(F32), axis=0, keepdims=True)
        d = jnp.exp(-rates[...] * span)
        block_decays[pl.ds(k, 1), :] = d
        carry = d * carry + got[k, 0:PLACES, :].astype(F32)


def backward_scan_body(got, block_decays, send):
    carry = jnp.zeros((PLACES, CHANS), F32)
    for k in reversed(range(BLOCKS)):
        send[k] = carry.astype(BF)
        carry = block_decays[pl.ds(k, 1), :] * carry + got[k].astype(F32)


def states_body(steps, local, carry, rates, state, first, last, state_f):
    d0, d1 = decay(rates, steps[0]), decay(rates, steps[1])
    c = carry[...].reshape(HEIGHT, WIDTH, CHANS).astype(F32)
    s0 = local[0] + d0 * c
    s1 = local[1] + (d0 * d1) * c
    state_f[...] = s0
    for t, s in enumerate((s0, s1)):
        s = s.astype(BF)
        state[t] = s
        first[t] = s[0:1]
        last[t] = s[HEIGHT - 1 :]


GELU_A = math.sqrt(2 / math.pi)


def output_body(state, above, below, x, cot, weight, gain, out, gz_f, gz, first, last, skip):
    total = jnp.zeros((1, CHANS), F32)
    for t in range(FRAMES):
        xt = x[t].astype(F32)
        z = conv(padded(t, above, state, below), weight, False) + gain[...] * xt
        th = jnp.tanh(GELU_A * (z + 0.044715 * (z * z * z)))
        half = 0.5 * (1.0 + th)
        out[t] = (z * half).astype(BF)
        slope = half + 0.5 * z * (1.0 - th * th) * (GELU_A * (1.0 + 3 * 0.044715 * (z * z)))
        g = cot[t].astype(F32) * slope
        gz_f[t] = g
        gb = g.astype(BF)
        gz[t] = gb
        first[t] = gb[0:1]
        last[t] = gb[HEIGHT - 1 :]
        total += jnp.sum((g * xt).reshape(-1, CHANS), axis=0, keepdims=True)
    skip[...] = spread(total, None)


def spread(vector, extra):
    row = lax.broadcasted_iota(jnp.int32, (8, 128), 0) % 4
    low = jnp.broadcast_to(vector[:, 0:128], (8, 128))
    high = jnp.broadcast_to(vector[:, 128:256], (8, 128))
    out = jnp.where(row == 0, low, jnp.where(row == 1, high, 0.0))
    if extra is not None:
        out = jnp.where(row == 2, extra, out)
    return out


def split_pairs(both):
    row = lax.broadcasted_iota(jnp.int32, (8, 128), 0)
    top = both.astype(BF).astype(F32)
    return jnp.where(row < 4, top, both - top)


def joined(pairs):
    return pairs + pltpu.roll(pairs, 4, 0)


def adjoint_body(steps, gz, above, below, weight, rates, local, send):
    d0, d1 = decay(rates, steps[0]), decay(rates, steps[1])
    a1 = conv(padded(1, above, gz, below), weight, True)
    local[1] = a1
    a0 = conv(padded(0, above, gz, below), weight, True) + d1 * a1
    local[0] = a0
    send[...] = (d0 * a0).reshape(BLOCKS, PLACES, CHANS).astype(BF)


def adjoints_body(scale, steps, place, local, incoming, state_f, carry, rates, adj, first, last, small):
    d0, d1 = decay(rates, steps[0]), decay(rates, steps[1])
    c = incoming[...].reshape(HEIGHT, WIDTH, CHANS).astype(F32)
    a0 = local[0] + d1 * c
    a1 = local[1] + c
    earlier = carry[...].reshape(HEIGHT, WIDTH, CHANS).astype(F32)
    for t, s in enumerate((a0, a1)):
        s = s.astype(BF)
        adj[t] = s
        first[t] = s[0:1]
        last[t] = s[HEIGHT - 1 :]
    k0 = jnp.sum((a0 * earlier).reshape(-1, CHANS), axis=0, keepdims=True) * d0
    k1 = jnp.sum((a1 * state_f[...]).reshape(-1, CHANS), axis=0, keepdims=True) * d1
    rate_part = (k0 * steps[0] + k1 * steps[1]) * (-scale[0])
    s0 = jnp.sum(k0 * rates[...], axis=1, keepdims=True) * (-scale[1])
    s1 = jnp.sum(k1 * rates[...], axis=1, keepdims=True) * (-scale[1])
    lane = lax.broadcasted_iota(jnp.int32, (8, 128), 1)
    at = place[0] * FRAMES
    extra = jnp.where(lane == at, s0, jnp.where(lane == at + 1, s1, 0.0))
    small[...] = spread(rate_part, extra)


def grad_inputs_body(adj, above, below, weight, gain, gz_f, out):
    for t in range(FRAMES):
        out[t] = (conv(padded(t, above, adj, below), weight, True) + gain[...] * gz_f[t]).astype(BF)


def weight_grad_body(scale, flat, field, above, below, small, out):
    for a in range(3):
        rhs = jnp.concatenate(
            [padded(t, above, field, below)[2 - a : 2 - a + HEIGHT] for t in range(FRAMES)], axis=0
        ).reshape(FRAMES * HEIGHT * WIDTH, CHANS)
        for b in range(3):
            g = jnp.dot(flat[b * CHANS : (b + 1) * CHANS, :], rhs, preferred_element_type=F32)
            g = g * scale[0]
            tap = 3 * a + b
            for lg in range(2):
                part = g[:, lg * 128 : (lg + 1) * 128].reshape(32, 8, 128)
                out[:, lg, tap * 8 : tap * 8 + 8, :] = part.astype(BF)
    out[:, :, 72:80, :] = jnp.zeros((32, 2, 8, 128), BF)
    out[0, 0, 72:80, :] = split_pairs(small[...] * scale[1]).astype(BF)


def pair_sum_body(core, out_own, out_got, in_own, in_got, send):
    def add(own, got):
        send[...] = (own[...].astype(F32) + got[...].astype(F32)).astype(BF)
        pairs = own[0, 0, 72:80, :].astype(F32) + got[0, 0, 72:80, :].astype(F32)
        send[0, 0, 72:80, :] = split_pairs(joined(pairs)).astype(BF)

    @pl.when(core[0] == 0)
    def _():
        add(out_own, out_got)

    @pl.when(core[0] == 1)
    def _():
        add(in_own, in_got)


def all_sum_body(got, send):
    total = jnp.zeros((80, 128), F32)
    for k in range(CHIPS):
        total = total + got[k].astype(F32)
    extras = split_pairs(joined(total[72:80]))
    total = jnp.concatenate([total[0:72], extras], axis=0).astype(BF)
    send[...] = jnp.broadcast_to(total[None], (CHIPS, 80, 128))


def unpack_body(core, own, got, grad_in, grad_out, small_in, small_out):
    def write(src, grad, small):
        for tap in range(9):
            for lg in range(2):
                part = src[:, lg, tap * 8 : tap * 8 + 8, :].astype(F32).reshape(CHANS, 128)
                grad[tap // 3, tap % 3, :, lg * 128 : (lg + 1) * 128] = part
        small[...] = joined(src[0, 0, 72:80, :].astype(F32))

    @pl.when(core[0] == 0)
    def _():
        write(own, grad_out, small_out)
        write(got, grad_in, small_in)

    @pl.when(core[0] == 1)
    def _():
        write(own, grad_in, small_in)
        write(got, grad_out, small_out)


ROWS_AXES = ("z", "core")
TM_AXES = ("x", "y")


def halos(first, last):
    count = 8
    up = [(i, i + 1) for i in range(count - 1)]
    down = [(i + 1, i) for i in range(count - 1)]
    above = lax.ppermute(last, ROWS_AXES, up)
    below = lax.ppermute(first, ROWS_AXES, down)
    return above, below


def swap(chunks, axes):
    return lax.all_to_all(chunks, axes, 0, 0)


def on_device(inputs, in_weight, out_weight, skip_gain, rates, step_sizes, cotangent):
    scale = 1.0 / math.sqrt(32 * 32 * 128)
    step_scale = 1.0 / math.sqrt(1048576)
    gain, rates = skip_gain[None, :], rates[None, :]
    place = (lax.axis_index("x") * 4 + lax.axis_index("y")).astype(jnp.int32)[None]
    core = lax.axis_index("core").astype(jnp.int32)[None]
    field = (FRAMES, HEIGHT, WIDTH, CHANS)
    edge = sds((FRAMES, 1, WIDTH, CHANS), BF)
    chunk = sds((BLOCKS, PLACES, CHANS), BF)
    packed = sds((32, 2, 80, 128), BF)
    small = sds((8, 128), F32)

    x_above, x_below = halos(inputs[:, 0:1], inputs[:, HEIGHT - 1 :])
    inputs_t = transposed(inputs)
    local, send = call(
        drive_body,
        [sds(field, F32), sds((BLOCKS, PLACES + 16, CHANS), BF)],
        [step_sizes, inputs, x_above, x_below, in_weight, rates],
        CONV_FLOPS,
    )
    got = swap(send, TM_AXES)
    send, block_decays = call(forward_scan_body, [chunk, sds((BLOCKS, CHANS), F32)], [got, rates])
    carry = swap(send, TM_AXES)
    state, first, last, state_f = call(
        states_body,
        [sds(field, BF), edge, edge, sds(field[1:], F32)],
        [step_sizes, local, carry, rates],
    )
    s_above, s_below = halos(first, last)
    state_t = transposed(state)
    outputs, gz_f, gz, first, last, skip_part = call(
        output_body,
        [sds(field, BF), sds(field, F32), sds(field, BF), edge, edge, small],
        [state, s_above, s_below, inputs, cotangent, out_weight, gain],
        CONV_FLOPS,
    )
    g_above, g_below = halos(first, last)
    local_adj, send = call(
        adjoint_body,
        [sds(field, F32), chunk],
        [step_sizes, gz, g_above, g_below, out_weight, rates],
        CONV_FLOPS,
    )
    got = swap(send, TM_AXES)
    (out_part,) = call(
        weight_grad_body,
        [packed],
        [jnp.array([scale, scale], F32), state_t, gz, g_above, g_below, skip_part],
        CONV_FLOPS,
    )
    to_first = [(2 * k + 1, 2 * k) for k in range(4)]
    to_second = [(2 * k, 2 * k + 1) for k in range(4)]
    out_got = lax.ppermute(out_part, ROWS_AXES, to_first)
    (send,) = call(backward_scan_body, [chunk], [got, block_decays])
    incoming = swap(send, TM_AXES)
    adj, first, last, small_part = call(
        adjoints_body,
        [sds(field, BF), edge, edge, small],
        [
            jnp.array([scale, step_scale], F32),
            step_sizes,
            place,
            local_adj,
            incoming,
            state_f,
            carry,
            rates,
        ],
    )
    a_above, a_below = halos(first, last)
    (in_part,) = call(
        weight_grad_body,
        [packed],
        [jnp.array([scale, 1.0], F32), inputs_t, adj, a_above, a_below, small_part],
        CONV_FLOPS,
    )
    in_got = lax.ppermute(in_part, ROWS_AXES, to_second)
    (grad_inputs,) = call(
        grad_inputs_body,
        [sds(field, BF)],
        [adj, a_above, a_below, in_weight, gain, gz_f],
        CONV_FLOPS,
    )
    (send,) = call(pair_sum_body, [packed], [core, out_part, out_got, in_part, in_got])
    got = swap(send.reshape(CHIPS, 80, 128), ("x", "y", "z"))
    (send,) = call(all_sum_body, [sds((CHIPS, 80, 128), BF)], [got])
    own = swap(send, ("x", "y", "z")).reshape(packed.shape)
    other = lax.ppermute(own, "core", [(0, 1), (1, 0)])
    weights = sds((3, 3, CHANS, CHANS), F32)
    grad_in_weight, grad_out_weight, small_in, small_out = call(
        unpack_body, [weights, weights, small, small], [core, own, other]
    )
    grad_skip = small_out[0:2].reshape(CHANS)
    grad_rates = small_in[0:2].reshape(CHANS)
    grad_steps = lax.dynamic_slice(small_in[2], (place[0] * FRAMES,), (FRAMES,))
    return (
        outputs,
        grad_inputs,
        grad_in_weight,
        grad_out_weight,
        grad_skip,
        grad_rates,
        grad_steps,
    )


def solution(mesh):
    fine = Mesh(mesh.devices.reshape(4, 4, 4, 2), ("x", "y", "z", "core"))
    spread_out = P(TM_AXES, ROWS_AXES, None, None)
    placed = (spread_out, P(), P(), P(), P(), P(TM_AXES), spread_out)
    return jax.shard_map(
        on_device,
        mesh=fine,
        in_specs=placed,
        out_specs=(spread_out, spread_out, P(), P(), P(), P(), P(TM_AXES)),
        check_vma=False,
    )
```

time: 545 us -> 182 us (0.33)
  waiting for transfers between devices: 273 us -> 22.2 us
  other arithmetic: 62.9 us -> 0 us
  local copies, waits for them, and re-layouts: 57.4 us -> 9.82 us
  matrix products: 26.8 us -> 0 us
  Pallas kernels: 0 us -> 22.3 us
  between operations: 14.7 us -> 0.97 us
  starting transfers between devices: 22.7 us -> 36.1 us
  blocking collectives: 83.6 us -> 89.6 us
    psum x1 -> x0, waiting for transfers between devices: 144 us -> none  [on_device(): lax.psum((in_part, out_part, skip_part, rate_part, step_vector), ('tm', '...]
    all_gather x2 -> x0, waiting for transfers between devices: 115 us -> none  [prefix(): everything = jax.tree.map(lambda part: lax.all_gather(part, axis), shard)]
    all_to_all x0 -> x5, blocking collectives: none -> 89.6 us  [swap(): return lax.all_to_all(chunks, axes, 0, 0)]
    psum x1 -> x0, blocking collectives: 64.7 us -> none  [on_device(): lax.psum((in_part, out_part, skip_part, rate_part, step_vector), ('tm', '...]
    select_n x32 -> x0, other arithmetic: 47.5 us -> none  [turn(): return jax.tree.map(lambda a, b: jnp.where(reached, a, b), new, before)]
    slice x28 -> x2, local copies, waits for them, and re-layouts: 32.9 us -> 1 us  [the longest x1 0.99 us: on_device(): x_above, x_below = halos(inputs[:, 0:1], inputs[:, HEIGHT - 1:])]
    dot_general x54 -> x0, matrix products: 26.8 us -> none  [the longest x36 16.6 us: conv_taps(): jnp.dot(window.reshape(-1, chans), matrix, preferred_element_type=jnp.flo...]
    pallas_call x0 -> x15, Pallas kernels: none -> 22.3 us  [call(): pl.pallas_call(body, out_shape=outs, in_specs=specs, out_specs=[VM] * len...]
  transfers between devices with their start and end apart: 11 -> 12, of which waited for: 7 -> 6; matrix products, arithmetic and copies ran while one was open for 3% -> 0% of each run, Pallas kernels for 0% -> 5%
where the time goes in v1:
time: 182 us; the launch traced here: 181 us
  blocking collectives  89.6 us (49%)
  starting transfers between devices  36.1 us (20%)
  Pallas kernels  22.3 us (12%)
  waiting for transfers between devices  22.2 us (12%)
  local copies, waits for them, and re-layouts  9.82 us (5%)
    all_to_all x5, blocking collectives, swap(): return lax.all_to_all(chunks, axes, 0, 0)  89.6 us
    pallas_call x15, Pallas kernels, call(): pl.pallas_call(body, out_shape=outs, in_specs=specs, out_specs=[VM] * len...  22.3 us
    ppermute x4, starting transfers between devices, halos(): above = lax.ppermute(last, ROWS_AXES, up)  16.8 us
    ppermute x4, starting transfers between devices, halos(): below = lax.ppermute(first, ROWS_AXES, down)  9.58 us
    ppermute x4, waiting for transfers between devices, halos(): below = lax.ppermute(first, ROWS_AXES, down)  8.92 us
    all_to_all x1, waiting for transfers between devices, swap(): return lax.all_to_all(chunks, axes, 0, 0)  8.13 us
    unnamed x46, local copies, waits for them, and re-layouts  7.67 us
    ppermute x1, waiting for transfers between devices, on_device(): in_got = lax.ppermute(in_part, ROWS_AXES, to_second)  3.96 us
  transfers between devices with their start and end apart: 12, of which 6 were waited for; matrix products, arithmetic and copies ran while one was open for 0% of the time, Pallas kernels for 5%

profile of v1, /device:TPU:1, one launch (start us, length us, event | category | flops | bytes accessed | tf_op | source)
XLA Modules:
  0.0 181.1 jit_solution(3342204813698303698)
XLA Ops:
  0.6 1.0 fusion
  1.6 3.3 %collective-permute-start.1 = (bf16[2,1,128,256]{3,2,1,0:T(8,128)(2,1)S(1)}, bf16[2,1,128,256]{3,2,1,0:T(8,128)(2,1)S(1)}, u32[]{:S(2)}, u32[]{:S(2)}) collective-permute-start(bf16[2,1,128,256]{3,2,1,0:T(8,128)(2,1)S(1)} %get-tuple-element.55), channel_id=1, source_target_pairs={{1,0},{2,1},{3,2},{4,3},{5,4},{6,5},{7,6},{9,8},{10,9},{11,10},{12... | collective-permute-start | bytes 393224 | tf_op jit(solution)/shard_map/ppermute | solution.py:280
  5.0 3.5 %collective-permute-start = (bf16[2,1,128,256]{3,2,1,0:T(8,128)(2,1)S(1)}, bf16[2,1,128,256]{3,2,1,0:T(8,128)(2,1)S(1)}, u32[]{:S(2)}, u32[]{:S(2)}) collective-permute-start(bf16[2,1,128,256]{3,2,1,0:T(8,128)(2,1)S(1)} %get-tuple-element.56), channel_id=1, source_target_pairs={{0,1},{1,2},{2,3},{3,4},{4,5},{5,6},{6,7},{8,9},{9,10},{10,11},{11... | collective-permute-start | bytes 393224 | tf_op jit(solution)/shard_map/ppermute | solution.py:279
  8.5 0.7 collective-permute-done.1.below
  9.2 1.2 collective-permute-done.above
  10.4 1.0 copy-done
  11.5 0.7 copy-done.2
  12.1 0.7 copy-done.4
  12.8 1.3 copy-done.8
  14.1 1.9 %shard_map.153 = (f32[2,4,128,256]{3,2,1,0:T(8,128)S(1)}, bf16[16,48,256]{2,1,0:T(8,128)(2,1)S(1)}) custom-call(f32[2]{0:T(128)S(1)} %copy-done.4, bf16[2,4,128,256]{3,2,1,0:T(8,128)(2,1)S(1)} %copy-done, bf16[2,1,128,256]{3,2,1,0:T(8,128)(2,1)S(1)} %collective-permute-done.above, bf16[2,1,128,256]{3,2,1,0:T(8,128)(2,1)S(1)} %collective-permute-done.1.below, ...), custom_call_target="tpu_custom_call" | custom-call | flops 1207959552 | bytes 3408904 | tf_op jit(solution)/shard_map/pallas_call | solution.py:28
  16.0 0.0 copy-start.3
  16.0 15.4 %all_to_all.30.got = bf16[16,48,256]{2,1,0:T(8,128)(2,1)S(1)} all-to-all(bf16[16,48,256]{2,1,0:T(8,128)(2,1)S(1)} %get-tuple-element.32), channel_id=1, replica_groups=mesh['x'=4,'y'=4,'z'=4,'core'=2] {'x','y'}, dimensions={0} | all-to-all | bytes 786432 | tf_op jit(solution)/shard_map/all_to_all | solution.py:285
  31.4 0.1 shard_map.154
  31.6 11.3 %all_to_all.31.carry = bf16[16,32,256]{2,1,0:T(8,128)(2,1)S(1)} all-to-all(bf16[16,32,256]{2,1,0:T(8,128)(2,1)S(1)} %get-tuple-element.33), channel_id=1, replica_groups=mesh['x'=4,'y'=4,'z'=4,'core'=2] {'x','y'}, dimensions={0} | all-to-all | bytes 524288 | tf_op jit(solution)/shard_map/all_to_all | solution.py:285
  42.9 0.0 copy-done.3
  42.9 0.7 shard_map.155
  43.6 6.2 %collective-permute-start.2 = (bf16[2,1,128,256]{3,2,1,0:T(8,128)(2,1)S(1)}, bf16[2,1,128,256]{3,2,1,0:T(8,128)(2,1)S(1)}, u32[]{:S(2)}, u32[]{:S(2)}) collective-permute-start(bf16[2,1,128,256]{3,2,1,0:T(8,128)(2,1)S(1)} %get-tuple-element.35), channel_id=1, source_target_pairs={{0,1},{1,2},{2,3},{3,4},{4,5},{5,6},{6,7},{8,9},{9,10},{10,11},{11... | collective-permute-start | bytes 393224 | tf_op jit(solution)/shard_map/ppermute | solution.py:279
  49.8 1.9 %collective-permute-start.3 = (bf16[2,1,128,256]{3,2,1,0:T(8,128)(2,1)S(1)}, bf16[2,1,128,256]{3,2,1,0:T(8,128)(2,1)S(1)}, u32[]{:S(2)}, u32[]{:S(2)}) collective-permute-start(bf16[2,1,128,256]{3,2,1,0:T(8,128)(2,1)S(1)} %get-tuple-element.36), channel_id=1, source_target_pairs={{1,0},{2,1},{3,2},{4,3},{5,4},{6,5},{7,6},{9,8},{10,9},{11,10},{12... | collective-permute-start | bytes 393224 | tf_op jit(solution)/shard_map/ppermute | solution.py:280
  51.7 0.0 collective-permute-done.2.above
  51.7 4.3 %collective-permute-done.3.below = bf16[2,1,128,256]{3,2,1,0:T(8,128)(2,1)S(1)} collective-permute-done((bf16[2,1,128,256]{3,2,1,0:T(8,128)(2,1)S(1)}, bf16[2,1,128,256]{3,2,1,0:T(8,128)(2,1)S(1)}, u32[]{:S(2)}, u32[]{:S(2)}) %collective-permute-start.3) | collective-permute-done | bytes 131104 | tf_op jit(solution)/shard_map/ppermute | solution.py:280
  56.1 0.0 copy-done.1
  56.1 0.0 copy-done.7
  56.1 3.0 %shard_map.156 = (bf16[2,4,128,256]{3,2,1,0:T(8,128)(2,1)}, f32[2,4,128,256]{3,2,1,0:T(8,128)S(1)}, bf16[2,4,128,256]{3,2,1,0:T(8,128)(2,1)S(1)}, bf16[2,1,128,2...) custom-call(bf16[2,4,128,256]{3,2,1,0:T(8,128)(2,1)S(1)} %get-tuple-element.34.state.v_ref, ...), custom_call_target="tpu_custom_call" | custom-call | flops 1207959552 | bytes 5379072 | tf_op jit(solution)/shard_map/pallas_call | solution.py:28
  59.1 1.0 copy-done.17
  60.1 1.9 %collective-permute-start.4 = (bf16[2,1,128,256]{3,2,1,0:T(8,128)(2,1)S(1)}, bf16[2,1,128,256]{3,2,1,0:T(8,128)(2,1)S(1)}, u32[]{:S(2)}, u32[]{:S(2)}) collective-permute-start(bf16[2,1,128,256]{3,2,1,0:T(8,128)(2,1)S(1)} %get-tuple-element.39), channel_id=1, source_target_pairs={{0,1},{1,2},{2,3},{3,4},{4,5},{5,6},{6,7},{8,9},{9,10},{10,11},{11... | collective-permute-start | bytes 393224 | tf_op jit(solution)/shard_map/ppermute | solution.py:279
  62.0 2.4 %collective-permute-start.5 = (bf16[2,1,128,256]{3,2,1,0:T(8,128)(2,1)S(1)}, bf16[2,1,128,256]{3,2,1,0:T(8,128)(2,1)S(1)}, u32[]{:S(2)}, u32[]{:S(2)}) collective-permute-start(bf16[2,1,128,256]{3,2,1,0:T(8,128)(2,1)S(1)} %get-tuple-element.40), channel_id=1, source_target_pairs={{1,0},{2,1},{3,2},{4,3},{5,4},{6,5},{7,6},{9,8},{10,9},{11,10},{12... | collective-permute-start | bytes 393224 | tf_op jit(solution)/shard_map/ppermute | solution.py:280
  64.4 0.0 collective-permute-done.4.above
  64.4 3.9 %collective-permute-done.5.below = bf16[2,1,128,256]{3,2,1,0:T(8,128)(2,1)S(1)} collective-permute-done((bf16[2,1,128,256]{3,2,1,0:T(8,128)(2,1)S(1)}, bf16[2,1,128,256]{3,2,1,0:T(8,128)(2,1)S(1)}, u32[]{:S(2)}, u32[]{:S(2)}) %collective-permute-start.5) | collective-permute-done | bytes 131104 | tf_op jit(solution)/shard_map/ppermute | solution.py:280
  68.3 2.0 %shard_map.157 = (f32[2,4,128,256]{3,2,1,0:T(8,128)S(1)}, bf16[16,32,256]{2,1,0:T(8,128)(2,1)S(1)}) custom-call(f32[2]{0:T(128)S(1)} %copy-done.4, bf16[2,4,128,256]{3,2,1,0:T(8,128)(2,1)S(1)} %get-tuple-element.38.gz.field, bf16[2,1,128,256]{3,2,1,0:T(8,128)(2,1)S(1)} %collective-permute-done.4.above, ...), custom_call_target="tpu_custom_call" | custom-call | flops 1207959552 | bytes 3277832 | tf_op jit(solution)/shard_map/pallas_call | solution.py:28
  70.3 0.0 copy-start.5
  70.3 0.0 copy-start.6
  70.3 10.5 %all_to_all.32.got = bf16[16,32,256]{2,1,0:T(8,128)(2,1)S(1)} all-to-all(bf16[16,32,256]{2,1,0:T(8,128)(2,1)S(1)} %get-tuple-element.42), channel_id=1, replica_groups=mesh['x'=4,'y'=4,'z'=4,'core'=2] {'x','y'}, dimensions={0} | all-to-all | bytes 524288 | tf_op jit(solution)/shard_map/all_to_all | solution.py:285
  80.9 0.8 shard_map.158
  81.6 3.5 %all-to-all-start.3 = ((bf16[16,32,256]{2,1,0:T(8,128)(2,1)}), bf16[16,32,256]{2,1,0:T(8,128)(2,1)S(1)}, u32[]{:S(2)}, u32[]{:S(2)}) async-start(bf16[16,32,256]{2,1,0:T(8,128)(2,1)} %shard_map.158), calls=%async_computation.3 | async-start | bytes 524288 | tf_op jit(solution)/shard_map/all_to_all | solution.py:285
  85.2 8.1 %all-to-all-done.3.incoming = bf16[16,32,256]{2,1,0:T(8,128)(2,1)S(1)} async-done(((bf16[16,32,256]{2,1,0:T(8,128)(2,1)}), bf16[16,32,256]{2,1,0:T(8,128)(2,1)S(1)}, u32[]{:S(2)}, u32[]{:S(2)}) %all-to-all-start.3) | async-done | bytes 262176 | tf_op jit(solution)/shard_map/all_to_all | solution.py:285
  93.3 0.0 copy-done.6
  93.3 0.8 shard_map.159
  94.1 5.2 %collective-permute-start.6 = (bf16[2,1,128,256]{3,2,1,0:T(8,128)(2,1)S(1)}, bf16[2,1,128,256]{3,2,1,0:T(8,128)(2,1)S(1)}, u32[]{:S(2)}, u32[]{:S(2)}) collective-permute-start(bf16[2,1,128,256]{3,2,1,0:T(8,128)(2,1)S(1)} %get-tuple-element.46), channel_id=1, source_target_pairs={{0,1},{1,2},{2,3},{3,4},{4,5},{5,6},{6,7},{8,9},{9,10},{10,11},{11... | collective-permute-start | bytes 393224 | tf_op jit(solution)/shard_map/ppermute | solution.py:279
  99.3 1.9 %collective-permute-start.7 = (bf16[2,1,128,256]{3,2,1,0:T(8,128)(2,1)S(1)}, bf16[2,1,128,256]{3,2,1,0:T(8,128)(2,1)S(1)}, u32[]{:S(2)}, u32[]{:S(2)}) collective-permute-start(bf16[2,1,128,256]{3,2,1,0:T(8,128)(2,1)S(1)} %get-tuple-element.47), channel_id=1, source_target_pairs={{1,0},{2,1},{3,2},{4,3},{5,4},{6,5},{7,6},{9,8},{10,9},{11,10},{12... | collective-permute-start | bytes 393224 | tf_op jit(solution)/shard_map/ppermute | solution.py:280
  101.3 0.5 shard_map.163.flat
  101.8 0.0 copy-start.20
  101.8 0.5 shard_map.161.flat
  102.3 0.5 copy-done.20
  102.8 2.0 %shard_map.162.out_own = bf16[32,2,80,128]{3,2,1,0:T(8,128)(2,1)S(1)} custom-call(f32[2]{0:T(128)S(1)} %call_exported.0.scale, bf16[768,1024]{1,0:T(8,128)(2,1)S(1)} %shard_map.161.flat, bf16[2,4,128,256]{3,2,1,0:T(8,128)(2,1)S(1)} %copy-done.20, bf16[2,1,128,256]{3,2,1,0:T(8,128)(2,1)S(1)} %collective-permute-done.4.above, ...), custom_call_target="tpu_custom_call" | custom-call | flops 1207959552 | bytes 3674120 | tf_op jit(solution)/shard_map/pallas_call | solution.py:28
  104.8 1.4 collective-permute-start.8
  106.2 0.0 collective-permute-done.6.above
  106.2 0.0 collective-permute-done.7.below
  106.2 3.0 %shard_map.164.in_own = bf16[32,2,80,128]{3,2,1,0:T(8,128)(2,1)} custom-call(f32[2]{0:T(128)S(1)} %copy-done.16, bf16[768,1024]{1,0:T(8,128)(2,1)S(1)} %shard_map.163.flat, bf16[2,4,128,256]{3,2,1,0:T(8,128)(2,1)S(1)} %get-tuple-element.45.adj.field, bf16[2,1,128,256]{3,2,1,0:T(8,128)(2,1)S(1)} %collective-permute-done.6.above, ...), custom_call_target="tpu_custom_call" | custom-call | flops 1207959552 | bytes 3674120 | tf_op jit(solution)/shard_map/pallas_call | solution.py:28
  109.2 1.3 collective-permute-start.9
  110.5 0.0 collective-permute-done.8.out_got
  110.5 4.0 %collective-permute-done.9.in_got = bf16[32,2,80,128]{3,2,1,0:T(8,128)(2,1)} collective-permute-done((bf16[32,2,80,128]{3,2,1,0:T(8,128)(2,1)}, bf16[32,2,80,128]{3,2,1,0:T(8,128)(2,1)}, u32[]{:S(2)}, u32[]{:S(2)}) %collective-permute-start.9) | collective-permute-done | bytes 1310752 | tf_op jit(solution)/shard_map/ppermute | solution.py:364
  114.5 2.0 %shard_map.165 = bf16[32,2,80,128]{3,2,1,0:T(8,128)(2,1)S(1)} custom-call(s32[1]{0:T(128)} %bitcast.3.core, bf16[32,2,80,128]{3,2,1,0:T(8,128)(2,1)S(1)} %shard_map.162.out_own, bf16[32,2,80,128]{3,2,1,0:T(8,128)(2,1)S(1)} %collective-permute-done.8.out_got, bf16[32,2,80,128]{3,2,1,0:T(8,128)(2,1)} %shard_map.164.in_own, ...), custom_call_target="tpu_custom_call" | custom-call | bytes 6553604 | tf_op jit(solution)/shard_map/pallas_call | solution.py:28
  116.5 27.6 %all_to_all.33.got = bf16[64,80,128]{2,1,0:T(8,128)(2,1)S(1)} all-to-all(bf16[64,80,128]{2,1,0:T(8,128)(2,1)S(1)} %bitcast.14), channel_id=1, replica_groups=mesh['x'=4,'y'=4,'z'=4,'core'=2] {'x','y','z'}, dimensions={0} | all-to-all | bytes 2621440 | tf_op jit(solution)/shard_map/all_to_all | solution.py:285
  144.1 0.2 shard_map.166
  144.3 0.0 copy-start.12
  144.4 24.8 %all_to_all.34 = bf16[64,80,128]{2,1,0:T(8,128)(2,1)S(1)} all-to-all(bf16[64,80,128]{2,1,0:T(8,128)(2,1)S(1)} %shard_map.166), channel_id=1, replica_groups=mesh['x'=4,'y'=4,'z'=4,'core'=2] {'x','y','z'}, dimensions={0} | all-to-all | bytes 2621440 | tf_op jit(solution)/shard_map/all_to_all | solution.py:285
  169.2 3.5 %collective-permute-start.10 = (bf16[32,2,80,128]{3,2,1,0:T(8,128)(2,1)S(1)}, bf16[32,2,80,128]{3,2,1,0:T(8,128)(2,1)S(1)}, u32[]{:S(2)}, u32[]{:S(2)}) collective-permute-start(bf16[32,2,80,128]{3,2,1,0:T(8,128)(2,1)S(1)} %bitcast.12), channel_id=1, source_target_pairs={{0,1},{1,0},{2,3},{3,2},{4,5},{5,4},{6,7},{7,6},{8,9},{9,8},{10,11... | collective-permute-start | bytes 3932168 | tf_op jit(solution)/shard_map/ppermute | solution.py:375
  172.7 1.3 copy-done.9
  174.0 1.2 copy-done.18
  175.2 2.2 %shard_map.160 = bf16[2,4,128,256]{3,2,1,0:T(8,128)(2,1)} custom-call(bf16[2,4,128,256]{3,2,1,0:T(8,128)(2,1)S(1)} %copy-done.12, bf16[2,1,128,256]{3,2,1,0:T(8,128)(2,1)S(1)} %collective-permute-done.6.above, bf16[2,1,128,256]{3,2,1,0:T(8,128)(2,1)S(1)} %copy-done.14, bf16[3,3,256,256]{3,2,1,0:T(8,128)(2,1)S(1)} %copy-done.9, f32[1,256]{1,0:T(1,128)S(1)} %bitcast.21, ...), custom_call_target="tpu_custom_call" | custom-call | flops 1207959552 | bytes 3539968 | tf_op jit(solution)/shard_map/pallas_call | solution.py:28
  177.4 0.0 collective-permute-done.10.got
  177.4 2.5 %shard_map.167 = (f32[3,3,256,256]{3,2,1,0:T(8,128)}, f32[3,3,256,256]{3,2,1,0:T(8,128)}, f32[8,128]{1,0:T(8,128)S(1)}, f32[8,128]{1,0:T(8,128)S(1)}) custom-call(s32[1]{0:T(128)} %bitcast.3.core, bf16[32,2,80,128]{3,2,1,0:T(8,128)(2,1)S(1)} %bitcast.13, bf16[32,2,80,128]{3,2,1,0:T(8,128)(2,1)S(1)} %collective-permute-done.10.got), custom_call_target="tpu_custom_call" | custom-call | bytes 7348228 | tf_op jit(solution)/shard_map/pallas_call | solution.py:28
  180.0 0.6 slice_bitcast_fusion
  180.5 0.6 dynamic-slice_bitcast_fusion
  (31 shorter events, 0.1 us)
Async XLA Ops:
  1.6 7.6 %collective-permute-start.1 = (bf16[2,1,128,256]{3,2,1,0:T(8,128)(2,1)S(1)}, bf16[2,1,128,256]{3,2,1,0:T(8,128)(2,1)S(1)}, u32[]{:S(2)}, u32[]{:S(2)}) collective-permute-start(bf16[2,1,128,256]{3,2,1,0:T(8,128)(2,1)S(1)} %get-tuple-element.55), channel_id=1, source_target_pairs={{1,0},{2,1},{3,2},{4,3},{5,4},{6,5},{7,6},{9,8},{10,9},{11,10},{12... | collective-permute-start | bytes 393224 | tf_op jit(solution)/shard_map/ppermute | solution.py:280
  5.0 5.5 %collective-permute-start = (bf16[2,1,128,256]{3,2,1,0:T(8,128)(2,1)S(1)}, bf16[2,1,128,256]{3,2,1,0:T(8,128)(2,1)S(1)}, u32[]{:S(2)}, u32[]{:S(2)}) collective-permute-start(bf16[2,1,128,256]{3,2,1,0:T(8,128)(2,1)S(1)} %get-tuple-element.56), channel_id=1, source_target_pairs={{0,1},{1,2},{2,3},{3,4},{4,5},{5,6},{6,7},{8,9},{9,10},{10,11},{11... | collective-permute-start | bytes 393224 | tf_op jit(solution)/shard_map/ppermute | solution.py:279
  10.4 1.0 copy-start
  11.5 0.7 copy-start.2
  12.1 0.7 copy-start.4
  12.8 1.3 copy-start.8
  16.0 26.9 %copy-start.3 = (f32[256]{0:T(256)S(1)}, f32[256]{0:T(256)}, u32[]{:S(2)}) copy-start(f32[256]{0:T(256)} %param.14) | copy-start | bytes 3076
  31.4 24.6 %copy-start.1 = (bf16[2,4,128,256]{3,2,1,0:T(8,128)(2,1)S(1)}, bf16[2,4,128,256]{3,2,1,0:T(8,128)(2,1)}, u32[]{:S(2)}) copy-start(bf16[2,4,128,256]{3,2,1,0:T(8,128)(2,1)} %v_ref.1) | copy-start | bytes 1572868
  31.4 24.6 %copy-start.7 = (bf16[3,3,256,256]{3,2,1,0:T(8,128)(2,1)S(1)}, bf16[3,3,256,256]{3,2,1,0:T(8,128)(2,1)}, u32[]{:S(2)}) copy-start(bf16[3,3,256,256]{3,2,1,0:T(8,128)(2,1)} %weight.6) | copy-start | bytes 3538948
  31.4 24.6 %copy-start.10 = (bf16[2,4,128,256]{3,2,1,0:T(8,128)(2,1)S(1)}, bf16[2,4,128,256]{3,2,1,0:T(8,128)(2,1)}, u32[]{:S(2)}) copy-start(bf16[2,4,128,256]{3,2,1,0:T(8,128)(2,1)} %cot.1) | copy-start | bytes 1572868
  31.4 24.6 %copy-start.15 = (f32[256]{0:T(256)S(1)}, f32[256]{0:T(256)}, u32[]{:S(2)}) copy-start(f32[256]{0:T(256)} %param.13) | copy-start | bytes 3076
  43.6 8.1 %collective-permute-start.2 = (bf16[2,1,128,256]{3,2,1,0:T(8,128)(2,1)S(1)}, bf16[2,1,128,256]{3,2,1,0:T(8,128)(2,1)S(1)}, u32[]{:S(2)}, u32[]{:S(2)}) collective-permute-start(bf16[2,1,128,256]{3,2,1,0:T(8,128)(2,1)S(1)} %get-tuple-element.35), channel_id=1, source_target_pairs={{0,1},{1,2},{2,3},{3,4},{4,5},{5,6},{6,7},{8,9},{9,10},{10,11},{11... | collective-permute-start | bytes 393224 | tf_op jit(solution)/shard_map/ppermute | solution.py:279
  49.8 6.3 %collective-permute-start.3 = (bf16[2,1,128,256]{3,2,1,0:T(8,128)(2,1)S(1)}, bf16[2,1,128,256]{3,2,1,0:T(8,128)(2,1)S(1)}, u32[]{:S(2)}, u32[]{:S(2)}) collective-permute-start(bf16[2,1,128,256]{3,2,1,0:T(8,128)(2,1)S(1)} %get-tuple-element.36), channel_id=1, source_target_pairs={{1,0},{2,1},{3,2},{4,3},{5,4},{6,5},{7,6},{9,8},{10,9},{11,10},{12... | collective-permute-start | bytes 393224 | tf_op jit(solution)/shard_map/ppermute | solution.py:280
  59.1 1.0 copy-start.17
  60.1 10.2 %copy-start.19 = (bf16[2,4,128,256]{3,2,1,0:T(8,128)(2,1)}, bf16[2,4,128,256]{3,2,1,0:T(8,128)(2,1)S(1)}, u32[]{:S(2)}) copy-start(bf16[2,4,128,256]{3,2,1,0:T(8,128)(2,1)S(1)} %get-tuple-element.38.gz.field) | copy-start | bytes 1572868
  60.1 10.2 %copy-start.21 = (f32[8,128]{1,0:T(8,128)}, f32[8,128]{1,0:T(8,128)S(1)}, u32[]{:S(2)}) copy-start(f32[8,128]{1,0:T(8,128)S(1)} %get-tuple-element.49.small) | copy-start | bytes 12292
  60.1 4.3 %collective-permute-start.4 = (bf16[2,1,128,256]{3,2,1,0:T(8,128)(2,1)S(1)}, bf16[2,1,128,256]{3,2,1,0:T(8,128)(2,1)S(1)}, u32[]{:S(2)}, u32[]{:S(2)}) collective-permute-start(bf16[2,1,128,256]{3,2,1,0:T(8,128)(2,1)S(1)} %get-tuple-element.39), channel_id=1, source_target_pairs={{0,1},{1,2},{2,3},{3,4},{4,5},{5,6},{6,7},{8,9},{9,10},{10,11},{11... | collective-permute-start | bytes 393224 | tf_op jit(solution)/shard_map/ppermute | solution.py:279
  62.0 6.3 %collective-permute-start.5 = (bf16[2,1,128,256]{3,2,1,0:T(8,128)(2,1)S(1)}, bf16[2,1,128,256]{3,2,1,0:T(8,128)(2,1)S(1)}, u32[]{:S(2)}, u32[]{:S(2)}) collective-permute-start(bf16[2,1,128,256]{3,2,1,0:T(8,128)(2,1)S(1)} %get-tuple-element.40), channel_id=1, source_target_pairs={{1,0},{2,1},{3,2},{4,3},{5,4},{6,5},{7,6},{9,8},{10,9},{11,10},{12... | collective-permute-start | bytes 393224 | tf_op jit(solution)/shard_map/ppermute | solution.py:280
  70.3 23.0 %copy-start.5 = (f32[2]{0:T(128)S(1)}, f32[2]{0:T(128)}, u32[]{:S(2)}) copy-start(f32[2]{0:T(128)} %steps.7) | copy-start | bytes 28
  70.3 23.0 %copy-start.6 = (f32[2]{0:T(128)S(1)}, f32[2]{0:T(128)}, u32[]{:S(2)}) copy-start(f32[2]{0:T(128)} %constant.29.clone.scale) | copy-start | bytes 28
  81.6 11.7 %all-to-all-start.3 = ((bf16[16,32,256]{2,1,0:T(8,128)(2,1)}), bf16[16,32,256]{2,1,0:T(8,128)(2,1)S(1)}, u32[]{:S(2)}, u32[]{:S(2)}) async-start(bf16[16,32,256]{2,1,0:T(8,128)(2,1)} %shard_map.158), calls=%async_computation.3 | async-start | bytes 524288 | tf_op jit(solution)/shard_map/all_to_all | solution.py:285
  94.1 12.1 %copy-start.11 = (bf16[2,4,128,256]{3,2,1,0:T(8,128)(2,1)}, bf16[2,4,128,256]{3,2,1,0:T(8,128)(2,1)S(1)}, u32[]{:S(2)}) copy-start(bf16[2,4,128,256]{3,2,1,0:T(8,128)(2,1)S(1)} %get-tuple-element.45.adj.field) | copy-start | bytes 1572868
  94.1 12.0 %collective-permute-start.6 = (bf16[2,1,128,256]{3,2,1,0:T(8,128)(2,1)S(1)}, bf16[2,1,128,256]{3,2,1,0:T(8,128)(2,1)S(1)}, u32[]{:S(2)}, u32[]{:S(2)}) collective-permute-start(bf16[2,1,128,256]{3,2,1,0:T(8,128)(2,1)S(1)} %get-tuple-element.46), channel_id=1, source_target_pairs={{0,1},{1,2},{2,3},{3,4},{4,5},{5,6},{6,7},{8,9},{9,10},{10,11},{11... | collective-permute-start | bytes 393224 | tf_op jit(solution)/shard_map/ppermute | solution.py:279
  99.3 6.9 %collective-permute-start.7 = (bf16[2,1,128,256]{3,2,1,0:T(8,128)(2,1)S(1)}, bf16[2,1,128,256]{3,2,1,0:T(8,128)(2,1)S(1)}, u32[]{:S(2)}, u32[]{:S(2)}) collective-permute-start(bf16[2,1,128,256]{3,2,1,0:T(8,128)(2,1)S(1)} %get-tuple-element.47), channel_id=1, source_target_pairs={{1,0},{2,1},{3,2},{4,3},{5,4},{6,5},{7,6},{9,8},{10,9},{11,10},{12... | collective-permute-start | bytes 393224 | tf_op jit(solution)/shard_map/ppermute | solution.py:280
  101.8 1.0 copy-start.20
  101.8 1.0 copy-start.22
  102.8 3.4 %copy-start.16 = (f32[2]{0:T(128)S(1)}, f32[2]{0:T(128)}, u32[]{:S(2)}) copy-start(f32[2]{0:T(128)} %constant.30.clone.scale) | copy-start | bytes 28
  104.8 5.7 %collective-permute-start.8 = (bf16[32,2,80,128]{3,2,1,0:T(8,128)(2,1)S(1)}, bf16[32,2,80,128]{3,2,1,0:T(8,128)(2,1)S(1)}, u32[]{:S(2)}, u32[]{:S(2)}) collective-permute-start(bf16[32,2,80,128]{3,2,1,0:T(8,128)(2,1)S(1)} %shard_map.162.out_own), channel_id=1, source_target_pairs={{1,0},{3,2},{5,4},{7,6},{9,8},{11,10},{13,12},{15,14},{17,16},{19,... | collective-permute-start | bytes 3932168 | tf_op jit(solution)/shard_map/ppermute | solution.py:340
  106.2 3.0 %copy-start.13 = (bf16[2,1,128,256]{3,2,1,0:T(8,128)(2,1)}, bf16[2,1,128,256]{3,2,1,0:T(8,128)(2,1)S(1)}, u32[]{:S(2)}) copy-start(bf16[2,1,128,256]{3,2,1,0:T(8,128)(2,1)S(1)} %collective-permute-done.7.below) | copy-start | bytes 393220
  109.2 5.3 %collective-permute-start.9 = (bf16[32,2,80,128]{3,2,1,0:T(8,128)(2,1)}, bf16[32,2,80,128]{3,2,1,0:T(8,128)(2,1)}, u32[]{:S(2)}, u32[]{:S(2)}) collective-permute-start(bf16[32,2,80,128]{3,2,1,0:T(8,128)(2,1)} %shard_map.164.in_own), channel_id=1, source_target_pairs={{0,1},{2,3},{4,5},{6,7},{8,9},{10,11},{12,13},{14,15},{16,17},{18,... | collective-permute-start | bytes 3932168 | tf_op jit(solution)/shard_map/ppermute | solution.py:364
  144.3 28.4 %copy-start.12 = (bf16[2,4,128,256]{3,2,1,0:T(8,128)(2,1)S(1)}, bf16[2,4,128,256]{3,2,1,0:T(8,128)(2,1)}, u32[]{:S(2)}) copy-start(bf16[2,4,128,256]{3,2,1,0:T(8,128)(2,1)} %copy-done.11) | copy-start | bytes 1572868
  144.4 28.4 %copy-start.14 = (bf16[2,1,128,256]{3,2,1,0:T(8,128)(2,1)S(1)}, bf16[2,1,128,256]{3,2,1,0:T(8,128)(2,1)}, u32[]{:S(2)}) copy-start(bf16[2,1,128,256]{3,2,1,0:T(8,128)(2,1)} %copy-done.13) | copy-start | bytes 393220
  169.2 8.3 %collective-permute-start.10 = (bf16[32,2,80,128]{3,2,1,0:T(8,128)(2,1)S(1)}, bf16[32,2,80,128]{3,2,1,0:T(8,128)(2,1)S(1)}, u32[]{:S(2)}, u32[]{:S(2)}) collective-permute-start(bf16[32,2,80,128]{3,2,1,0:T(8,128)(2,1)S(1)} %bitcast.12), channel_id=1, source_target_pairs={{0,1},{1,0},{2,3},{3,2},{4,5},{5,4},{6,7},{7,6},{8,9},{9,8},{10,11... | collective-permute-start | bytes 3932168 | tf_op jit(solution)/shard_map/ppermute | solution.py:375
  172.7 1.3 copy-start.9
  174.0 1.2 copy-start.18

commit v2 on v1

v2 whole, which is shorter than its diff:
```python
import math

import jax
import jax.numpy as jnp
from jax import lax
from jax.experimental import pallas as pl
from jax.experimental.pallas import tpu as pltpu
from jax.sharding import Mesh, PartitionSpec as P

BF, F32 = jnp.bfloat16, jnp.float32
VM = pl.BlockSpec(memory_space=pltpu.VMEM)
SM = pl.BlockSpec(memory_space=pltpu.SMEM)
FRAMES, HEIGHT, WIDTH, CHANS = 2, 4, 128, 256
WIDE, WIDER = HEIGHT + 2, HEIGHT + 4
BLOCKS = 16
PLACES = WIDE * WIDTH // BLOCKS
NOTE = 8
CHIPS = 64
GROUPS = 32
TAPS = 72
PACK = TAPS + 8


def sds(shape, dtype):
    return jax.ShapeDtypeStruct(shape, dtype)


def call(body, outs, ins, flops=0, scratch=()):
    nbytes = sum(math.prod(o.shape) * o.dtype.itemsize for o in outs)
    nbytes += sum(math.prod(i.shape) * i.dtype.itemsize for i in ins)
    specs = [SM if i.ndim == 1 else VM for i in ins]
    return pl.pallas_call(
        body,
        out_shape=outs,
        in_specs=specs,
        out_specs=[VM] * len(outs),
        scratch_shapes=list(scratch),
        compiler_params=pltpu.CompilerParams(vmem_limit_bytes=40 << 20),
        cost_estimate=pl.CostEstimate(flops=flops, bytes_accessed=nbytes, transcendentals=0),
    )(*ins)


ROW_FLOPS = 2 * 9 * FRAMES * WIDTH * CHANS * CHANS


def col_shift(v, by):
    turned = pltpu.roll(v, by % WIDTH, 1)
    at = lax.broadcasted_iota(jnp.int32, v.shape, 1)
    return jnp.where(at == (0 if by == 1 else WIDTH - 1), 0.0, turned)


def conv(rows, weight, flipped):
    height = rows.shape[0] - 2
    lhs = jnp.concatenate([rows[a : a + height] for a in range(3)], axis=-1)
    lhs = lhs.reshape(height * WIDTH, 3 * CHANS)
    parts = []
    for b in range(3):
        if flipped:
            rhs = jnp.concatenate([weight[2 - a, 2 - b] for a in range(3)], axis=1)
            y = lax.dot_general(lhs, rhs, (((1,), (1,)), ((), ())), preferred_element_type=F32)
        else:
            rhs = jnp.concatenate([weight[a, b] for a in range(3)], axis=0)
            y = jnp.dot(lhs, rhs, preferred_element_type=F32)
        parts.append(y.reshape(height, WIDTH, CHANS))
    return parts[1] + col_shift(parts[0], 1) + col_shift(parts[2], -1)


def inside(spot, rows):
    top = jnp.where(spot[1] == 1, 0.0, rows[0:1])
    bottom = jnp.where(spot[2] == 1, 0.0, rows[WIDE - 1 :])
    return jnp.concatenate([top, rows[1 : WIDE - 1], bottom], axis=0)


def transpose_rows(v_ref, out_ref, rows):
    lane = lax.broadcasted_iota(jnp.int32, (CHANS, WIDTH), 1)
    for t in range(FRAMES):
        for h in range(rows):
            flat = v_ref[t, h].astype(F32).T
            at = pl.ds((t * rows + h) * WIDTH, WIDTH)
            left = jnp.where(lane == 0, 0.0, pltpu.roll(flat, 1, 1))
            right = jnp.where(lane == WIDTH - 1, 0.0, pltpu.roll(flat, WIDTH - 1, 1))
            out_ref[0:CHANS, at] = left.astype(BF)
            out_ref[CHANS : 2 * CHANS, at] = flat.astype(BF)
            out_ref[2 * CHANS : 3 * CHANS, at] = right.astype(BF)


def transposed_body(v_ref, out_ref):
    transpose_rows(v_ref, out_ref, WIDER)


def decay(rates_ref, step):
    return jnp.exp(-rates_ref[...] * step)


def place_halos(spot, from_core, from_chip, above, below):
    @pl.when(spot[0] == 0)
    def _():
        above[...] = from_chip[...]
        below[...] = from_core[...]

    @pl.when(spot[0] == 1)
    def _():
        above[...] = from_core[...]
        below[...] = from_chip[...]

    @pl.when(spot[1] == 1)
    def _():
        above[...] = jnp.zeros_like(above)

    @pl.when(spot[2] == 1)
    def _():
        below[...] = jnp.zeros_like(below)


def drive_body(spot, steps, x, from_core, from_chip, weight, rates, local, send, wider):
    place_halos(spot, from_core, from_chip, wider.at[:, 0:2], wider.at[:, WIDER - 2 :])
    wider[:, 2 : WIDER - 2] = x[...]
    d1 = decay(rates, steps[1])
    first = inside(spot, conv(wider[0], weight, False))
    local[0] = first
    last = d1 * first + inside(spot, conv(wider[1], weight, False))
    local[1] = last
    send[:, 0:PLACES, :] = last.reshape(BLOCKS, PLACES, CHANS).astype(BF)
    total = jnp.full((BLOCKS, NOTE, CHANS), steps[0] + steps[1], F32)
    row = lax.broadcasted_iota(jnp.int32, total.shape, 1)
    one = total.astype(BF).astype(F32)
    two = (total - one).astype(BF).astype(F32)
    three = total - one - two
    send[:, PLACES : PLACES + NOTE, :] = jnp.where(
        row == 0, one, jnp.where(row == 1, two, jnp.where(row == 2, three, 0.0))
    ).astype(BF)


def forward_scan_body(got, rates, send, block_decays):
    carry = jnp.zeros((PLACES, CHANS), F32)
    for k in range(BLOCKS):
        send[k] = carry.astype(BF)
        span = jnp.sum(got[k, PLACES : PLACES + NOTE, :].astype(F32), axis=0, keepdims=True)
        d = jnp.exp(-rates[...] * span)
        block_decays[pl.ds(k, 1), :] = d
        carry = d * carry + got[k, 0:PLACES, :].astype(F32)


def backward_scan_body(got, block_decays, send):
    carry = jnp.zeros((PLACES, CHANS), F32)
    for k in reversed(range(BLOCKS)):
        send[k] = carry.astype(BF)
        carry = block_decays[pl.ds(k, 1), :] * carry + got[k].astype(F32)


GELU_A = math.sqrt(2 / math.pi)


def spread(vector, extra):
    row = lax.broadcasted_iota(jnp.int32, (8, 128), 0) % 4
    low = jnp.broadcast_to(vector[:, 0:128], (8, 128))
    high = jnp.broadcast_to(vector[:, 128:256], (8, 128))
    low, high = (jnp.where(row == 0, v, 0.0) for v in (low, high))
    if extra is not None:
        low = jnp.where(row == 1, extra, low)
    return low, high


def split_pairs(both):
    row = lax.broadcasted_iota(jnp.int32, (8, 128), 0)
    top = both.astype(BF).astype(F32)
    return jnp.where(row < 4, top, both - top)


def joined(pairs):
    return pairs + pltpu.roll(pairs, 4, 0)


def middle_body(
    spot, steps, local, carry, x, cot, weight, gain, rates,
    out, gz_f, gz, state, state_f, local_adj, send, small,
):
    d0, d1 = decay(rates, steps[0]), decay(rates, steps[1])
    c = carry[...].reshape(WIDE, WIDTH, CHANS).astype(F32)
    s0 = local[0] + d0 * c
    state_f[...] = s0
    state[0] = s0.astype(BF)
    state[1] = (local[1] + (d0 * d1) * c).astype(BF)
    total = jnp.zeros((1, CHANS), F32)
    later = None
    for t in (1, 0):
        xt = x[t].astype(F32)
        z = conv(state[t], weight, False) + gain[...] * xt
        th = jnp.tanh(GELU_A * (z + 0.044715 * (z * z * z)))
        half = 0.5 * (1.0 + th)
        out[t] = (z * half).astype(BF)
        slope = half + 0.5 * z * (1.0 - th * th) * (GELU_A * (1.0 + 3 * 0.044715 * (z * z)))
        g = cot[t].astype(F32) * slope
        gz_f[t] = g
        gb = g.astype(BF)
        gz[t] = gb
        total += jnp.sum((g * xt).reshape(-1, CHANS), axis=0, keepdims=True)
        blank = jnp.zeros((2, WIDTH, CHANS), BF)
        grad = inside(spot, conv(jnp.concatenate([blank, gb, blank], axis=0), weight, True))
        later = grad if later is None else grad + d1 * later
        local_adj[t] = later
    send[...] = (d0 * later).reshape(BLOCKS, PLACES, CHANS).astype(BF)
    small[0], small[1] = spread(total, None)


def pack_grad(core, g, a, scale, mine, theirs):
    for b in range(3):
        tap = (3 * a + b) * 8
        low = g[b * CHANS : (b + 1) * CHANS, 0:128] * scale
        high = g[b * CHANS : (b + 1) * CHANS, 128:256] * scale
        mine[:, tap : tap + 8, :] = (
            jnp.where(core == 0, low, high).astype(BF).reshape(GROUPS, 8, 128)
        )
        theirs[:, tap : tap + 8, :] = (
            jnp.where(core == 0, high, low).astype(BF).reshape(GROUPS, 8, 128)
        )


def pack_small(core, low, high, scale, mine, theirs):
    blank = jnp.zeros((GROUPS, 8, 128), BF)
    for ref, half in (
        (mine, jnp.where(core == 0, low, high)),
        (theirs, jnp.where(core == 0, high, low)),
    ):
        ref[:, TAPS:PACK, :] = blank
        ref[0, TAPS:PACK, :] = split_pairs(half * scale).astype(BF)


def out_grad_body(spot, scale, state, gz, small, mine, theirs, flat):
    transpose_rows(state, flat, WIDE)
    rhs = gz[...].reshape(FRAMES * HEIGHT * WIDTH, CHANS)
    for a in range(3):
        lhs = jnp.concatenate(
            [flat[:, pl.ds((t * WIDE + a) * WIDTH, HEIGHT * WIDTH)] for t in range(FRAMES)], axis=1
        )
        g = jnp.dot(lhs, rhs, preferred_element_type=F32)
        pack_grad(spot[0], g, a, scale[0], mine, theirs)
    pack_small(spot[0], small[0], small[1], scale[0], mine, theirs)


def in_grad_body(
    spot, scale, steps, local, incoming, state_f, carry, rates, flat,
    mine, theirs, adj, to_core, to_chip,
):
    d0, d1 = decay(rates, steps[0]), decay(rates, steps[1])
    c = incoming[...].reshape(WIDE, WIDTH, CHANS).astype(F32)
    a0 = local[0] + d1 * c
    a1 = local[1] + c
    earlier = carry[...].reshape(WIDE, WIDTH, CHANS).astype(F32)
    for t, s in enumerate((a0, a1)):
        adj[t] = s.astype(BF)

    @pl.when(spot[0] == 0)
    def _():
        to_chip[...] = adj[:, 0:2]
        to_core[...] = adj[:, WIDE - 2 :]

    @pl.when(spot[0] == 1)
    def _():
        to_core[...] = adj[:, 0:2]
        to_chip[...] = adj[:, WIDE - 2 :]

    rhs = adj[...].reshape(FRAMES * WIDE * WIDTH, CHANS)
    for a in range(3):
        lhs = jnp.concatenate(
            [flat[:, pl.ds((t * WIDER + a) * WIDTH, WIDE * WIDTH)] for t in range(FRAMES)], axis=1
        )
        g = jnp.dot(lhs, rhs, preferred_element_type=F32)
        pack_grad(spot[0], g, a, scale[0], mine, theirs)
    k0 = jnp.sum((a0 * earlier).reshape(-1, CHANS), axis=0, keepdims=True) * d0
    k1 = jnp.sum((a1 * state_f[...]).reshape(-1, CHANS), axis=0, keepdims=True) * d1
    rate_part = (k0 * steps[0] + k1 * steps[1]) * (-scale[0])
    s0 = jnp.sum(k0 * rates[...], axis=1, keepdims=True) * (-scale[1])
    s1 = jnp.sum(k1 * rates[...], axis=1, keepdims=True) * (-scale[1])
    lane = lax.broadcasted_iota(jnp.int32, (8, 128), 1)
    at = spot[3] * FRAMES
    low, high = spread(rate_part, jnp.where(lane == at, s0, jnp.where(lane == at + 1, s1, 0.0)))
    pack_small(spot[0], low, high, 1.0, mine, theirs)


def grad_inputs_body(spot, adj, from_core, from_chip, weight, gain, gz_f, out, above, below):
    place_halos(spot, from_core, from_chip, above, below)
    for t in range(FRAMES):
        up = (adj[t, 0:2].astype(F32) + above[t].astype(F32)).astype(BF)
        down = (adj[t, WIDE - 2 :].astype(F32) + below[t].astype(F32)).astype(BF)
        rows = jnp.concatenate([up, adj[t, 2 : WIDE - 2], down], axis=0)
        out[t] = (conv(rows, weight, True) + gain[...] * gz_f[t]).astype(BF)


def pair_sum_body(out_own, out_got, in_own, in_got, send):
    for g, (own, got) in enumerate(((out_own, out_got), (in_own, in_got))):
        send[g] = (own[...].astype(F32) + got[...].astype(F32)).astype(BF)
        pairs = own[0, TAPS:PACK, :].astype(F32) + got[0, TAPS:PACK, :].astype(F32)
        send[g, 0, TAPS:PACK, :] = split_pairs(joined(pairs)).astype(BF)


def all_sum_body(got, send):
    total = jnp.zeros((PACK, 128), F32)
    for k in range(CHIPS):
        total = total + got[k].astype(F32)
    extras = split_pairs(joined(total[TAPS:PACK]))
    total = jnp.concatenate([total[0:TAPS], extras], axis=0).astype(BF)
    send[...] = jnp.broadcast_to(total[None], (CHIPS, PACK, 128))


def unpack_body(spot, own, got, grad_in, grad_out, skip, rate, step):
    def write(src, lg):
        for g, grad, vector in ((0, grad_out, skip), (1, grad_in, rate)):
            for tap in range(9):
                part = src[g, :, tap * 8 : tap * 8 + 8, :].astype(F32).reshape(CHANS, 128)
                grad[tap // 3, tap % 3, :, lg * 128 : (lg + 1) * 128] = part
            extras = joined(src[g, 0, TAPS:PACK, :].astype(F32))
            vector[lg : lg + 1, :] = extras[0:1]
            if g == 1 and lg == 0:
                turned = pltpu.roll(extras, (128 - spot[3] * FRAMES) % 128, 1)
                step[...] = turned[1:2, 0:FRAMES]

    @pl.when(spot[0] == 0)
    def _():
        write(own, 0)
        write(got, 1)

    @pl.when(spot[0] == 1)
    def _():
        write(own, 1)
        write(got, 0)


ROWS_AXES = ("z", "core")
TM_AXES = ("x", "y")
CORE_PAIRS = [(i, i ^ 1) for i in range(8)]
CHIP_PAIRS = [(i, (i + 1) % 8 if i % 2 else (i - 1) % 8) for i in range(8)]


def halos(to_core, to_chip):
    from_chip = lax.ppermute(to_chip, ROWS_AXES, CHIP_PAIRS)
    from_core = lax.ppermute(to_core, ROWS_AXES, CORE_PAIRS)
    return from_core, from_chip


def swap(chunks, axes):
    return lax.all_to_all(chunks, axes, 0, 0)


def on_device(inputs, in_weight, out_weight, skip_gain, rates, step_sizes, cotangent):
    scale = 1.0 / math.sqrt(32 * 32 * 128)
    step_scale = 1.0 / math.sqrt(1048576)
    scales = jnp.array([scale, step_scale], F32)
    gain, rates = skip_gain[None, :], rates[None, :]
    core, z = lax.axis_index("core"), lax.axis_index("z")
    place = lax.axis_index("x") * 4 + lax.axis_index("y")
    top, bottom = (z == 0) & (core == 0), (z == 3) & (core == 1)
    spot = jnp.stack([core, top, bottom, place]).astype(jnp.int32)
    field = (FRAMES, HEIGHT, WIDTH, CHANS)
    wide = (FRAMES, WIDE, WIDTH, CHANS)
    edge = sds((FRAMES, 2, WIDTH, CHANS), BF)
    chunk = sds((BLOCKS, PLACES, CHANS), BF)
    packed = sds((GROUPS, PACK, 128), BF)

    to_core = lax.dynamic_slice(inputs, (0, 2 - 2 * core, 0, 0), edge.shape)
    to_chip = lax.dynamic_slice(inputs, (0, 2 * core, 0, 0), edge.shape)
    from_core, from_chip = halos(to_core, to_chip)
    local, send, wider = call(
        drive_body,
        [
            sds(wide, F32),
            sds((BLOCKS, PLACES + NOTE, CHANS), BF),
            sds((FRAMES, WIDER, WIDTH, CHANS), BF),
        ],
        [spot, step_sizes, inputs, from_core, from_chip, in_weight, rates],
        WIDE * ROW_FLOPS,
    )
    got = swap(send, TM_AXES)
    (flat,) = call(
        transposed_body, [sds((3 * CHANS, FRAMES * WIDER * WIDTH), BF)], [wider], 4 * ROW_FLOPS
    )
    send, block_decays = call(forward_scan_body, [chunk, sds((BLOCKS, CHANS), F32)], [got, rates])
    carry = swap(send, TM_AXES)
    outputs, gz_f, gz, state, state_f, local_adj, send, small = call(
        middle_body,
        [
            sds(field, BF),
            sds(field, F32),
            sds(field, BF),
            sds(wide, BF),
            sds(wide[1:], F32),
            sds(wide, F32),
            chunk,
            sds((2, 8, 128), F32),
        ],
        [spot, step_sizes, local, carry, inputs, cotangent, out_weight, gain, rates],
        (HEIGHT + WIDE) * ROW_FLOPS,
    )
    got = swap(send, TM_AXES)
    out_mine, out_theirs = call(
        out_grad_body,
        [packed, packed],
        [spot, scales, state, gz, small],
        HEIGHT * ROW_FLOPS,
        [pltpu.VMEM((3 * CHANS, FRAMES * WIDE * WIDTH), BF)],
    )
    out_got = lax.ppermute(out_theirs, ROWS_AXES, CORE_PAIRS)
    (send,) = call(backward_scan_body, [chunk], [got, block_decays])
    incoming = swap(send, TM_AXES)
    in_mine, in_theirs, adj, to_core, to_chip = call(
        in_grad_body,
        [packed, packed, sds(wide, BF), edge, edge],
        [spot, scales, step_sizes, local_adj, incoming, state_f, carry, rates, flat],
        WIDE * ROW_FLOPS,
    )
    in_got = lax.ppermute(in_theirs, ROWS_AXES, CORE_PAIRS)
    (send,) = call(
        pair_sum_body, [sds((2, GROUPS, PACK, 128), BF)], [out_mine, out_got, in_mine, in_got]
    )
    got = swap(send.reshape(CHIPS, PACK, 128), ("x", "y", "z"))
    from_core, from_chip = halos(to_core, to_chip)
    (grad_inputs,) = call(
        grad_inputs_body,
        [sds(field, BF)],
        [spot, adj, from_core, from_chip, in_weight, gain, gz_f],
        HEIGHT * ROW_FLOPS,
        [pltpu.VMEM(edge.shape, BF), pltpu.VMEM(edge.shape, BF)],
    )
    (send,) = call(all_sum_body, [sds((CHIPS, PACK, 128), BF)], [got])
    own = swap(send, ("x", "y", "z")).reshape(2, GROUPS, PACK, 128)
    other = lax.ppermute(own, ROWS_AXES, CORE_PAIRS)
    weights = sds((3, 3, CHANS, CHANS), F32)
    half = sds((2, 128), F32)
    grad_in_weight, grad_out_weight, grad_skip, grad_rates, grad_steps = call(
        unpack_body, [weights, weights, half, half, sds((1, FRAMES), F32)], [spot, own, other]
    )
    return (
        outputs,
        grad_inputs,
        grad_in_weight,
        grad_out_weight,
        grad_skip.reshape(CHANS),
        grad_rates.reshape(CHANS),
        grad_steps.reshape(FRAMES),
    )


def solution(mesh):
    fine = Mesh(mesh.devices.reshape(4, 4, 4, 2), ("x", "y", "z", "core"))
    spread_out = P(TM_AXES, ROWS_AXES, None, None)
    placed = (spread_out, P(), P(), P(), P(), P(TM_AXES), spread_out)
    return jax.shard_map(
        on_device,
        mesh=fine,
        in_specs=placed,
        out_specs=(spread_out, spread_out, P(), P(), P(), P(), P(TM_AXES)),
        check_vma=False,
    )
```

time: 182 us -> 161 us (0.88)
  starting transfers between devices: 36.1 us -> 21.6 us
  waiting for transfers between devices: 22.2 us -> 11.5 us
  local copies, waits for them, and re-layouts: 9.82 us -> 13.9 us
    ppermute x11 -> x7, starting transfers between devices: 32.6 us -> 18.1 us  [the longest x1 6.36 us: on_device(): out_got = lax.ppermute(out_theirs, ROWS_AXES, CORE_PAIRS)]
    all_to_all x1, waiting for transfers between devices: 8.13 us -> 0.01 us  [swap(): return lax.all_to_all(chunks, axes, 0, 0)]
    unnamed x46 -> x48, local copies, waits for them, and re-layouts: 7.67 us -> 12.8 us
    ppermute x11 -> x7, waiting for transfers between devices: 14.1 us -> 11.5 us  [the longest x2 7.37 us: halos(): from_chip = lax.ppermute(to_chip, ROWS_AXES, CHIP_PAIRS)]
    pallas_call x15 -> x11, Pallas kernels: 22.3 us -> 21.8 us  [call(): pl.pallas_call(body, out_shape=outs, in_specs=specs, out_specs=[VM] * len...]
  transfers between devices with their start and end apart: 12 -> 8, of which waited for: 6 -> 4; matrix products, arithmetic and copies ran while one was open for 0% -> 0% of each run, Pallas kernels for 5% -> 6%
where the time goes in v2:
time: 161 us; the launch traced here: 160 us
  blocking collectives  90.5 us (56%)
  Pallas kernels  21.8 us (14%)
  starting transfers between devices  21.6 us (13%)
  local copies, waits for them, and re-layouts  13.9 us (9%)
  waiting for transfers between devices  11.5 us (7%)
    all_to_all x5, blocking collectives, swap(): return lax.all_to_all(chunks, axes, 0, 0)  90.5 us
    pallas_call x11, Pallas kernels, call(): pl.pallas_call(body, out_shape=outs, in_specs=specs, out_specs=[VM] * len...  21.8 us
    unnamed x48, local copies, waits for them, and re-layouts  12.8 us
    ppermute x2, waiting for transfers between devices, halos(): from_chip = lax.ppermute(to_chip, ROWS_AXES, CHIP_PAIRS)  7.37 us
    ppermute x1, starting transfers between devices, on_device(): out_got = lax.ppermute(out_theirs, ROWS_AXES, CORE_PAIRS)  6.36 us
    ppermute x1, starting transfers between devices, on_device(): in_got = lax.ppermute(in_theirs, ROWS_AXES, CORE_PAIRS)  4.26 us
    ppermute x1, starting transfers between devices, on_device(): other = lax.ppermute(own, ROWS_AXES, CORE_PAIRS)  3.56 us
    all_to_all x1, starting transfers between devices, swap(): return lax.all_to_all(chunks, axes, 0, 0)  3.55 us
  transfers between devices with their start and end apart: 8, of which 4 were waited for; matrix products, arithmetic and copies ran while one was open for 0% of the time, Pallas kernels for 6%

profile of v2, /device:TPU:1, one launch (start us, length us, event | category | flops | bytes accessed | tf_op | source)
XLA Modules:
  0.0 160.1 jit_solution(9451831797175642024)
XLA Ops:
  0.6 1.1 constant_dynamic-slice_fusion
  1.7 1.5 collective-permute-start
  3.2 1.7 %collective-permute-start.1 = (bf16[2,2,128,256]{3,2,1,0:T(8,128)(2,1)S(1)}, bf16[2,2,128,256]{3,2,1,0:T(8,128)(2,1)S(1)}, u32[]{:S(2)}, u32[]{:S(2)}) collective-permute-start(bf16[2,2,128,256]{3,2,1,0:T(8,128)(2,1)S(1)} %get-tuple-element.57), channel_id=1, source_target_pairs={{0,7},{1,2},{2,1},{3,4},{4,3},{5,6},{6,5},{7,0},{8,15},{9,10},{10,... | collective-permute-start | bytes 786440 | tf_op jit(solution)/shard_map/ppermute | solution.py:336
  4.9 0.1 pad_add_fusion.spot
  5.0 0.0 collective-permute-done.from_core
  5.0 4.3 %collective-permute-done.1.from_chip = bf16[2,2,128,256]{3,2,1,0:T(8,128)(2,1)S(1)} collective-permute-done((bf16[2,2,128,256]{3,2,1,0:T(8,128)(2,1)S(1)}, bf16[2,2,128,256]{3,2,1,0:T(8,128)(2,1)S(1)}, u32[]{:S(2)}, u32[]{:S(2)}) %collective-permute-start.1) | collective-permute-done | bytes 262176 | tf_op jit(solution)/shard_map/ppermute | solution.py:336
  9.3 1.0 copy-done
  10.4 0.7 copy-done.2
  11.0 1.3 copy-done.5
  12.3 0.7 copy-done.9
  13.0 2.6 %shard_map.135 = (f32[2,6,128,256]{3,2,1,0:T(8,128)S(1)}, bf16[16,56,256]{2,1,0:T(8,128)(2,1)S(1)}, bf16[2,8,128,256]{3,2,1,0:T(8,128)(2,1)S(1)}) custom-call(s32[4]{0:T(128)S(1)} %pad_add_fusion.spot, f32[2]{0:T(128)S(1)} %copy-done.9, bf16[2,4,128,256]{3,2,1,0:T(8,128)(2,1)S(1)} %copy-done, bf16[2,2,128,256]{3,2,1,0:T(8,128)(2,1)S(1)} %collective-permute-done.from_core, ...), custom_call_target="tpu_custom_call" | custom-call | flops 1811939328 | bytes 5309464 | tf_op jit(solution)/shard_map/pallas_call | solution.py:32
  15.6 0.0 copy-start.14
  15.6 0.0 copy-start.1
  15.6 0.0 copy-start.4
  15.6 0.0 copy-start.8
  15.7 0.0 copy-start.10
  15.7 15.7 %all_to_all.30.got = bf16[16,56,256]{2,1,0:T(8,128)(2,1)S(1)} all-to-all(bf16[16,56,256]{2,1,0:T(8,128)(2,1)S(1)} %get-tuple-element.33), channel_id=1, replica_groups=mesh['x'=4,'y'=4,'z'=4,'core'=2] {'x','y'}, dimensions={0} | all-to-all | bytes 917504 | tf_op jit(solution)/shard_map/all_to_all | solution.py:342
  31.4 0.1 shard_map.136
  31.5 0.0 copy-done.14
  31.5 11.1 %all_to_all.31.carry = bf16[16,48,256]{2,1,0:T(8,128)(2,1)S(1)} all-to-all(bf16[16,48,256]{2,1,0:T(8,128)(2,1)S(1)} %get-tuple-element.34), channel_id=1, replica_groups=mesh['x'=4,'y'=4,'z'=4,'core'=2] {'x','y'}, dimensions={0} | all-to-all | bytes 786432 | tf_op jit(solution)/shard_map/all_to_all | solution.py:342
  42.6 0.0 copy-done.7
  42.6 0.0 copy-done.1
  42.6 0.0 copy-done.4
  42.6 0.0 copy-done.8
  42.6 0.0 copy-done.10
  42.6 5.2 %shard_map.137 = (bf16[2,4,128,256]{3,2,1,0:T(8,128)(2,1)}, f32[2,4,128,256]{3,2,1,0:T(8,128)S(1)}, bf16[2,4,128,256]{3,2,1,0:T(8,128)(2,1)S(1)}, bf16[2,6,128,2...) custom-call(s32[4]{0:T(128)S(1)} %pad_add_fusion.spot, ...), custom_call_target="tpu_custom_call" | custom-call | flops 3019898880 | bytes 9840664 | tf_op jit(solution)/shard_map/pallas_call | solution.py:32
  47.8 0.0 copy-start.16
  47.8 1.1 copy-done.16
  49.0 1.0 copy-done.18
  50.0 0.9 copy-done.22
  50.8 11.3 %all_to_all.32.got = bf16[16,48,256]{2,1,0:T(8,128)(2,1)S(1)} all-to-all(bf16[16,48,256]{2,1,0:T(8,128)(2,1)S(1)} %get-tuple-element.37), channel_id=1, replica_groups=mesh['x'=4,'y'=4,'z'=4,'core'=2] {'x','y'}, dimensions={0} | all-to-all | bytes 786432 | tf_op jit(solution)/shard_map/all_to_all | solution.py:342
  62.2 0.0 copy-done.20
  62.2 0.8 shard_map.138
  63.0 3.6 %all-to-all-start.3 = ((bf16[16,48,256]{2,1,0:T(8,128)(2,1)}), bf16[16,48,256]{2,1,0:T(8,128)(2,1)S(1)}, u32[]{:S(2)}, u32[]{:S(2)}) async-start(bf16[16,48,256]{2,1,0:T(8,128)(2,1)} %shard_map.138), calls=%async_computation.3 | async-start | bytes 786432 | tf_op jit(solution)/shard_map/all_to_all | solution.py:342
  66.6 0.0 copy-done.15
  66.6 0.0 copy-start.11
  66.6 0.0 copy-start.23
  66.6 0.9 shard_map.139.flat
  67.5 1.6 %copy-done.12 = bf16[768,2048]{1,0:T(8,128)(2,1)} copy-done((bf16[768,2048]{1,0:T(8,128)(2,1)}, bf16[768,2048]{1,0:T(8,128)(2,1)S(1)}, u32[]{:S(2)}) %copy-start.12) | copy-done | bytes 3145752
  69.1 0.0 copy-done.11
  69.2 2.2 %shard_map.142 = (bf16[32,80,128]{2,1,0:T(8,128)(2,1)S(1)}, bf16[32,80,128]{2,1,0:T(8,128)(2,1)S(1)}) custom-call(s32[4]{0:T(128)S(1)} %pad_add_fusion.spot, f32[2]{0:T(128)S(1)} %copy-done.11, bf16[2,6,128,256]{3,2,1,0:T(8,128)(2,1)S(1)} %copy-done.23, bf16[2,4,128,256]{3,2,1,0:T(8,128)(2,1)S(1)} %get-tuple-element.46.gz, ...), custom_call_target="tpu_custom_call" | custom-call | flops 1207959552 | bytes 2629656 | tf_op jit(solution)/shard_map/pallas_call | solution.py:32
  71.4 6.4 %collective-permute-start.4 = (bf16[32,80,128]{2,1,0:T(8,128)(2,1)S(1)}, bf16[32,80,128]{2,1,0:T(8,128)(2,1)S(1)}, u32[]{:S(2)}, u32[]{:S(2)}) collective-permute-start(bf16[32,80,128]{2,1,0:T(8,128)(2,1)S(1)} %get-tuple-element.49), channel_id=1, source_target_pairs={{0,1},{1,0},{2,3},{3,2},{4,5},{5,4},{6,7},{7,6},{8,9},{9,8},{10,11... | collective-permute-start | bytes 1966088 | tf_op jit(solution)/shard_map/ppermute | solution.py:402
  77.7 0.0 all-to-all-done.3.incoming
  77.8 1.9 %copy-done.13 = bf16[768,2048]{1,0:T(8,128)(2,1)S(1)} copy-done((bf16[768,2048]{1,0:T(8,128)(2,1)S(1)}, bf16[768,2048]{1,0:T(8,128)(2,1)}, u32[]{:S(2)}) %copy-start.13) | copy-done | bytes 3145752
  79.6 1.4 copy-done.17
  81.1 1.1 copy-done.21
  82.2 3.3 %shard_map.140 = (bf16[32,80,128]{2,1,0:T(8,128)(2,1)S(1)}, bf16[32,80,128]{2,1,0:T(8,128)(2,1)S(1)}, bf16[2,6,128,256]{3,2,1,0:T(8,128)(2,1)S(1)}, bf16[2,2,128...) custom-call(s32[4]{0:T(128)S(1)} %pad_add_fusion.spot, f32[2]{0:T(128)S(1)} %copy-done.11, f32[2]{0:T(128)S(1)} %copy-done.10, ...), custom_call_target="tpu_custom_call" | custom-call | flops 1811939328 | bytes 8913952 | tf_op jit(solution)/shard_map/pallas_call | solution.py:32
  85.4 4.3 %collective-permute-start.5 = (bf16[32,80,128]{2,1,0:T(8,128)(2,1)S(1)}, bf16[32,80,128]{2,1,0:T(8,128)(2,1)S(1)}, u32[]{:S(2)}, u32[]{:S(2)}) collective-permute-start(bf16[32,80,128]{2,1,0:T(8,128)(2,1)S(1)} %get-tuple-element.51), channel_id=1, source_target_pairs={{0,1},{1,0},{2,3},{3,2},{4,5},{5,4},{6,7},{7,6},{8,9},{9,8},{10,11... | collective-permute-start | bytes 1966088 | tf_op jit(solution)/shard_map/ppermute | solution.py:411
  89.7 0.0 collective-permute-done.4.out_got
  89.7 1.7 %collective-permute-done.5.in_got = bf16[32,80,128]{2,1,0:T(8,128)(2,1)S(1)} collective-permute-done((bf16[32,80,128]{2,1,0:T(8,128)(2,1)S(1)}, bf16[32,80,128]{2,1,0:T(8,128)(2,1)S(1)}, u32[]{:S(2)}, u32[]{:S(2)}) %collective-permute-start.5) | collective-permute-done | bytes 655392 | tf_op jit(solution)/shard_map/ppermute | solution.py:411
  91.4 0.3 shard_map.143
  91.7 28.1 %all_to_all.33.got = bf16[64,80,128]{2,1,0:T(8,128)(2,1)S(1)} all-to-all(bf16[64,80,128]{2,1,0:T(8,128)(2,1)S(1)} %bitcast.13), channel_id=1, replica_groups=mesh['x'=4,'y'=4,'z'=4,'core'=2] {'x','y','z'}, dimensions={0} | all-to-all | bytes 2621440 | tf_op jit(solution)/shard_map/all_to_all | solution.py:342
  119.8 0.2 shard_map.144
  120.1 0.0 copy-start.6
  120.1 0.0 copy-start.19
  120.1 24.4 %all_to_all.34 = bf16[64,80,128]{2,1,0:T(8,128)(2,1)S(1)} all-to-all(bf16[64,80,128]{2,1,0:T(8,128)(2,1)S(1)} %shard_map.144), channel_id=1, replica_groups=mesh['x'=4,'y'=4,'z'=4,'core'=2] {'x','y','z'}, dimensions={0} | all-to-all | bytes 2621440 | tf_op jit(solution)/shard_map/all_to_all | solution.py:342
  144.5 3.6 %collective-permute-start.6 = (bf16[2,32,80,128]{3,2,1,0:T(8,128)(2,1)S(1)}, bf16[2,32,80,128]{3,2,1,0:T(8,128)(2,1)S(1)}, u32[]{:S(2)}, u32[]{:S(2)}) collective-permute-start(bf16[2,32,80,128]{3,2,1,0:T(8,128)(2,1)S(1)} %bitcast.11), channel_id=1, source_target_pairs={{0,1},{1,0},{2,3},{3,2},{4,5},{5,4},{6,7},{7,6},{8,9},{9,8},{10,11... | collective-permute-start | bytes 3932168 | tf_op jit(solution)/shard_map/ppermute | solution.py:426
  148.0 0.0 collective-permute-start.2
  148.0 0.7 collective-permute-start.3
  148.7 2.4 %collective-permute-done.2.from_core = bf16[2,2,128,256]{3,2,1,0:T(8,128)(2,1)S(1)} collective-permute-done((bf16[2,2,128,256]{3,2,1,0:T(8,128)(2,1)S(1)}, bf16[2,2,128,256]{3,2,1,0:T(8,128)(2,1)S(1)}, u32[]{:S(2)}, u32[]{:S(2)}) %collective-permute-start.2) | collective-permute-done | bytes 262176 | tf_op jit(solution)/shard_map/ppermute | solution.py:337
  151.0 3.1 %collective-permute-done.3.from_chip = bf16[2,2,128,256]{3,2,1,0:T(8,128)(2,1)S(1)} collective-permute-done((bf16[2,2,128,256]{3,2,1,0:T(8,128)(2,1)S(1)}, bf16[2,2,128,256]{3,2,1,0:T(8,128)(2,1)S(1)}, u32[]{:S(2)}, u32[]{:S(2)}) %collective-permute-start.3) | collective-permute-done | bytes 262176 | tf_op jit(solution)/shard_map/ppermute | solution.py:336
  154.1 2.9 %shard_map.141 = bf16[2,4,128,256]{3,2,1,0:T(8,128)(2,1)} custom-call(s32[4]{0:T(128)S(1)} %pad_add_fusion.spot, bf16[2,6,128,256]{3,2,1,0:T(8,128)(2,1)S(1)} %get-tuple-element.41.adj, bf16[2,2,128,256]{3,2,1,0:T(8,128)(2,1)S(1)} %collective-permute-done.2.from_core, bf16[2,2,128,256]{3,2,1,0:T(8,128)(2,1)S(1)} %collective-permute-done.3.from_chip, ...), custom_call_target="tpu_custom_call" | custom-call | flops 1207959552 | bytes 4064272 | tf_op jit(solution)/shard_map/pallas_call | solution.py:32
  157.0 0.0 collective-permute-done.6.got
  157.0 3.1 %shard_map.145 = (f32[3,3,256,256]{3,2,1,0:T(8,128)}, f32[3,3,256,256]{3,2,1,0:T(8,128)}, f32[2,128]{1,0:T(2,128)}, f32[2,128]{1,0:T(2,128)}, f32[1,2]{1,0:T(1,128)}) custom-call(s32[4]{0:T(128)S(1)} %pad_add_fusion.spot, bf16[2,32,80,128]{3,2,1,0:T(8,128)(2,1)S(1)} %bitcast.12, bf16[2,32,80,128]{3,2,1,0:T(8,128)(2,1)S(1)} %collective-permute-done.6.got), custom_call_target="tpu_custom_call" | custom-call | bytes 7342104 | tf_op jit(solution)/shard_map/pallas_call | solution.py:32
  (18 shorter events, 0.0 us)
Async XLA Ops:
  1.7 3.3 %collective-permute-start = (bf16[2,2,128,256]{3,2,1,0:T(8,128)(2,1)S(1)}, bf16[2,2,128,256]{3,2,1,0:T(8,128)(2,1)S(1)}, u32[]{:S(2)}, u32[]{:S(2)}) collective-permute-start(bf16[2,2,128,256]{3,2,1,0:T(8,128)(2,1)S(1)} %get-tuple-element.58), channel_id=1, source_target_pairs={{0,1},{1,0},{2,3},{3,2},{4,5},{5,4},{6,7},{7,6},{8,9},{9,8},{10,11... | collective-permute-start | bytes 786440 | tf_op jit(solution)/shard_map/ppermute | solution.py:337
  3.2 6.1 %collective-permute-start.1 = (bf16[2,2,128,256]{3,2,1,0:T(8,128)(2,1)S(1)}, bf16[2,2,128,256]{3,2,1,0:T(8,128)(2,1)S(1)}, u32[]{:S(2)}, u32[]{:S(2)}) collective-permute-start(bf16[2,2,128,256]{3,2,1,0:T(8,128)(2,1)S(1)} %get-tuple-element.57), channel_id=1, source_target_pairs={{0,7},{1,2},{2,1},{3,4},{4,3},{5,6},{6,5},{7,0},{8,15},{9,10},{10,... | collective-permute-start | bytes 786440 | tf_op jit(solution)/shard_map/ppermute | solution.py:336
  9.3 1.0 copy-start
  10.4 0.7 copy-start.2
  11.0 1.3 copy-start.5
  12.3 0.7 copy-start.9
  13.0 29.6 %copy-start.7 = (bf16[2,4,128,256]{3,2,1,0:T(8,128)(2,1)S(1)}, bf16[2,4,128,256]{3,2,1,0:T(8,128)(2,1)}, u32[]{:S(2)}) copy-start(bf16[2,4,128,256]{3,2,1,0:T(8,128)(2,1)} %cot.1) | copy-start | bytes 1572868
  15.6 15.9 %copy-start.14 = (bf16[2,8,128,256]{3,2,1,0:T(8,128)(2,1)}, bf16[2,8,128,256]{3,2,1,0:T(8,128)(2,1)S(1)}, u32[]{:S(2)}) copy-start(bf16[2,8,128,256]{3,2,1,0:T(8,128)(2,1)S(1)} %get-tuple-element.40.v_ref) | copy-start | bytes 3145732
  15.6 27.0 %copy-start.1 = (bf16[2,4,128,256]{3,2,1,0:T(8,128)(2,1)S(1)}, bf16[2,4,128,256]{3,2,1,0:T(8,128)(2,1)}, u32[]{:S(2)}) copy-start(bf16[2,4,128,256]{3,2,1,0:T(8,128)(2,1)} %x.3) | copy-start | bytes 1572868
  15.6 27.0 %copy-start.4 = (bf16[3,3,256,256]{3,2,1,0:T(8,128)(2,1)S(1)}, bf16[3,3,256,256]{3,2,1,0:T(8,128)(2,1)}, u32[]{:S(2)}) copy-start(bf16[3,3,256,256]{3,2,1,0:T(8,128)(2,1)} %weight.4) | copy-start | bytes 3538948
  15.6 27.0 %copy-start.8 = (f32[256]{0:T(256)S(1)}, f32[256]{0:T(256)}, u32[]{:S(2)}) copy-start(f32[256]{0:T(256)} %param.11) | copy-start | bytes 3076
  15.7 27.0 %copy-start.10 = (f32[2]{0:T(128)S(1)}, f32[2]{0:T(128)}, u32[]{:S(2)}) copy-start(f32[2]{0:T(128)} %steps.5) | copy-start | bytes 28
  47.8 1.1 copy-start.16
  49.0 1.0 copy-start.18
  50.0 0.9 copy-start.22
  50.8 11.3 %copy-start.20 = (f32[6,128,256]{2,1,0:T(8,128)}, f32[6,128,256]{2,1,0:T(8,128)S(1)}, u32[]{:S(2)}) copy-start(f32[6,128,256]{2,1,0:T(8,128)S(1)} %get-tuple-element.39.state_f) | copy-start | bytes 2359300
  50.8 15.7 %copy-start.15 = (bf16[2,8,128,256]{3,2,1,0:T(8,128)(2,1)S(1)}, bf16[2,8,128,256]{3,2,1,0:T(8,128)(2,1)}, u32[]{:S(2)}) copy-start(bf16[2,8,128,256]{3,2,1,0:T(8,128)(2,1)} %copy-done.14) | copy-start | bytes 3145732
  63.0 14.7 %all-to-all-start.3 = ((bf16[16,48,256]{2,1,0:T(8,128)(2,1)}), bf16[16,48,256]{2,1,0:T(8,128)(2,1)S(1)}, u32[]{:S(2)}, u32[]{:S(2)}) async-start(bf16[16,48,256]{2,1,0:T(8,128)(2,1)} %shard_map.138), calls=%async_computation.3 | async-start | bytes 786432 | tf_op jit(solution)/shard_map/all_to_all | solution.py:342
  66.6 2.6 %copy-start.11 = (f32[2]{0:T(128)S(1)}, f32[2]{0:T(128)}, u32[]{:S(2)}) copy-start(f32[2]{0:T(128)} %constant.29.clone.scale) | copy-start | bytes 28
  66.6 2.6 %copy-start.23 = (bf16[2,6,128,256]{3,2,1,0:T(8,128)(2,1)S(1)}, bf16[2,6,128,256]{3,2,1,0:T(8,128)(2,1)}, u32[]{:S(2)}) copy-start(bf16[2,6,128,256]{3,2,1,0:T(8,128)(2,1)} %copy-done.22) | copy-start | bytes 2359300
  67.5 1.6 %copy-start.12 = (bf16[768,2048]{1,0:T(8,128)(2,1)}, bf16[768,2048]{1,0:T(8,128)(2,1)S(1)}, u32[]{:S(2)}) copy-start(bf16[768,2048]{1,0:T(8,128)(2,1)S(1)} %shard_map.139.flat) | copy-start | bytes 9437188
  69.2 8.6 %copy-start.3 = (f32[256]{0:T(256)S(1)}, f32[256]{0:T(256)}, u32[]{:S(2)}) copy-start(f32[256]{0:T(256)} %param.12) | copy-start | bytes 3076
  71.4 18.3 %collective-permute-start.4 = (bf16[32,80,128]{2,1,0:T(8,128)(2,1)S(1)}, bf16[32,80,128]{2,1,0:T(8,128)(2,1)S(1)}, u32[]{:S(2)}, u32[]{:S(2)}) collective-permute-start(bf16[32,80,128]{2,1,0:T(8,128)(2,1)S(1)} %get-tuple-element.49), channel_id=1, source_target_pairs={{0,1},{1,0},{2,3},{3,2},{4,5},{5,4},{6,7},{7,6},{8,9},{9,8},{10,11... | collective-permute-start | bytes 1966088 | tf_op jit(solution)/shard_map/ppermute | solution.py:402
  77.7 1.9 %copy-start.13 = (bf16[768,2048]{1,0:T(8,128)(2,1)S(1)}, bf16[768,2048]{1,0:T(8,128)(2,1)}, u32[]{:S(2)}) copy-start(bf16[768,2048]{1,0:T(8,128)(2,1)} %copy-done.12) | copy-start | bytes 9437188
  79.6 1.4 copy-start.17
  81.0 1.1 copy-start.21
  85.4 6.0 %collective-permute-start.5 = (bf16[32,80,128]{2,1,0:T(8,128)(2,1)S(1)}, bf16[32,80,128]{2,1,0:T(8,128)(2,1)S(1)}, u32[]{:S(2)}, u32[]{:S(2)}) collective-permute-start(bf16[32,80,128]{2,1,0:T(8,128)(2,1)S(1)} %get-tuple-element.51), channel_id=1, source_target_pairs={{0,1},{1,0},{2,3},{3,2},{4,5},{5,4},{6,7},{7,6},{8,9},{9,8},{10,11... | collective-permute-start | bytes 1966088 | tf_op jit(solution)/shard_map/ppermute | solution.py:411
  120.1 34.1 %copy-start.6 = (bf16[3,3,256,256]{3,2,1,0:T(8,128)(2,1)S(1)}, bf16[3,3,256,256]{3,2,1,0:T(8,128)(2,1)}, u32[]{:S(2)}) copy-start(bf16[3,3,256,256]{3,2,1,0:T(8,128)(2,1)} %weight.5) | copy-start | bytes 3538948
  120.1 34.0 %copy-start.19 = (f32[2,4,128,256]{3,2,1,0:T(8,128)S(1)}, f32[2,4,128,256]{3,2,1,0:T(8,128)}, u32[]{:S(2)}) copy-start(f32[2,4,128,256]{3,2,1,0:T(8,128)} %copy-done.18) | copy-start | bytes 3145732
  144.5 12.5 %collective-permute-start.6 = (bf16[2,32,80,128]{3,2,1,0:T(8,128)(2,1)S(1)}, bf16[2,32,80,128]{3,2,1,0:T(8,128)(2,1)S(1)}, u32[]{:S(2)}, u32[]{:S(2)}) collective-permute-start(bf16[2,32,80,128]{3,2,1,0:T(8,128)(2,1)S(1)} %bitcast.11), channel_id=1, source_target_pairs={{0,1},{1,0},{2,3},{3,2},{4,5},{5,4},{6,7},{7,6},{8,9},{9,8},{10,11... | collective-permute-start | bytes 3932168 | tf_op jit(solution)/shard_map/ppermute | solution.py:426
  148.0 3.0 %collective-permute-start.2 = (bf16[2,2,128,256]{3,2,1,0:T(8,128)(2,1)S(1)}, bf16[2,2,128,256]{3,2,1,0:T(8,128)(2,1)S(1)}, u32[]{:S(2)}, u32[]{:S(2)}) collective-permute-start(bf16[2,2,128,256]{3,2,1,0:T(8,128)(2,1)S(1)} %get-tuple-element.42), channel_id=1, source_target_pairs={{0,1},{1,0},{2,3},{3,2},{4,5},{5,4},{6,7},{7,6},{8,9},{9,8},{10,11... | collective-permute-start | bytes 786440 | tf_op jit(solution)/shard_map/ppermute | solution.py:337
  148.0 6.1 %collective-permute-start.3 = (bf16[2,2,128,256]{3,2,1,0:T(8,128)(2,1)S(1)}, bf16[2,2,128,256]{3,2,1,0:T(8,128)(2,1)S(1)}, u32[]{:S(2)}, u32[]{:S(2)}) collective-permute-start(bf16[2,2,128,256]{3,2,1,0:T(8,128)(2,1)S(1)} %get-tuple-element.43), channel_id=1, source_target_pairs={{0,7},{1,2},{2,1},{3,4},{4,3},{5,6},{6,5},{7,0},{8,15},{9,10},{10,... | collective-permute-start | bytes 786440 | tf_op jit(solution)/shard_map/ppermute | solution.py:336

commit v3 on v2

v3 whole, which is shorter than its diff:
```python
import functools
import math

import jax
import jax.numpy as jnp
from jax import lax
from jax.experimental import pallas as pl
from jax.experimental.pallas import tpu as pltpu
from jax.sharding import Mesh, PartitionSpec as P

BF, F32 = jnp.bfloat16, jnp.float32
VM = pl.BlockSpec(memory_space=pltpu.VMEM)
HB = pl.BlockSpec(memory_space=pltpu.HBM)
GRANT = 24 << 20
FRAMES, HEIGHT, WIDTH, CHANS = 2, 4, 128, 256
WIDE, WIDER = HEIGHT + 2, HEIGHT + 4
BLOCKS = 16
PLACES = WIDE * WIDTH // BLOCKS
NOTE = 8
CHIPS = 64
GROUPS = 32
TAPS = 72
PACK = TAPS + 8


def sds(shape, dtype):
    return jax.ShapeDtypeStruct(shape, dtype)


def call(body, outs, ins, flops=0, scratch=(), aliases=None):
    ins = [i if isinstance(i, tuple) else (i, VM) for i in ins]
    outs = [o if isinstance(o, tuple) else (o, VM) for o in outs]
    nbytes = sum(math.prod(a.shape) * a.dtype.itemsize for a, _ in ins + outs)
    return pl.pallas_call(
        body,
        out_shape=[o for o, _ in outs],
        in_specs=[s for _, s in ins],
        out_specs=[s for _, s in outs],
        scratch_shapes=list(scratch),
        input_output_aliases=aliases or {},
        compiler_params=pltpu.CompilerParams(vmem_limit_bytes=GRANT),
        cost_estimate=pl.CostEstimate(flops=flops, bytes_accessed=nbytes, transcendentals=0),
    )(*[i for i, _ in ins])


def far(array):
    return array, HB


def fetch_wait(sems, *pairs):
    for i, (s, d) in enumerate(pairs):
        pltpu.make_async_copy(s, d, sems.at[i]).wait()


def fetch(sems, *pairs):
    copies = [pltpu.make_async_copy(s, d, sems.at[i]) for i, (s, d) in enumerate(pairs)]
    for copy in copies:
        copy.start()
    return copies


class Spot:
    def __init__(self):
        z = lax.axis_index("z")
        self.core = lax.axis_index("core")
        self.top = jnp.logical_and(z == 0, self.core == 0)
        self.bottom = jnp.logical_and(z == 3, self.core == 1)
        self.place = lax.axis_index("x") * 4 + lax.axis_index("y")


ROW_FLOPS = 2 * 9 * FRAMES * WIDTH * CHANS * CHANS


def col_shift(v, by):
    turned = pltpu.roll(v, by % WIDTH, 0)
    at = lax.broadcasted_iota(jnp.int32, v.shape, 0)
    return jnp.where(at == (0 if by == 1 else WIDTH - 1), 0.0, turned)


HALVES = [slice(0, 128), slice(128, 256)]


def conv(rows, weight, flipped):
    height = rows.shape[0] - 2
    lhs = jnp.concatenate([rows[a : a + height] for a in range(3)], axis=-1)
    lhs = lhs.reshape(height * WIDTH, 3 * CHANS)
    parts = []
    for b in range(3):
        if flipped:
            rhs = jnp.concatenate([weight[2 - a, 2 - b] for a in range(3)], axis=1)
            y = lax.dot_general(lhs, rhs, (((1,), (1,)), ((), ())), preferred_element_type=F32)
        else:
            rhs = jnp.concatenate([weight[a, b] for a in range(3)], axis=0)
            y = jnp.dot(lhs, rhs, preferred_element_type=F32)
        parts.append(y.reshape(height, WIDTH, CHANS))

    def block(h, half):
        left, mid, right = (part[h, :, half] for part in parts)
        return mid + col_shift(left, 1) + col_shift(right, -1)

    return block


def blocks(height):
    return [(h, half) for h in range(height) for half in HALVES]


def outer(spot, h, v):
    if h == 0:
        return jnp.where(spot.top, 0.0, v)
    if h == WIDE - 1:
        return jnp.where(spot.bottom, 0.0, v)
    return v


def put_chunks(send, h, half, v):
    for k in range(WIDTH // 16):
        place = h * WIDTH + k * 16
        send[place // PLACES, place % PLACES : place % PLACES + 16, half] = v[
            k * 16 : (k + 1) * 16
        ].astype(BF)


def take_chunks(ref, h, half):
    pieces = []
    for k in range(WIDTH // 16):
        place = h * WIDTH + k * 16
        pieces.append(ref[place // PLACES, place % PLACES : place % PLACES + 16, half])
    return jnp.concatenate(pieces, axis=0).astype(F32)


def transpose_rows(v_ref, out_ref, rows, at_row):
    lane = lax.broadcasted_iota(jnp.int32, (CHANS, WIDTH), 1)
    for t in range(FRAMES):
        for h in range(rows):
            flat = v_ref[t, h].astype(F32).T
            at = pl.ds(at_row(t, h) * WIDTH, WIDTH)
            left = jnp.where(lane == 0, 0.0, pltpu.roll(flat, 1, 1))
            right = jnp.where(lane == WIDTH - 1, 0.0, pltpu.roll(flat, WIDTH - 1, 1))
            out_ref[0:CHANS, at] = left.astype(BF)
            out_ref[CHANS : 2 * CHANS, at] = flat.astype(BF)
            out_ref[2 * CHANS : 3 * CHANS, at] = right.astype(BF)


def ready_body(
    x_far, in_far, steps_far, rates_far, gain_far,
    x, in_weight, table, flat_mid, steps, rates, gain, sems,
):
    copies = fetch(
        sems,
        (x_far, x),
        (steps_far, steps),
        (rates_far, rates),
        (gain_far, gain),
        (in_far, in_weight),
    )
    for copy in copies[:4]:
        copy.wait()
    s0 = jnp.broadcast_to(steps[:, 0:1], (1, CHANS))
    s1 = jnp.broadcast_to(steps[:, 1:2], (1, CHANS))
    r = rates[...]
    lines = [jnp.exp(-r * s0), jnp.exp(-r * s1), s0, s1, r, gain[...], s0 + s1, r]
    for k, line in enumerate(lines):
        table[k : k + 1, :] = line
    transpose_rows(x, flat_mid, HEIGHT, lambda t, h: t * HEIGHT + h)
    copies[4].wait()


def place_halos(spot, from_core, from_chip, above, below):
    @pl.when(spot.core == 0)
    def _():
        above[...] = from_chip[...]
        below[...] = from_core[...]

    @pl.when(spot.core == 1)
    def _():
        above[...] = from_core[...]
        below[...] = from_chip[...]

    @pl.when(spot.top)
    def _():
        above[...] = jnp.zeros_like(above)

    @pl.when(spot.bottom)
    def _():
        below[...] = jnp.zeros_like(below)


def drive_body(
    x, from_core, from_chip, weight, table, local, send, flat_edge, above, below, edges
):
    spot = Spot()
    place_halos(spot, from_core, from_chip, above, below)
    for t in range(FRAMES):
        rows = jnp.concatenate([above[t], x[t], below[t]], axis=0)
        drive = conv(rows, weight, False)
        for h, half in blocks(WIDE):
            v = outer(spot, h, drive(h, half))
            if t == 1:
                v = table[1:2, half] * local[0, h, :, half] + v
                put_chunks(send, h, half, v)
            local[t, h, :, half] = v
    total = jnp.broadcast_to(table[6:7, :][None], (BLOCKS, NOTE, CHANS))
    row = lax.broadcasted_iota(jnp.int32, total.shape, 1)
    one = total.astype(BF).astype(F32)
    two = (total - one).astype(BF).astype(F32)
    three = total - one - two
    send[:, PLACES : PLACES + NOTE, :] = jnp.where(
        row == 0, one, jnp.where(row == 1, two, jnp.where(row == 2, three, 0.0))
    ).astype(BF)
    edges[:, 0:2] = above[...]
    edges[:, 2:4] = below[...]
    transpose_rows(edges, flat_edge, 4, lambda t, h: t * 4 + h)


def forward_scan_body(got, table, send, block_decays):
    carry = jnp.zeros((PLACES, CHANS), F32)
    for k in range(BLOCKS):
        send[k] = carry.astype(BF)
        span = jnp.sum(got[k, PLACES : PLACES + NOTE, :].astype(F32), axis=0, keepdims=True)
        d = jnp.exp(-table[4:5, :] * span)
        block_decays[pl.ds(k, 1), :] = d
        carry = d * carry + got[k, 0:PLACES, :].astype(F32)


def backward_scan_body(got, block_decays, send):
    carry = jnp.zeros((PLACES, CHANS), F32)
    for k in reversed(range(BLOCKS)):
        send[k] = carry.astype(BF)
        carry = block_decays[pl.ds(k, 1), :] * carry + got[k].astype(F32)


GELU_A = math.sqrt(2 / math.pi)


def spread(vector, extra):
    row = lax.broadcasted_iota(jnp.int32, (8, 128), 0) % 4
    low = jnp.broadcast_to(vector[:, 0:128], (8, 128))
    high = jnp.broadcast_to(vector[:, 128:256], (8, 128))
    low, high = (jnp.where(row == 0, v, 0.0) for v in (low, high))
    if extra is not None:
        low = jnp.where(row == 1, extra, low)
    return low, high


def split_pairs(both):
    row = lax.broadcasted_iota(jnp.int32, (8, 128), 0)
    top = both.astype(BF).astype(F32)
    return jnp.where(row < 4, top, both - top)


def joined(pairs):
    return pairs + pltpu.roll(pairs, 4, 0)


def middle_body(
    local, carry, x, cot, weight, table,
    out_far, gz_far, gz, state, state_f, local_adj, send, small, out, sems,
):
    spot = Spot()
    d0, d1 = table[0:1, :], table[1:2, :]
    for h, half in blocks(WIDE):
        c = take_chunks(carry, h, half)
        s0 = local[0, h, :, half] + d0[:, half] * c
        state_f[h, :, half] = s0
        state[0, h, :, half] = s0.astype(BF)
        s1 = local[1, h, :, half] + (d0 * d1)[:, half] * c
        state[1, h, :, half] = s1.astype(BF)
    totals = [jnp.zeros((8, 128), F32) for _ in HALVES]
    copies = []
    for t in (1, 0):
        pre_act = conv(state[t], weight, False)
        for h, half in blocks(HEIGHT):
            xt = x[t, h, :, half].astype(F32)
            z = pre_act(h, half) + table[5:6, half] * xt
            zz = z * z
            th = jnp.tanh(GELU_A * (z + 0.044715 * (zz * z)))
            gate = 0.5 * (1.0 + th)
            out[t, h, :, half] = (z * gate).astype(BF)
            slope = gate + 0.5 * z * (1.0 - th * th) * (GELU_A * (1.0 + 3 * 0.044715 * zz))
            g = cot[t, h, :, half].astype(F32) * slope
            gz[t, h, :, half] = g.astype(BF)
            k = HALVES.index(half)
            totals[k] = totals[k] + jnp.sum((g * xt).reshape(WIDTH // 8, 8, 128), axis=0)
        copies += fetch(sems.at[t], (out.at[t], out_far.at[t]), (gz.at[t], gz_far.at[t]))
        blank = jnp.zeros((2, WIDTH, CHANS), BF)
        grad = conv(jnp.concatenate([blank, gz[t], blank], axis=0), weight, True)
        for h, half in blocks(WIDE):
            v = outer(spot, h, grad(h, half))
            if t == 0:
                v = v + d1[:, half] * local_adj[1, h, :, half]
                put_chunks(send, h, half, d0[:, half] * v)
            local_adj[t, h, :, half] = v
    total = jnp.concatenate([jnp.sum(v, axis=0, keepdims=True) for v in totals], axis=1)
    small[0], small[1] = spread(total, None)
    for copy in copies:
        copy.wait()


def pack_grad(core, g, a, scale, mine, theirs):
    for b in range(3):
        tap = (3 * a + b) * 8
        low = g[b * CHANS : (b + 1) * CHANS, 0:128] * scale
        high = g[b * CHANS : (b + 1) * CHANS, 128:256] * scale
        mine[:, tap : tap + 8, :] = (
            jnp.where(core == 0, low, high).astype(BF).reshape(GROUPS, 8, 128)
        )
        theirs[:, tap : tap + 8, :] = (
            jnp.where(core == 0, high, low).astype(BF).reshape(GROUPS, 8, 128)
        )


def pack_small(core, low, high, scale, mine, theirs):
    blank = jnp.zeros((GROUPS, 8, 128), BF)
    for ref, half in (
        (mine, jnp.where(core == 0, low, high)),
        (theirs, jnp.where(core == 0, high, low)),
    ):
        ref[:, TAPS:PACK, :] = blank
        ref[0, TAPS:PACK, :] = split_pairs(half * scale).astype(BF)


def out_grad_body(scale, state, gz, small, mine, theirs, flat):
    spot = Spot()
    transpose_rows(state, flat, WIDE, lambda t, h: t * WIDE + h)
    rhs = gz[...].reshape(FRAMES * HEIGHT * WIDTH, CHANS)
    for a in range(3):
        lhs = jnp.concatenate(
            [flat[:, pl.ds((t * WIDE + a) * WIDTH, HEIGHT * WIDTH)] for t in range(FRAMES)], axis=1
        )
        g = jnp.dot(lhs, rhs, preferred_element_type=F32)
        pack_grad(spot.core, g, a, scale, mine, theirs)
    pack_small(spot.core, small[0], small[1], scale, mine, theirs)


def in_grad_body(
    scale, step_scale, local, incoming, state_f, carry, table, flat_mid, flat_edge, out_theirs,
    mine, theirs, adj_far, to_core, to_chip, adj, sems,
):
    spot = Spot()
    d0, d1 = table[0:1, :], table[1:2, :]
    sums = [[jnp.zeros((8, 128), F32) for _ in HALVES] for _ in range(FRAMES)]
    for h, half in blocks(WIDE):
        c = take_chunks(incoming, h, half)
        a0 = local[0, h, :, half] + d1[:, half] * c
        a1 = local[1, h, :, half] + c
        adj[0, h, :, half] = a0.astype(BF)
        adj[1, h, :, half] = a1.astype(BF)
        k = HALVES.index(half)
        pairs = ((a0, take_chunks(carry, h, half)), (a1, state_f[h, :, half]))
        for t, (a, earlier) in enumerate(pairs):
            sums[t][k] = sums[t][k] + jnp.sum((a * earlier).reshape(WIDTH // 8, 8, 128), axis=0)
    up, down = adj.at[:, 0:2], adj.at[:, WIDE - 2 :]

    @pl.when(spot.core == 0)
    def _():
        fetch(sems, (up, to_chip), (down, to_core))

    @pl.when(spot.core == 1)
    def _():
        fetch(sems, (down, to_chip), (up, to_core))

    others = fetch(sems.at[2:4], (adj, adj_far), (out_theirs, theirs.at[0]))
    rhs = adj[...].reshape(FRAMES * WIDE * WIDTH, CHANS)
    for a in range(3):
        pieces = []
        for t in range(FRAMES):
            at = t * 4 * WIDTH
            if a < 2:
                pieces.append(flat_edge[:, at + a * WIDTH : at + 2 * WIDTH])
            pieces.append(flat_mid[:, at : at + 4 * WIDTH])
            if a > 0:
                pieces.append(flat_edge[:, at + 2 * WIDTH : at + (2 + a) * WIDTH])
        g = jnp.dot(jnp.concatenate(pieces, axis=1), rhs, preferred_element_type=F32)
        pack_grad(spot.core, g, a, scale, mine, theirs.at[1])
    k0, k1 = (
        jnp.concatenate([jnp.sum(v, axis=0, keepdims=True) for v in pair], axis=1) * d
        for pair, d in zip(sums, (d0, d1))
    )
    rate_part = (k0 * table[2:3, :] + k1 * table[3:4, :]) * (-scale)
    s0 = jnp.sum(k0 * table[4:5, :], axis=1, keepdims=True) * (-step_scale)
    s1 = jnp.sum(k1 * table[4:5, :], axis=1, keepdims=True) * (-step_scale)
    lane = lax.broadcasted_iota(jnp.int32, (8, 128), 1)
    at = spot.place * FRAMES
    low, high = spread(rate_part, jnp.where(lane == at, s0, jnp.where(lane == at + 1, s1, 0.0)))
    pack_small(spot.core, low, high, 1.0, mine, theirs.at[1])
    fetch_wait(sems, (up, to_chip), (down, to_core))
    for copy in others:
        copy.wait()


def grad_inputs_body(
    adj_far, core_far, chip_far, weight_far, gain_far, gz_far,
    out, adj, from_core, from_chip, weight, gain, gz, above, below, sems,
):
    spot = Spot()
    copies = fetch(
        sems,
        (core_far, from_core),
        (chip_far, from_chip),
        (adj_far, adj),
        (weight_far, weight),
        (gain_far, gain),
        (gz_far, gz),
    )
    for copy in copies:
        copy.wait()
    place_halos(spot, from_core, from_chip, above, below)
    for t in range(FRAMES):
        up = (adj[t, 0:2].astype(F32) + above[t].astype(F32)).astype(BF)
        down = (adj[t, WIDE - 2 :].astype(F32) + below[t].astype(F32)).astype(BF)
        rows = jnp.concatenate([up, adj[t, 2 : WIDE - 2], down], axis=0)
        grad = conv(rows, weight, True)
        for h, half in blocks(HEIGHT):
            direct = gain[:, half] * gz[t, h, :, half].astype(F32)
            out[t, h, :, half] = (grad(h, half) + direct).astype(BF)


def pair_sum_body(out_own, in_own, both_got, send):
    for g, own in enumerate((out_own, in_own)):
        got = both_got.at[g]
        for k in range(GROUPS):
            send[g, k] = (own[k].astype(F32) + got[k].astype(F32)).astype(BF)
        pairs = own[0, TAPS:PACK, :].astype(F32) + got[0, TAPS:PACK, :].astype(F32)
        send[g, 0, TAPS:PACK, :] = split_pairs(joined(pairs)).astype(BF)


def all_sum_body(got, send):
    total = jnp.zeros((PACK, 128), F32)
    for k in range(CHIPS):
        total = total + got[k].astype(F32)
    extras = split_pairs(joined(total[TAPS:PACK]))
    total = jnp.concatenate([total[0:TAPS], extras], axis=0).astype(BF)
    send[...] = jnp.broadcast_to(total[None], (CHIPS, PACK, 128))


def write_half(src, lane_half, grads, stage, sems):
    lanes = pl.ds(pl.multiple_of(lane_half * 128, 128), 128)
    copies = []
    for g, grad in enumerate(grads):
        for a in range(3):
            for b in range(3):
                tap = (3 * a + b) * 8
                part = src[g, :, tap : tap + 8, :].astype(F32)
                stage[g, a, b] = part.reshape(CHANS, 128)
            copy = pltpu.make_async_copy(
                stage.at[g, a], grad.at[a, :, :, lanes], sems.at[3 * g + a]
            )
            copy.start()
            copies.append(copy)
    return copies


def unpack_own_body(own, grad_out, grad_in, stage, sems):
    for copy in write_half(own, Spot().core, (grad_out, grad_in), stage, sems):
        copy.wait()


def unpack_other_body(
    own, got, out_half, in_half, grad_out, grad_in, skip, rate, step, stage, sems
):
    del out_half, in_half
    spot = Spot()
    copies = write_half(got, 1 - spot.core, (grad_out, grad_in), stage, sems)

    def smalls(low, high):
        for g, vector in enumerate((skip, rate)):
            for lg, src in enumerate((low, high)):
                extras = joined(src[g, 0, TAPS:PACK, :].astype(F32))
                vector[lg : lg + 1, :] = extras[0:1]
                if g == 1 and lg == 0:
                    turned = pltpu.roll(extras, (128 - spot.place * FRAMES) % 128, 1)
                    step[...] = turned[1:2, 0:FRAMES]

    @pl.when(spot.core == 0)
    def _():
        smalls(own, got)

    @pl.when(spot.core == 1)
    def _():
        smalls(got, own)

    for copy in copies:
        copy.wait()


ROWS_AXES = ("z", "core")
TM_AXES = ("x", "y")
CORE_PAIRS = [(i, i ^ 1) for i in range(8)]
CHIP_PAIRS = [(i, (i + 1) % 8 if i % 2 else (i - 1) % 8) for i in range(8)]


def halos(to_core, to_chip):
    from_chip = lax.ppermute(to_chip, ROWS_AXES, CHIP_PAIRS)
    from_core = lax.ppermute(to_core, ROWS_AXES, CORE_PAIRS)
    return from_core, from_chip


def swap(chunks, axes):
    return lax.all_to_all(chunks, axes, 0, 0)


def vmem(shape, dtype=BF):
    return pltpu.VMEM(shape, dtype)


def sems(*shape):
    return pltpu.SemaphoreType.DMA(shape)


def on_device(inputs, in_weight, out_weight, skip_gain, rates, step_sizes, cotangent):
    scale = 1.0 / math.sqrt(32 * 32 * 128)
    step_scale = 1.0 / math.sqrt(1048576)
    core = lax.axis_index("core")
    field = (FRAMES, HEIGHT, WIDTH, CHANS)
    wide = (FRAMES, WIDE, WIDTH, CHANS)
    edge = (FRAMES, 2, WIDTH, CHANS)
    kernel = (3, 3, CHANS, CHANS)
    chunk = sds((BLOCKS, PLACES, CHANS), BF)
    packed = sds((GROUPS, PACK, 128), BF)
    flat = sds((3 * CHANS, FRAMES * 4 * WIDTH), BF)
    gain = skip_gain[None, :]

    to_core = lax.dynamic_slice(inputs, (0, 2 - 2 * core, 0, 0), edge)
    to_chip = lax.dynamic_slice(inputs, (0, 2 * core, 0, 0), edge)
    from_core, from_chip = halos(to_core, to_chip)
    x, in_w, table, flat_mid = call(
        ready_body,
        [sds(field, BF), sds(kernel, BF), sds((8, CHANS), F32), flat],
        [far(a) for a in (inputs, in_weight, step_sizes[None, :], rates[None, :], gain)],
        2 * ROW_FLOPS,
        [vmem((1, FRAMES), F32), vmem((1, CHANS), F32), vmem((1, CHANS), F32), sems(5)],
    )
    local, send, flat_edge = call(
        drive_body,
        [sds(wide, F32), sds((BLOCKS, PLACES + NOTE, CHANS), BF), flat],
        [x, from_core, from_chip, in_w, table],
        WIDE * ROW_FLOPS,
        [vmem(edge), vmem(edge), vmem(field)],
    )
    got = swap(send, TM_AXES)
    send, block_decays = call(forward_scan_body, [chunk, sds((BLOCKS, CHANS), F32)], [got, table])
    carry = swap(send, TM_AXES)
    outputs, gz_far, gz, state, state_f, local_adj, send, small = call(
        middle_body,
        [
            far(sds(field, BF)),
            far(sds(field, BF)),
            sds(field, BF),
            sds(wide, BF),
            sds(wide[1:], F32),
            sds(wide, F32),
            chunk,
            sds((2, 8, 128), F32),
        ],
        [local, carry, x, cotangent, out_weight, table],
        (HEIGHT + WIDE) * ROW_FLOPS,
        [vmem(field), sems(FRAMES, 2)],
    )
    out_mine, out_theirs = call(
        functools.partial(out_grad_body, scale),
        [packed, packed],
        [state, gz, small],
        HEIGHT * ROW_FLOPS,
        [vmem((3 * CHANS, FRAMES * WIDE * WIDTH))],
    )
    send, out_mine, out_theirs = lax.optimization_barrier((send, out_mine, out_theirs))
    got = swap(send, TM_AXES)
    (send,) = call(backward_scan_body, [chunk], [got, block_decays])
    incoming = swap(send, TM_AXES)
    in_mine, theirs, adj_far, to_core, to_chip = call(
        functools.partial(in_grad_body, scale, step_scale),
        [
            packed,
            sds((2, GROUPS, PACK, 128), BF),
            far(sds(wide, BF)),
            far(sds(edge, BF)),
            far(sds(edge, BF)),
        ],
        [local_adj, incoming, state_f, carry, table, flat_mid, flat_edge, out_theirs],
        WIDE * ROW_FLOPS,
        [vmem(wide), sems(4)],
    )
    both_got = lax.ppermute(theirs, ROWS_AXES, CORE_PAIRS)
    from_core, from_chip = halos(to_core, to_chip)
    (send,) = call(
        pair_sum_body, [sds((2, GROUPS, PACK, 128), BF)], [out_mine, in_mine, both_got]
    )
    got = swap(send.reshape(CHIPS, PACK, 128), ("x", "y", "z"))
    (send,) = call(all_sum_body, [sds((CHIPS, PACK, 128), BF)], [got])
    send, from_core, from_chip = lax.optimization_barrier((send, from_core, from_chip))
    own = swap(send, ("x", "y", "z"))
    (grad_inputs,) = call(
        grad_inputs_body,
        [sds(field, BF)],
        [far(a) for a in (adj_far, from_core, from_chip, in_weight, gain, gz_far)],
        HEIGHT * ROW_FLOPS,
        [
            vmem(wide),
            vmem(edge),
            vmem(edge),
            vmem(kernel),
            vmem((1, CHANS), F32),
            vmem(field),
            vmem(edge),
            vmem(edge),
            sems(6),
        ],
    )
    own, grad_inputs = lax.optimization_barrier((own, grad_inputs))
    own = own.reshape(2, GROUPS, PACK, 128)
    other = lax.ppermute(own, ROWS_AXES, CORE_PAIRS)
    weights = sds(kernel, F32)
    half = sds((2, 128), F32)
    stage = vmem((2, 3, 3, CHANS, 128), F32)
    grad_out_weight, grad_in_weight = call(
        unpack_own_body, [far(weights), far(weights)], [own], 0, [stage, sems(6)]
    )
    grad_out_weight, grad_in_weight, grad_skip, grad_rates, grad_steps = call(
        unpack_other_body,
        [far(weights), far(weights), half, half, sds((1, FRAMES), F32)],
        [own, other, far(grad_out_weight), far(grad_in_weight)],
        0,
        [stage, sems(6)],
        {2: 0, 3: 1},
    )
    return (
        outputs,
        grad_inputs,
        grad_in_weight,
        grad_out_weight,
        grad_skip.reshape(CHANS),
        grad_rates.reshape(CHANS),
        grad_steps.reshape(FRAMES),
    )


def solution(mesh):
    fine = Mesh(mesh.devices.reshape(4, 4, 4, 2), ("x", "y", "z", "core"))
    spread_out = P(TM_AXES, ROWS_AXES, None, None)
    placed = (spread_out, P(), P(), P(), P(), P(TM_AXES), spread_out)
    return jax.shard_map(
        on_device,
        mesh=fine,
        in_specs=placed,
        out_specs=(spread_out, spread_out, P(), P(), P(), P(), P(TM_AXES)),
        check_vma=False,
    )
```

time: 161 us -> 148 us (0.919)
  blocking collectives: 90.5 us -> 51.5 us
  waiting for transfers between devices: 11.5 us -> 36.8 us
  starting transfers between devices: 21.6 us -> 28.5 us
  local copies, waits for them, and re-layouts: 13.9 us -> 7.24 us
    all_to_all x5 -> x4, blocking collectives: 90.5 us -> 51.5 us  [swap(): return lax.all_to_all(chunks, axes, 0, 0)]
    all_to_all x1 -> x2, waiting for transfers between devices: 0.01 us -> 32.9 us  [swap(): return lax.all_to_all(chunks, axes, 0, 0)]
    all_to_all x1 -> x2, starting transfers between devices: 3.55 us -> 13.7 us  [swap(): return lax.all_to_all(chunks, axes, 0, 0)]
    ppermute x2, waiting for transfers between devices: 7.37 us -> 0.01 us  [halos(): from_chip = lax.ppermute(to_chip, ROWS_AXES, CHIP_PAIRS)]
    unnamed x48 -> x22, local copies, waits for them, and re-layouts: 12.8 us -> 6.17 us
    ppermute x2 -> x1, starting transfers between devices: 10.6 us -> 5.14 us  [on_device(): both_got = lax.ppermute(theirs, ROWS_AXES, CORE_PAIRS)]
    ppermute x2, waiting for transfers between devices: 2.35 us -> 0.01 us  [halos(): from_core = lax.ppermute(to_core, ROWS_AXES, CORE_PAIRS)]
    ppermute x2, starting transfers between devices: 2.38 us -> 4.38 us  [halos(): from_chip = lax.ppermute(to_chip, ROWS_AXES, CHIP_PAIRS)]
  transfers between devices with their start and end apart: 8 -> 8, of which waited for: 4 -> 4; matrix products, arithmetic and copies ran while one was open for 0% -> 0% of each run, Pallas kernels for 6% -> 5%
where the time goes in v3:
time: 148 us; the launch traced here: 147 us
  blocking collectives  51.5 us (35%)
  waiting for transfers between devices  36.8 us (25%)
  starting transfers between devices  28.5 us (19%)
  Pallas kernels  22.3 us (15%)
  local copies, waits for them, and re-layouts  7.24 us (5%)
    all_to_all x4, blocking collectives, swap(): return lax.all_to_all(chunks, axes, 0, 0)  51.5 us
    all_to_all x2, waiting for transfers between devices, swap(): return lax.all_to_all(chunks, axes, 0, 0)  32.9 us
    pallas_call x12, Pallas kernels, call(): pl.pallas_call(body, out_shape=[o for o, _ in outs], in_specs=[s for _, s...  22.3 us
    all_to_all x2, starting transfers between devices, swap(): return lax.all_to_all(chunks, axes, 0, 0)  13.7 us
    unnamed x22, local copies, waits for them, and re-layouts  6.17 us
    ppermute x1, starting transfers between devices, on_device(): both_got = lax.ppermute(theirs, ROWS_AXES, CORE_PAIRS)  5.14 us
    ppermute x2, starting transfers between devices, halos(): from_chip = lax.ppermute(to_chip, ROWS_AXES, CHIP_PAIRS)  4.38 us
  transfers between devices with their start and end apart: 8, of which 4 were waited for; matrix products, arithmetic and copies ran while one was open for 0% of the time, Pallas kernels for 5%

profile of v3, /device:TPU:1, one launch (start us, length us, event | category | flops | bytes accessed | tf_op | source)
XLA Modules:
  0.0 147.2 jit_solution(12982109782805847651)
XLA Ops:
  0.6 1.1 constant_dynamic-slice_fusion
  1.7 3.1 %collective-permute-start.1 = (bf16[2,2,128,256]{3,2,1,0:T(8,128)(2,1)S(1)}, bf16[2,2,128,256]{3,2,1,0:T(8,128)(2,1)S(1)}, u32[]{:S(2)}, u32[]{:S(2)}) collective-permute-start(bf16[2,2,128,256]{3,2,1,0:T(8,128)(2,1)S(1)} %get-tuple-element.85), channel_id=1, source_target_pairs={{0,7},{1,2},{2,1},{3,4},{4,3},{5,6},{6,5},{7,0},{8,15},{9,10},{10,... | collective-permute-start | bytes 786440 | tf_op jit(solution)/shard_map/ppermute | solution.py:494
  4.8 2.0 %collective-permute-start = (bf16[2,2,128,256]{3,2,1,0:T(8,128)(2,1)S(1)}, bf16[2,2,128,256]{3,2,1,0:T(8,128)(2,1)S(1)}, u32[]{:S(2)}, u32[]{:S(2)}) collective-permute-start(bf16[2,2,128,256]{3,2,1,0:T(8,128)(2,1)S(1)} %get-tuple-element.86), channel_id=1, source_target_pairs={{0,1},{1,0},{2,3},{3,2},{4,5},{5,4},{6,7},{7,6},{8,9},{9,8},{10,11... | collective-permute-start | bytes 786440 | tf_op jit(solution)/shard_map/ppermute | solution.py:495
  6.8 0.0 copy-start
  6.8 1.0 copy-done
  7.8 0.0 copy-start.2
  7.8 1.3 copy-done.2
  9.1 0.0 copy-start.5
  9.1 0.7 copy-done.5
  9.8 0.0 copy-start.6
  9.8 0.7 copy-done.6
  10.4 0.0 copy-start.8
  10.4 0.7 copy-done.8
  11.1 0.8 shard_map.126
  12.0 0.0 collective-permute-done.1.from_chip
  12.0 0.0 collective-permute-done.from_core
  12.0 2.1 %shard_map.127 = (f32[2,6,128,256]{3,2,1,0:T(8,128)S(1)}, bf16[16,56,256]{2,1,0:T(8,128)(2,1)S(1)}, bf16[768,1024]{1,0:T(8,128)(2,1)S(1)}) custom-call(bf16[2,4,128,256]{3,2,1,0:T(8,128)(2,1)S(1)} %get-tuple-element.46.x, bf16[2,2,128,256]{3,2,1,0:T(8,128)(2,1)S(1)} %collective-permute-done.from_core, ...), custom_call_target="tpu_custom_call" | custom-call | flops 1811939328 | bytes 5840896 | tf_op jit(solution)/shard_map/pallas_call | solution.py:34
  14.1 0.0 copy-start.1
  14.1 0.0 copy-start.4
  14.1 16.3 %all_to_all.30.got = bf16[16,56,256]{2,1,0:T(8,128)(2,1)S(1)} all-to-all(bf16[16,56,256]{2,1,0:T(8,128)(2,1)S(1)} %get-tuple-element.50), channel_id=1, replica_groups=mesh['x'=4,'y'=4,'z'=4,'core'=2] {'x','y'}, dimensions={0} | all-to-all | bytes 917504 | tf_op jit(solution)/shard_map/all_to_all | solution.py:500
  30.4 0.1 shard_map.128
  30.6 12.1 %all_to_all.31.carry = bf16[16,48,256]{2,1,0:T(8,128)(2,1)S(1)} all-to-all(bf16[16,48,256]{2,1,0:T(8,128)(2,1)S(1)} %get-tuple-element.51), channel_id=1, replica_groups=mesh['x'=4,'y'=4,'z'=4,'core'=2] {'x','y'}, dimensions={0} | all-to-all | bytes 786432 | tf_op jit(solution)/shard_map/all_to_all | solution.py:500
  42.7 0.0 copy-done.1
  42.7 0.0 copy-done.4
  42.7 5.2 %shard_map.129 = (bf16[2,4,128,256]{3,2,1,0:T(8,128)(2,1)}, bf16[2,4,128,256]{3,2,1,0:T(8,128)(2,1)S(1)}, bf16[2,4,128,256]{3,2,1,0:T(8,128)(2,1)S(1)}, bf16[2,6...) custom-call(f32[2,6,128,256]{3,2,1,0:T(8,128)S(1)} %get-tuple-elemen, ...), custom_call_target="tpu_custom_call" | custom-call | flops 3019898880 | bytes 9322496 | tf_op jit(solution)/shard_map/pallas_call | solution.py:34
  47.9 0.0 copy-start.9
  47.9 0.8 copy-done.9
  48.7 1.7 %shard_map.130 = (bf16[32,80,128]{2,1,0:T(8,128)(2,1)S(1)}, bf16[32,80,128]{2,1,0:T(8,128)(2,1)S(1)}) custom-call(bf16[2,6,128,256]{3,2,1,0:T(8,128)(2,1)S(1)} %get-tuple-element.54.state, bf16[2,4,128,256]{3,2,1,0:T(8,128)(2,1)S(1)} %get-tuple-element.55.gz, f32[2,8,128]{2,1,0:T(8,128)S(1)} %get-tuple-element.56.small), custom_call_target="tpu_custom_call" | custom-call | flops 1207959552 | bytes 2629632 | tf_op jit(solution)/shard_map/pallas_call | solution.py:34
  50.4 11.6 %all_to_all.32.got = bf16[16,48,256]{2,1,0:T(8,128)(2,1)S(1)} all-to-all(bf16[16,48,256]{2,1,0:T(8,128)(2,1)S(1)} %get-tuple-element.61), channel_id=1, replica_groups=mesh['x'=4,'y'=4,'z'=4,'core'=2] {'x','y'}, dimensions={0} | all-to-all | bytes 786432 | tf_op jit(solution)/shard_map/all_to_all | solution.py:500
  62.0 0.1 shard_map.131
  62.1 11.5 %all_to_all.33.incoming = bf16[16,48,256]{2,1,0:T(8,128)(2,1)S(1)} all-to-all(bf16[16,48,256]{2,1,0:T(8,128)(2,1)S(1)} %shard_map.131), channel_id=1, replica_groups=mesh['x'=4,'y'=4,'z'=4,'core'=2] {'x','y'}, dimensions={0} | all-to-all | bytes 786432 | tf_op jit(solution)/shard_map/all_to_all | solution.py:500
  73.5 2.6 %shard_map.132 = (bf16[32,80,128]{2,1,0:T(8,128)(2,1)S(1)}, bf16[2,32,80,128]{3,2,1,0:T(8,128)(2,1)S(1)}, bf16[2,6,128,256]{3,2,1,0:T(8,128)(2,1)S(1)}, bf16[2,2...) custom-call(f32[2,6,128,256]{3,2,1,0:T(8,128)S(1)} %get-tuple-element.60.local, ...), custom_call_target="tpu_custom_call" | custom-call | flops 1811939328 | bytes 10231808 | tf_op jit(solution)/shard_map/pallas_call | solution.py:34
  76.2 5.1 %collective-permute-start.2 = (bf16[2,32,80,128]{3,2,1,0:T(8,128)(2,1)S(1)}, bf16[2,32,80,128]{3,2,1,0:T(8,128)(2,1)S(1)}, u32[]{:S(2)}, u32[]{:S(2)}) collective-permute-start(bf16[2,32,80,128]{3,2,1,0:T(8,128)(2,1)S(1)} %get-tuple-element.68), channel_id=1, source_target_pairs={{0,1},{1,0},{2,3},{3,2},{4,5},{5,4},{6,7},{7,6},{8,9},{9,8},{10,11... | collective-permute-start | bytes 3932168 | tf_op jit(solution)/shard_map/ppermute | solution.py:584
  81.3 2.7 %collective-permute-done.2.both_got = bf16[2,32,80,128]{3,2,1,0:T(8,128)(2,1)S(1)} collective-permute-done((bf16[2,32,80,128]{3,2,1,0:T(8,128)(2,1)S(1)}, bf16[2,32,80,128]{3,2,1,0:T(8,128)(2,1)S(1)}, u32[]{:S(2)}, u32[]{:S(2)}) %collective-permute-start.2) | collective-permute-done | bytes 1310752 | tf_op jit(solution)/shard_map/ppermute | solution.py:584
  84.0 1.4 shard_map.133
  85.4 6.0 %all-to-all-start.4 = ((bf16[64,80,128]{2,1,0:T(8,128)(2,1)}), bf16[64,80,128]{2,1,0:T(8,128)(2,1)S(1)}, u32[]{:S(2)}, u32[]{:S(2)}) async-start(bf16[64,80,128]{2,1,0:T(8,128)(2,1)} %bitcast.3), calls=%async_computation.4 | async-start | bytes 2621440 | tf_op jit(solution)/shard_map/all_to_all | solution.py:500
  91.4 0.7 collective-permute-start.3
  92.1 1.3 collective-permute-start.4
  93.4 17.6 %all-to-all-done.4.got = bf16[64,80,128]{2,1,0:T(8,128)(2,1)S(1)} async-done(((bf16[64,80,128]{2,1,0:T(8,128)(2,1)}), bf16[64,80,128]{2,1,0:T(8,128)(2,1)S(1)}, u32[]{:S(2)}, u32[]{:S(2)}) %all-to-all-start.4) | async-done | bytes 1310752 | tf_op jit(solution)/shard_map/all_to_all | solution.py:500
  111.0 1.3 shard_map.134
  112.3 0.0 copy-start.3
  112.3 0.0 copy-start.7
  112.3 0.0 collective-permute-done.3.core_far
  112.3 0.0 collective-permute-done.4.chip_far
  112.3 7.6 %all-to-all-start.5 = ((bf16[64,80,128]{2,1,0:T(8,128)(2,1)}), bf16[64,80,128]{2,1,0:T(8,128)(2,1)S(1)}, u32[]{:S(2)}, u32[]{:S(2)}) async-start(bf16[64,80,128]{2,1,0:T(8,128)(2,1)} %shard_map.134), calls=%async_computation.5 | async-start | bytes 2621440 | tf_op jit(solution)/shard_map/all_to_all | solution.py:500
  120.0 0.0 copy-done.3
  120.0 0.0 copy-done.7
  120.0 0.0 copy-start.10
  120.0 1.0 copy-done.10
  121.0 3.4 %shard_map.135 = bf16[2,4,128,256]{3,2,1,0:T(8,128)(2,1)} custom-call(bf16[2,6,128,256]{3,2,1,0:T(8,128)(2,1)S(1)} %get-tuple-element.72.adj_far, bf16[2,2,128,256]{3,2,1,0:T(8,128)(2,1)} %collective-permute-done.3.core_far, bf16[2,2,128,256]{3,2,1,0:T(8,128)(2,1)} %collective-permute-done.4.chip_far, bf16[3,3,256,256]{3,2,1,0:T(8,128)(2,1)S(1)} %copy-done.3, ...), custom_call_target="tpu_custom_call" | custom-call | flops 1207959552 | bytes 3539968 | tf_op jit(solution)/shard_map/pallas_call | solution.py:34
  124.4 15.3 %all-to-all-done.5 = bf16[64,80,128]{2,1,0:T(8,128)(2,1)S(1)} async-done(((bf16[64,80,128]{2,1,0:T(8,128)(2,1)}), bf16[64,80,128]{2,1,0:T(8,128)(2,1)S(1)}, u32[]{:S(2)}, u32[]{:S(2)}) %all-to-all-start.5) | async-done | bytes 1310752 | tf_op jit(solution)/shard_map/all_to_all | solution.py:500
  139.8 2.6 %collective-permute-start.5 = (bf16[2,32,80,128]{3,2,1,0:T(8,128)(2,1)S(1)}, bf16[2,32,80,128]{3,2,1,0:T(8,128)(2,1)S(1)}, u32[]{:S(2)}, u32[]{:S(2)}) collective-permute-start(bf16[2,32,80,128]{3,2,1,0:T(8,128)(2,1)S(1)} %bitcast.8), channel_id=1, source_target_pairs={{0,1},{1,0},{2,3},{3,2},{4,5},{5,4},{6,7},{7,6},{8,9},{9,8},{10,11... | collective-permute-start | bytes 3932168 | tf_op jit(solution)/shard_map/ppermute | solution.py:612
  142.4 1.5 shard_map.136
  143.9 1.2 collective-permute-done.5.got
  145.0 2.0 %shard_map.137 = (f32[3,3,256,256]{3,2,1,0:T(8,128)}, f32[3,3,256,256]{3,2,1,0:T(8,128)}, f32[2,128]{1,0:T(2,128)}, f32[2,128]{1,0:T(2,128)}, f32[1,2]{1,0:T(1,128)}) custom-call(bf16[2,32,80,128]{3,2,1,0:T(8,128)(2,1)S(1)} %bitcast.10, bf16[2,32,80,128]{3,2,1,0:T(8,128)(2,1)S(1)} %collective-permute-done.5.got, ...), custom_call_target="tpu_custom_call", output_to_operand_aliasing={{0}: (2, {}), {1}: (3, {})} | custom-call | bytes 12060680 | tf_op jit(solution)/shard_map/pallas_call | solution.py:34
Async XLA Ops:
  1.7 10.2 %collective-permute-start.1 = (bf16[2,2,128,256]{3,2,1,0:T(8,128)(2,1)S(1)}, bf16[2,2,128,256]{3,2,1,0:T(8,128)(2,1)S(1)}, u32[]{:S(2)}, u32[]{:S(2)}) collective-permute-start(bf16[2,2,128,256]{3,2,1,0:T(8,128)(2,1)S(1)} %get-tuple-element.85), channel_id=1, source_target_pairs={{0,7},{1,2},{2,1},{3,4},{4,3},{5,6},{6,5},{7,0},{8,15},{9,10},{10,... | collective-permute-start | bytes 786440 | tf_op jit(solution)/shard_map/ppermute | solution.py:494
  4.8 7.1 %collective-permute-start = (bf16[2,2,128,256]{3,2,1,0:T(8,128)(2,1)S(1)}, bf16[2,2,128,256]{3,2,1,0:T(8,128)(2,1)S(1)}, u32[]{:S(2)}, u32[]{:S(2)}) collective-permute-start(bf16[2,2,128,256]{3,2,1,0:T(8,128)(2,1)S(1)} %get-tuple-element.86), channel_id=1, source_target_pairs={{0,1},{1,0},{2,3},{3,2},{4,5},{5,4},{6,7},{7,6},{8,9},{9,8},{10,11... | collective-permute-start | bytes 786440 | tf_op jit(solution)/shard_map/ppermute | solution.py:495
  6.8 1.0 copy-start
  7.8 1.3 copy-start.2
  9.1 0.7 copy-start.5
  9.8 0.7 copy-start.6
  10.4 0.7 copy-start.8
  14.1 28.6 %copy-start.1 = (bf16[3,3,256,256]{3,2,1,0:T(8,128)(2,1)S(1)}, bf16[3,3,256,256]{3,2,1,0:T(8,128)(2,1)}, u32[]{:S(2)}) copy-start(bf16[3,3,256,256]{3,2,1,0:T(8,128)(2,1)} %weight.1) | copy-start | bytes 3538948
  14.1 28.6 %copy-start.4 = (bf16[2,4,128,256]{3,2,1,0:T(8,128)(2,1)S(1)}, bf16[2,4,128,256]{3,2,1,0:T(8,128)(2,1)}, u32[]{:S(2)}) copy-start(bf16[2,4,128,256]{3,2,1,0:T(8,128)(2,1)} %cot.1) | copy-start | bytes 1572868
  47.9 0.8 copy-start.9
  76.2 7.8 %collective-permute-start.2 = (bf16[2,32,80,128]{3,2,1,0:T(8,128)(2,1)S(1)}, bf16[2,32,80,128]{3,2,1,0:T(8,128)(2,1)S(1)}, u32[]{:S(2)}, u32[]{:S(2)}) collective-permute-start(bf16[2,32,80,128]{3,2,1,0:T(8,128)(2,1)S(1)} %get-tuple-element.68), channel_id=1, source_target_pairs={{0,1},{1,0},{2,3},{3,2},{4,5},{5,4},{6,7},{7,6},{8,9},{9,8},{10,11... | collective-permute-start | bytes 3932168 | tf_op jit(solution)/shard_map/ppermute | solution.py:584
  85.4 25.6 %all-to-all-start.4 = ((bf16[64,80,128]{2,1,0:T(8,128)(2,1)}), bf16[64,80,128]{2,1,0:T(8,128)(2,1)S(1)}, u32[]{:S(2)}, u32[]{:S(2)}) async-start(bf16[64,80,128]{2,1,0:T(8,128)(2,1)} %bitcast.3), calls=%async_computation.4 | async-start | bytes 2621440 | tf_op jit(solution)/shard_map/all_to_all | solution.py:500
  91.4 20.9 %collective-permute-start.3 = (bf16[2,2,128,256]{3,2,1,0:T(8,128)(2,1)}, bf16[2,2,128,256]{3,2,1,0:T(8,128)(2,1)}, u32[]{:S(2)}, u32[]{:S(2)}) collective-permute-start(bf16[2,2,128,256]{3,2,1,0:T(8,128)(2,1)} %get-tuple-element.69), channel_id=1, source_target_pairs={{0,1},{1,0},{2,3},{3,2},{4,5},{5,4},{6,7},{7,6},{8,9},{9,8},{10,11... | collective-permute-start | bytes 786440 | tf_op jit(solution)/shard_map/ppermute | solution.py:495
  92.1 20.2 %collective-permute-start.4 = (bf16[2,2,128,256]{3,2,1,0:T(8,128)(2,1)S(1)}, bf16[2,2,128,256]{3,2,1,0:T(8,128)(2,1)}, u32[]{:S(2)}, u32[]{:S(2)}) collective-permute-start(bf16[2,2,128,256]{3,2,1,0:T(8,128)(2,1)S(1)} %get-tuple-element.70), channel_id=1, source_target_pairs={{0,7},{1,2},{2,1},{3,4},{4,3},{5,6},{6,5},{7,0},{8,15},{9,10},{10,... | collective-permute-start | bytes 786440 | tf_op jit(solution)/shard_map/ppermute | solution.py:494
  112.3 7.7 %copy-start.3 = (bf16[3,3,256,256]{3,2,1,0:T(8,128)(2,1)S(1)}, bf16[3,3,256,256]{3,2,1,0:T(8,128)(2,1)}, u32[]{:S(2)}) copy-start(bf16[3,3,256,256]{3,2,1,0:T(8,128)(2,1)} %weight_far.1) | copy-start | bytes 3538948
  112.3 7.7 %copy-start.7 = (f32[256]{0:T(256)S(1)}, f32[256]{0:T(256)}, u32[]{:S(2)}) copy-start(f32[256]{0:T(256)} %param.10) | copy-start | bytes 3076
  112.3 27.5 %all-to-all-start.5 = ((bf16[64,80,128]{2,1,0:T(8,128)(2,1)}), bf16[64,80,128]{2,1,0:T(8,128)(2,1)S(1)}, u32[]{:S(2)}, u32[]{:S(2)}) async-start(bf16[64,80,128]{2,1,0:T(8,128)(2,1)} %shard_map.134), calls=%async_computation.5 | async-start | bytes 2621440 | tf_op jit(solution)/shard_map/all_to_all | solution.py:500
  120.0 1.0 copy-start.10
  139.8 5.3 %collective-permute-start.5 = (bf16[2,32,80,128]{3,2,1,0:T(8,128)(2,1)S(1)}, bf16[2,32,80,128]{3,2,1,0:T(8,128)(2,1)S(1)}, u32[]{:S(2)}, u32[]{:S(2)}) collective-permute-start(bf16[2,32,80,128]{3,2,1,0:T(8,128)(2,1)S(1)} %bitcast.8), channel_id=1, source_target_pairs={{0,1},{1,0},{2,3},{3,2},{4,5},{5,4},{6,7},{7,6},{8,9},{9,8},{10,11... | collective-permute-start | bytes 3932168 | tf_op jit(solution)/shard_map/ppermute | solution.py:612

commit v4 on v3

--- a/solution.py
+++ b/solution.py
@@ -101,6 +101,27 @@
     return block
 
 
+def spread_conv(field, weight):
+    pieces = []
+    for first, count, taps in ((0, 1, (2,)), (1, 1, (1, 2)), (2, 2, (0, 1, 2)), (4, 1, (0, 1)), (5, 1, (0,))):
+        lhs = jnp.concatenate(
+            [field[:, first + a - 2 : first + a - 2 + count] for a in taps], axis=-1
+        ).reshape(FRAMES * count * WIDTH, len(taps) * CHANS)
+        parts = []
+        for b in range(3):
+            rhs = jnp.concatenate([weight[2 - a, 2 - b] for a in taps], axis=1)
+            y = lax.dot_general(lhs, rhs, (((1,), (1,)), ((), ())), preferred_element_type=F32)
+            parts.append(y.reshape(FRAMES, count, WIDTH, CHANS))
+        pieces += [(parts, k) for k in range(count)]
+
+    def block(t, h, half):
+        parts, k = pieces[h]
+        left, mid, right = (part[t, k, :, half] for part in parts)
+        return mid + col_shift(left, 1) + col_shift(right, -1)
+
+    return block
+
+
 def blocks(height):
     return [(h, half) for h in range(height) for half in HALVES]
 
@@ -142,28 +163,17 @@
             out_ref[2 * CHANS : 3 * CHANS, at] = right.astype(BF)
 
 
-def ready_body(
-    x_far, in_far, steps_far, rates_far, gain_far,
-    x, in_weight, table, flat_mid, steps, rates, gain, sems,
-):
-    copies = fetch(
-        sems,
-        (x_far, x),
-        (steps_far, steps),
-        (rates_far, rates),
-        (gain_far, gain),
-        (in_far, in_weight),
-    )
-    for copy in copies[:4]:
-        copy.wait()
-    s0 = jnp.broadcast_to(steps[:, 0:1], (1, CHANS))
-    s1 = jnp.broadcast_to(steps[:, 1:2], (1, CHANS))
-    r = rates[...]
-    lines = [jnp.exp(-r * s0), jnp.exp(-r * s1), s0, s1, r, gain[...], s0 + s1, r]
+def ready_body(x_far, in_far, params, x, in_weight, table, flat_mid, sems):
+    copies = fetch(sems, (x_far, x), (in_far, in_weight))
+    r = params[0:1, :]
+    s0 = jnp.broadcast_to(params[2:3, 0:1], (1, CHANS))
+    s1 = jnp.broadcast_to(params[2:3, 1:2], (1, CHANS))
+    lines = [jnp.exp(-r * s0), jnp.exp(-r * s1), s0, s1, r, params[1:2, :], s0 + s1, r]
     for k, line in enumerate(lines):
         table[k : k + 1, :] = line
+    copies[0].wait()
     transpose_rows(x, flat_mid, HEIGHT, lambda t, h: t * HEIGHT + h)
-    copies[4].wait()
+    copies[1].wait()
 
 
 def place_halos(spot, from_core, from_chip, above, below):
@@ -255,7 +265,7 @@
 
 def middle_body(
     local, carry, x, cot, weight, table,
-    out_far, gz_far, gz, state, state_f, local_adj, send, small, out, sems,
+    out_far, direct_far, gz, state, state_f, local_adj, send, small, out, direct, sems,
 ):
     spot = Spot()
     d0, d1 = table[0:1, :], table[1:2, :]
@@ -280,13 +290,14 @@
             slope = gate + 0.5 * z * (1.0 - th * th) * (GELU_A * (1.0 + 3 * 0.044715 * zz))
             g = cot[t, h, :, half].astype(F32) * slope
             gz[t, h, :, half] = g.astype(BF)
+            direct[t, h, :, half] = (table[5:6, half] * g).astype(BF)
             k = HALVES.index(half)
             totals[k] = totals[k] + jnp.sum((g * xt).reshape(WIDTH // 8, 8, 128), axis=0)
-        copies += fetch(sems.at[t], (out.at[t], out_far.at[t]), (gz.at[t], gz_far.at[t]))
-        blank = jnp.zeros((2, WIDTH, CHANS), BF)
-        grad = conv(jnp.concatenate([blank, gz[t], blank], axis=0), weight, True)
+        copies += fetch(sems.at[t], (out.at[t], out_far.at[t]), (direct.at[t], direct_far.at[t]))
+    grad = spread_conv(gz, weight)
+    for t in (1, 0):
         for h, half in blocks(WIDE):
-            v = outer(spot, h, grad(h, half))
+            v = outer(spot, h, grad(t, h, half))
             if t == 0:
                 v = v + d1[:, half] * local_adj[1, h, :, half]
                 put_chunks(send, h, half, d0[:, half] * v)
@@ -390,8 +401,8 @@
 
 
 def grad_inputs_body(
-    adj_far, core_far, chip_far, weight_far, gain_far, gz_far,
-    out, adj, from_core, from_chip, weight, gain, gz, above, below, sems,
+    adj_far, core_far, chip_far, weight_far, direct_far,
+    out_far, adj, from_core, from_chip, weight, direct, out, above, below, sems,
 ):
     spot = Spot()
     copies = fetch(
@@ -400,8 +411,7 @@
         (chip_far, from_chip),
         (adj_far, adj),
         (weight_far, weight),
-        (gain_far, gain),
-        (gz_far, gz),
+        (direct_far, direct),
     )
     for copy in copies:
         copy.wait()
@@ -412,26 +422,40 @@
         rows = jnp.concatenate([up, adj[t, 2 : WIDE - 2], down], axis=0)
         grad = conv(rows, weight, True)
         for h, half in blocks(HEIGHT):
-            direct = gain[:, half] * gz[t, h, :, half].astype(F32)
-            out[t, h, :, half] = (grad(h, half) + direct).astype(BF)
-
-
-def pair_sum_body(out_own, in_own, both_got, send):
+            own = direct[t, h, :, half].astype(F32)
+            out[t, h, :, half] = (grad(h, half) + own).astype(BF)
+    (copy,) = fetch(sems, (out, out_far))
+    copy.wait()
+
+
+def pair_sum_body(out_own, in_own, both_got, send_far, send, sems):
+    copies = []
     for g, own in enumerate((out_own, in_own)):
         got = both_got.at[g]
         for k in range(GROUPS):
             send[g, k] = (own[k].astype(F32) + got[k].astype(F32)).astype(BF)
-        pairs = own[0, TAPS:PACK, :].astype(F32) + got[0, TAPS:PACK, :].astype(F32)
-        send[g, 0, TAPS:PACK, :] = split_pairs(joined(pairs)).astype(BF)
-
-
-def all_sum_body(got, send):
+            if k == 0:
+                pairs = own[0, TAPS:PACK, :].astype(F32) + got[0, TAPS:PACK, :].astype(F32)
+                send[g, 0, TAPS:PACK, :] = split_pairs(joined(pairs)).astype(BF)
+            if k % 8 == 7:
+                part = slice(k - 7, k + 1)
+                copies += fetch(
+                    sems.at[g, k // 8 : k // 8 + 1], (send.at[g, part], send_far.at[g, part])
+                )
+    for copy in copies:
+        copy.wait()
+
+
+def all_sum_body(got, send_far, send, sems):
     total = jnp.zeros((PACK, 128), F32)
     for k in range(CHIPS):
         total = total + got[k].astype(F32)
     extras = split_pairs(joined(total[TAPS:PACK]))
     total = jnp.concatenate([total[0:TAPS], extras], axis=0).astype(BF)
-    send[...] = jnp.broadcast_to(total[None], (CHIPS, PACK, 128))
+    send[...] = jnp.broadcast_to(total[None], send.shape)
+    pairs = [(send, send_far.at[8 * k : 8 * k + 8]) for k in range(8)]
+    for copy in fetch(sems, *pairs):
+        copy.wait()
 
 
 def write_half(src, lane_half, grads, stage, sems):
@@ -519,7 +543,8 @@
     chunk = sds((BLOCKS, PLACES, CHANS), BF)
     packed = sds((GROUPS, PACK, 128), BF)
     flat = sds((3 * CHANS, FRAMES * 4 * WIDTH), BF)
-    gain = skip_gain[None, :]
+    params = jnp.concatenate([rates, skip_gain, jnp.pad(step_sizes, (0, CHANS - FRAMES))])
+    params = params.reshape(3, CHANS)
 
     to_core = lax.dynamic_slice(inputs, (0, 2 - 2 * core, 0, 0), edge)
     to_chip = lax.dynamic_slice(inputs, (0, 2 * core, 0, 0), edge)
@@ -527,9 +552,9 @@
     x, in_w, table, flat_mid = call(
         ready_body,
         [sds(field, BF), sds(kernel, BF), sds((8, CHANS), F32), flat],
-        [far(a) for a in (inputs, in_weight, step_sizes[None, :], rates[None, :], gain)],
+        [far(inputs), far(in_weight), params],
         2 * ROW_FLOPS,
-        [vmem((1, FRAMES), F32), vmem((1, CHANS), F32), vmem((1, CHANS), F32), sems(5)],
+        [sems(2)],
     )
     local, send, flat_edge = call(
         drive_body,
@@ -541,7 +566,7 @@
     got = swap(send, TM_AXES)
     send, block_decays = call(forward_scan_body, [chunk, sds((BLOCKS, CHANS), F32)], [got, table])
     carry = swap(send, TM_AXES)
-    outputs, gz_far, gz, state, state_f, local_adj, send, small = call(
+    outputs, direct, gz, state, state_f, local_adj, send, small = call(
         middle_body,
         [
             far(sds(field, BF)),
@@ -555,7 +580,7 @@
         ],
         [local, carry, x, cotangent, out_weight, table],
         (HEIGHT + WIDE) * ROW_FLOPS,
-        [vmem(field), sems(FRAMES, 2)],
+        [vmem(field), vmem(field), sems(FRAMES, 2)],
     )
     out_mine, out_theirs = call(
         functools.partial(out_grad_body, scale),
@@ -584,28 +609,39 @@
     both_got = lax.ppermute(theirs, ROWS_AXES, CORE_PAIRS)
     from_core, from_chip = halos(to_core, to_chip)
     (send,) = call(
-        pair_sum_body, [sds((2, GROUPS, PACK, 128), BF)], [out_mine, in_mine, both_got]
+        pair_sum_body,
+        [far(sds((2, GROUPS, PACK, 128), BF))],
+        [out_mine, in_mine, both_got],
+        0,
+        [vmem((2, GROUPS, PACK, 128)), sems(2, 4)],
     )
     got = swap(send.reshape(CHIPS, PACK, 128), ("x", "y", "z"))
-    (send,) = call(all_sum_body, [sds((CHIPS, PACK, 128), BF)], [got])
+    (send,) = call(
+        all_sum_body,
+        [far(sds((CHIPS, PACK, 128), BF))],
+        [got],
+        0,
+        [vmem((8, PACK, 128)), sems(8)],
+    )
     send, from_core, from_chip = lax.optimization_barrier((send, from_core, from_chip))
     own = swap(send, ("x", "y", "z"))
     (grad_inputs,) = call(
         grad_inputs_body,
-        [sds(field, BF)],
-        [far(a) for a in (adj_far, from_core, from_chip, in_weight, gain, gz_far)],
+        [far(sds(field, BF))],
+        [far(a) for a in (adj_far, from_core, from_chip, in_weight, direct)],
         HEIGHT * ROW_FLOPS,
         [
             vmem(wide),
             vmem(edge),
             vmem(edge),
             vmem(kernel),
-            vmem((1, CHANS), F32),
+            vmem(field),
             vmem(field),
             vmem(edge),
             vmem(edge),
-            sems(6),
+            sems(5),
         ],
+        {4: 0},
     )
     own, grad_inputs = lax.optimization_barrier((own, grad_inputs))
     own = own.reshape(2, GROUPS, PACK, 128)

time: 148 us -> 145 us (0.980)
  local copies, waits for them, and re-layouts: 7.24 us -> 3.41 us
    unnamed x22 -> x10, local copies, waits for them, and re-layouts: 6.17 us -> 2.33 us
  transfers between devices with their start and end apart: 8 -> 8, of which waited for: 4 -> 4; matrix products, arithmetic and copies ran while one was open for 0% -> 1% of each run, Pallas kernels for 5% -> 5%
where the time goes in v4:
time: 145 us
  blocking collectives  51.3 us (35%)
  waiting for transfers between devices  37.5 us (26%)
  starting transfers between devices  29.7 us (20%)
  Pallas kernels  20.9 us (14%)
  local copies, waits for them, and re-layouts  3.41 us (2%)
    all_to_all x4, blocking collectives, swap(): return lax.all_to_all(chunks, axes, 0, 0)  51.3 us
    all_to_all x2, waiting for transfers between devices, swap(): return lax.all_to_all(chunks, axes, 0, 0)  33.7 us
    pallas_call x12, Pallas kernels, call(): pl.pallas_call(body, out_shape=[o for o, _ in outs], in_specs=[s for _, s...  20.9 us
    all_to_all x2, starting transfers between devices, swap(): return lax.all_to_all(chunks, axes, 0, 0)  14.9 us
    ppermute x1, starting transfers between devices, on_device(): both_got = lax.ppermute(theirs, ROWS_AXES, CORE_PAIRS)  5.04 us
    ppermute x2, starting transfers between devices, halos(): from_chip = lax.ppermute(to_chip, ROWS_AXES, CHIP_PAIRS)  4.38 us
  transfers between devices with their start and end apart: 8, of which 4 were waited for; matrix products, arithmetic and copies ran while one was open for 1% of the time, Pallas kernels for 5%

profile of v4, /device:TPU:1, one launch (start us, length us, event | category | flops | bytes accessed | tf_op | source)
XLA Modules:
  0.0 144.5 jit_solution(15717127005720807519)
XLA Ops:
  0.6 1.1 constant_dynamic-slice_fusion
  1.7 3.1 %collective-permute-start.1 = (bf16[2,2,128,256]{3,2,1,0:T(8,128)(2,1)S(1)}, bf16[2,2,128,256]{3,2,1,0:T(8,128)(2,1)S(1)}, u32[]{:S(2)}, u32[]{:S(2)}) collective-permute-start(bf16[2,2,128,256]{3,2,1,0:T(8,128)(2,1)S(1)} %get-tuple-element.85), channel_id=1, source_target_pairs={{0,7},{1,2},{2,1},{3,4},{4,3},{5,6},{6,5},{7,0},{8,15},{9,10},{10,... | collective-permute-start | bytes 786440 | tf_op jit(solution)/shard_map/ppermute | solution.py:518
  4.8 2.0 %collective-permute-start = (bf16[2,2,128,256]{3,2,1,0:T(8,128)(2,1)S(1)}, bf16[2,2,128,256]{3,2,1,0:T(8,128)(2,1)S(1)}, u32[]{:S(2)}, u32[]{:S(2)}) collective-permute-start(bf16[2,2,128,256]{3,2,1,0:T(8,128)(2,1)S(1)} %get-tuple-element.86), channel_id=1, source_target_pairs={{0,1},{1,0},{2,3},{3,2},{4,5},{5,4},{6,7},{7,6},{8,9},{9,8},{10,11... | collective-permute-start | bytes 786440 | tf_op jit(solution)/shard_map/ppermute | solution.py:519
  6.8 0.7 select_maximum_fusion
  7.5 0.0 copy-start
  7.5 1.0 copy-done
  8.5 0.0 copy-start.2
  8.6 1.3 copy-done.2
  9.8 0.9 shard_map.126
  10.7 0.0 collective-permute-done.1.from_chip
  10.7 0.0 collective-permute-done.from_core
  10.7 2.1 %shard_map.127 = (f32[2,6,128,256]{3,2,1,0:T(8,128)S(1)}, bf16[16,56,256]{2,1,0:T(8,128)(2,1)S(1)}, bf16[768,1024]{1,0:T(8,128)(2,1)S(1)}) custom-call(bf16[2,4,128,256]{3,2,1,0:T(8,128)(2,1)S(1)} %get-tuple-element.46.x, bf16[2,2,128,256]{3,2,1,0:T(8,128)(2,1)S(1)} %collective-permute-done.from_core, ...), custom_call_target="tpu_custom_call" | custom-call | flops 1811939328 | bytes 5840896 | tf_op jit(solution)/shard_map/pallas_call | solution.py:34
  12.8 0.0 copy-start.1
  12.9 0.0 copy-start.4
  12.9 16.3 %all_to_all.30.got = bf16[16,56,256]{2,1,0:T(8,128)(2,1)S(1)} all-to-all(bf16[16,56,256]{2,1,0:T(8,128)(2,1)S(1)} %get-tuple-element.50), channel_id=1, replica_groups=mesh['x'=4,'y'=4,'z'=4,'core'=2] {'x','y'}, dimensions={0} | all-to-all | bytes 917504 | tf_op jit(solution)/shard_map/all_to_all | solution.py:524
  29.2 0.1 shard_map.128
  29.3 12.0 %all_to_all.31.carry = bf16[16,48,256]{2,1,0:T(8,128)(2,1)S(1)} all-to-all(bf16[16,48,256]{2,1,0:T(8,128)(2,1)S(1)} %get-tuple-element.51), channel_id=1, replica_groups=mesh['x'=4,'y'=4,'z'=4,'core'=2] {'x','y'}, dimensions={0} | all-to-all | bytes 786432 | tf_op jit(solution)/shard_map/all_to_all | solution.py:524
  41.4 0.0 copy-done.1
  41.4 0.0 copy-done.4
  41.4 3.7 %shard_map.129 = (bf16[2,4,128,256]{3,2,1,0:T(8,128)(2,1)}, bf16[2,4,128,256]{3,2,1,0:T(8,128)(2,1)}, bf16[2,4,128,256]{3,2,1,0:T(8,128)(2,1)S(1)}, bf16[2,6,128...) custom-call(f32[2,6,128,256]{3,2,1,0:T(8,128)S(1)} %get-tuple-elemen, ...), custom_call_target="tpu_custom_call" | custom-call | flops 3019898880 | bytes 9322496 | tf_op jit(solution)/shard_map/pallas_call | solution.py:34
  45.1 1.7 %shard_map.130 = (bf16[32,80,128]{2,1,0:T(8,128)(2,1)S(1)}, bf16[32,80,128]{2,1,0:T(8,128)(2,1)S(1)}) custom-call(bf16[2,6,128,256]{3,2,1,0:T(8,128)(2,1)S(1)} %get-tuple-element.54.state, bf16[2,4,128,256]{3,2,1,0:T(8,128)(2,1)S(1)} %get-tuple-element.55.gz, f32[2,8,128]{2,1,0:T(8,128)S(1)} %get-tuple-element.56.small), custom_call_target="tpu_custom_call" | custom-call | flops 1207959552 | bytes 2629632 | tf_op jit(solution)/shard_map/pallas_call | solution.py:34
  46.8 11.5 %all_to_all.32.got = bf16[16,48,256]{2,1,0:T(8,128)(2,1)S(1)} all-to-all(bf16[16,48,256]{2,1,0:T(8,128)(2,1)S(1)} %get-tuple-element.61), channel_id=1, replica_groups=mesh['x'=4,'y'=4,'z'=4,'core'=2] {'x','y'}, dimensions={0} | all-to-all | bytes 786432 | tf_op jit(solution)/shard_map/all_to_all | solution.py:524
  58.2 0.1 shard_map.131
  58.3 11.5 %all_to_all.33.incoming = bf16[16,48,256]{2,1,0:T(8,128)(2,1)S(1)} all-to-all(bf16[16,48,256]{2,1,0:T(8,128)(2,1)S(1)} %shard_map.131), channel_id=1, replica_groups=mesh['x'=4,'y'=4,'z'=4,'core'=2] {'x','y'}, dimensions={0} | all-to-all | bytes 786432 | tf_op jit(solution)/shard_map/all_to_all | solution.py:524
  69.8 2.6 %shard_map.132 = (bf16[32,80,128]{2,1,0:T(8,128)(2,1)S(1)}, bf16[2,32,80,128]{3,2,1,0:T(8,128)(2,1)S(1)}, bf16[2,6,128,256]{3,2,1,0:T(8,128)(2,1)S(1)}, bf16[2,2...) custom-call(f32[2,6,128,256]{3,2,1,0:T(8,128)S(1)} %get-tuple-element.60.local, ...), custom_call_target="tpu_custom_call" | custom-call | flops 1811939328 | bytes 10231808 | tf_op jit(solution)/shard_map/pallas_call | solution.py:34
  72.4 5.0 %collective-permute-start.2 = (bf16[2,32,80,128]{3,2,1,0:T(8,128)(2,1)S(1)}, bf16[2,32,80,128]{3,2,1,0:T(8,128)(2,1)S(1)}, u32[]{:S(2)}, u32[]{:S(2)}) collective-permute-start(bf16[2,32,80,128]{3,2,1,0:T(8,128)(2,1)S(1)} %get-tuple-element.68), channel_id=1, source_target_pairs={{0,1},{1,0},{2,3},{3,2},{4,5},{5,4},{6,7},{7,6},{8,9},{9,8},{10,11... | collective-permute-start | bytes 3932168 | tf_op jit(solution)/shard_map/ppermute | solution.py:609
  77.5 2.7 %collective-permute-done.2.both_got = bf16[2,32,80,128]{3,2,1,0:T(8,128)(2,1)S(1)} collective-permute-done((bf16[2,32,80,128]{3,2,1,0:T(8,128)(2,1)S(1)}, bf16[2,32,80,128]{3,2,1,0:T(8,128)(2,1)S(1)}, u32[]{:S(2)}, u32[]{:S(2)}) %collective-permute-start.2) | collective-permute-done | bytes 1310752 | tf_op jit(solution)/shard_map/ppermute | solution.py:609
  80.1 1.2 shard_map.133
  81.3 7.3 %all-to-all-start.4 = ((bf16[64,80,128]{2,1,0:T(8,128)(2,1)}), bf16[64,80,128]{2,1,0:T(8,128)(2,1)S(1)}, u32[]{:S(2)}, u32[]{:S(2)}) async-start(bf16[64,80,128]{2,1,0:T(8,128)(2,1)} %bitcast), calls=%async_computation.4 | async-start | bytes 2621440 | tf_op jit(solution)/shard_map/all_to_all | solution.py:524
  88.7 0.7 collective-permute-start.3
  89.4 1.3 collective-permute-start.4
  90.7 17.6 %all-to-all-done.4.got = bf16[64,80,128]{2,1,0:T(8,128)(2,1)S(1)} async-done(((bf16[64,80,128]{2,1,0:T(8,128)(2,1)}), bf16[64,80,128]{2,1,0:T(8,128)(2,1)S(1)}, u32[]{:S(2)}, u32[]{:S(2)}) %all-to-all-start.4) | async-done | bytes 1310752 | tf_op jit(solution)/shard_map/all_to_all | solution.py:524
  108.3 1.3 shard_map.134
  109.6 0.0 copy-start.3
  109.6 0.0 collective-permute-done.3.core_far
  109.6 0.0 collective-permute-done.4.chip_far
  109.6 7.6 %all-to-all-start.5 = ((bf16[64,80,128]{2,1,0:T(8,128)(2,1)}), bf16[64,80,128]{2,1,0:T(8,128)(2,1)S(1)}, u32[]{:S(2)}, u32[]{:S(2)}) async-start(bf16[64,80,128]{2,1,0:T(8,128)(2,1)} %shard_map.134), calls=%async_computation.5 | async-start | bytes 2621440 | tf_op jit(solution)/shard_map/all_to_all | solution.py:524
  117.2 0.0 copy-done.3
  117.2 3.7 %shard_map.135 = bf16[2,4,128,256]{3,2,1,0:T(8,128)(2,1)} custom-call(bf16[2,6,128,256]{3,2,1,0:T(8,128)(2,1)S(1)} %get-tuple-element.72.adj_far, bf16[2,2,128,256]{3,2,1,0:T(8,128)(2,1)} %collective-permute-done.3.core_far, bf16[2,2,128,256]{3,2,1,0:T(8,128)(2,1)} %collective-permute-done.4.chip_far, ...), custom_call_target="tpu_custom_call", output_to_operand_aliasing={{}: (4, {})} | custom-call | flops 1207959552 | bytes 3538944 | tf_op jit(solution)/shard_map/pallas_call | solution.py:34
  121.0 16.1 %all-to-all-done.5 = bf16[64,80,128]{2,1,0:T(8,128)(2,1)S(1)} async-done(((bf16[64,80,128]{2,1,0:T(8,128)(2,1)}), bf16[64,80,128]{2,1,0:T(8,128)(2,1)S(1)}, u32[]{:S(2)}, u32[]{:S(2)}) %all-to-all-start.5) | async-done | bytes 1310752 | tf_op jit(solution)/shard_map/all_to_all | solution.py:524
  137.0 2.6 %collective-permute-start.5 = (bf16[2,32,80,128]{3,2,1,0:T(8,128)(2,1)S(1)}, bf16[2,32,80,128]{3,2,1,0:T(8,128)(2,1)S(1)}, u32[]{:S(2)}, u32[]{:S(2)}) collective-permute-start(bf16[2,32,80,128]{3,2,1,0:T(8,128)(2,1)S(1)} %bitcast.5), channel_id=1, source_target_pairs={{0,1},{1,0},{2,3},{3,2},{4,5},{5,4},{6,7},{7,6},{8,9},{9,8},{10,11... | collective-permute-start | bytes 3932168 | tf_op jit(solution)/shard_map/ppermute | solution.py:648
  139.7 1.5 %shard_map.136 = (f32[3,3,256,256]{3,2,1,0:T(8,128)}, f32[3,3,256,256]{3,2,1,0:T(8,128)}) custom-call(bf16[2,32,80,128]{3,2,1,0:T(8,128)(2,1)S(1)} %bitcast.6), custom_call_target="tpu_custom_call" | custom-call | bytes 6029312 | tf_op jit(solution)/shard_map/pallas_call | solution.py:34
  141.1 1.2 collective-permute-done.5.got
  142.3 2.0 %shard_map.137 = (f32[3,3,256,256]{3,2,1,0:T(8,128)}, f32[3,3,256,256]{3,2,1,0:T(8,128)}, f32[2,128]{1,0:T(2,128)}, f32[2,128]{1,0:T(2,128)}, f32[1,2]{1,0:T(1,128)}) custom-call(bf16[2,32,80,128]{3,2,1,0:T(8,128)(2,1)S(1)} %bitcast.7, bf16[2,32,80,128]{3,2,1,0:T(8,128)(2,1)S(1)} %collective-permute-done.5.got, ...), custom_call_target="tpu_custom_call", output_to_operand_aliasing={{0}: (2, {}), {1}: (3, {})} | custom-call | bytes 12060680 | tf_op jit(solution)/shard_map/pallas_call | solution.py:34
  (1 shorter events, 0.0 us)
Async XLA Ops:
  1.7 9.0 %collective-permute-start.1 = (bf16[2,2,128,256]{3,2,1,0:T(8,128)(2,1)S(1)}, bf16[2,2,128,256]{3,2,1,0:T(8,128)(2,1)S(1)}, u32[]{:S(2)}, u32[]{:S(2)}) collective-permute-start(bf16[2,2,128,256]{3,2,1,0:T(8,128)(2,1)S(1)} %get-tuple-element.85), channel_id=1, source_target_pairs={{0,7},{1,2},{2,1},{3,4},{4,3},{5,6},{6,5},{7,0},{8,15},{9,10},{10,... | collective-permute-start | bytes 786440 | tf_op jit(solution)/shard_map/ppermute | solution.py:518
  4.8 5.9 %collective-permute-start = (bf16[2,2,128,256]{3,2,1,0:T(8,128)(2,1)S(1)}, bf16[2,2,128,256]{3,2,1,0:T(8,128)(2,1)S(1)}, u32[]{:S(2)}, u32[]{:S(2)}) collective-permute-start(bf16[2,2,128,256]{3,2,1,0:T(8,128)(2,1)S(1)} %get-tuple-element.86), channel_id=1, source_target_pairs={{0,1},{1,0},{2,3},{3,2},{4,5},{5,4},{6,7},{7,6},{8,9},{9,8},{10,11... | collective-permute-start | bytes 786440 | tf_op jit(solution)/shard_map/ppermute | solution.py:519
  7.5 1.0 copy-start
  8.5 1.3 copy-start.2
  12.8 28.5 %copy-start.1 = (bf16[3,3,256,256]{3,2,1,0:T(8,128)(2,1)S(1)}, bf16[3,3,256,256]{3,2,1,0:T(8,128)(2,1)}, u32[]{:S(2)}) copy-start(bf16[3,3,256,256]{3,2,1,0:T(8,128)(2,1)} %weight.1) | copy-start | bytes 3538948
  12.9 28.5 %copy-start.4 = (bf16[2,4,128,256]{3,2,1,0:T(8,128)(2,1)S(1)}, bf16[2,4,128,256]{3,2,1,0:T(8,128)(2,1)}, u32[]{:S(2)}) copy-start(bf16[2,4,128,256]{3,2,1,0:T(8,128)(2,1)} %cot.1) | copy-start | bytes 1572868
  72.4 7.7 %collective-permute-start.2 = (bf16[2,32,80,128]{3,2,1,0:T(8,128)(2,1)S(1)}, bf16[2,32,80,128]{3,2,1,0:T(8,128)(2,1)S(1)}, u32[]{:S(2)}, u32[]{:S(2)}) collective-permute-start(bf16[2,32,80,128]{3,2,1,0:T(8,128)(2,1)S(1)} %get-tuple-element.68), channel_id=1, source_target_pairs={{0,1},{1,0},{2,3},{3,2},{4,5},{5,4},{6,7},{7,6},{8,9},{9,8},{10,11... | collective-permute-start | bytes 3932168 | tf_op jit(solution)/shard_map/ppermute | solution.py:609
  81.3 27.0 %all-to-all-start.4 = ((bf16[64,80,128]{2,1,0:T(8,128)(2,1)}), bf16[64,80,128]{2,1,0:T(8,128)(2,1)S(1)}, u32[]{:S(2)}, u32[]{:S(2)}) async-start(bf16[64,80,128]{2,1,0:T(8,128)(2,1)} %bitcast), calls=%async_computation.4 | async-start | bytes 2621440 | tf_op jit(solution)/shard_map/all_to_all | solution.py:524
  88.7 21.0 %collective-permute-start.3 = (bf16[2,2,128,256]{3,2,1,0:T(8,128)(2,1)}, bf16[2,2,128,256]{3,2,1,0:T(8,128)(2,1)}, u32[]{:S(2)}, u32[]{:S(2)}) collective-permute-start(bf16[2,2,128,256]{3,2,1,0:T(8,128)(2,1)} %get-tuple-element.69), channel_id=1, source_target_pairs={{0,1},{1,0},{2,3},{3,2},{4,5},{5,4},{6,7},{7,6},{8,9},{9,8},{10,11... | collective-permute-start | bytes 786440 | tf_op jit(solution)/shard_map/ppermute | solution.py:519
  89.4 20.2 %collective-permute-start.4 = (bf16[2,2,128,256]{3,2,1,0:T(8,128)(2,1)S(1)}, bf16[2,2,128,256]{3,2,1,0:T(8,128)(2,1)}, u32[]{:S(2)}, u32[]{:S(2)}) collective-permute-start(bf16[2,2,128,256]{3,2,1,0:T(8,128)(2,1)S(1)} %get-tuple-element.70), channel_id=1, source_target_pairs={{0,7},{1,2},{2,1},{3,4},{4,3},{5,6},{6,5},{7,0},{8,15},{9,10},{10,... | collective-permute-start | bytes 786440 | tf_op jit(solution)/shard_map/ppermute | solution.py:518
  109.6 7.6 %copy-start.3 = (bf16[3,3,256,256]{3,2,1,0:T(8,128)(2,1)S(1)}, bf16[3,3,256,256]{3,2,1,0:T(8,128)(2,1)}, u32[]{:S(2)}) copy-start(bf16[3,3,256,256]{3,2,1,0:T(8,128)(2,1)} %weight_far.1) | copy-start | bytes 3538948
  109.6 27.4 %all-to-all-start.5 = ((bf16[64,80,128]{2,1,0:T(8,128)(2,1)}), bf16[64,80,128]{2,1,0:T(8,128)(2,1)S(1)}, u32[]{:S(2)}, u32[]{:S(2)}) async-start(bf16[64,80,128]{2,1,0:T(8,128)(2,1)} %shard_map.134), calls=%async_computation.5 | async-start | bytes 2621440 | tf_op jit(solution)/shard_map/all_to_all | solution.py:524
  137.0 5.3 %collective-permute-start.5 = (bf16[2,32,80,128]{3,2,1,0:T(8,128)(2,1)S(1)}, bf16[2,32,80,128]{3,2,1,0:T(8,128)(2,1)S(1)}, u32[]{:S(2)}, u32[]{:S(2)}) collective-permute-start(bf16[2,32,80,128]{3,2,1,0:T(8,128)(2,1)S(1)} %bitcast.5), channel_id=1, source_target_pairs={{0,1},{1,0},{2,3},{3,2},{4,5},{5,4},{6,7},{7,6},{8,9},{9,8},{10,11... | collective-permute-start | bytes 3932168 | tf_op jit(solution)/shard_map/ppermute | solution.py:648

commit v5 on v4

--- a/solution.py
+++ b/solution.py
@@ -243,14 +243,15 @@
 GELU_A = math.sqrt(2 / math.pi)
 
 
-def spread(vector, extra):
+def spread(*vectors):
     row = lax.broadcasted_iota(jnp.int32, (8, 128), 0) % 4
-    low = jnp.broadcast_to(vector[:, 0:128], (8, 128))
-    high = jnp.broadcast_to(vector[:, 128:256], (8, 128))
-    low, high = (jnp.where(row == 0, v, 0.0) for v in (low, high))
-    if extra is not None:
-        low = jnp.where(row == 1, extra, low)
-    return low, high
+    halves = []
+    for half in HALVES:
+        out = jnp.zeros((8, 128), F32)
+        for k, vector in enumerate(vectors):
+            out = jnp.where(row == k, jnp.broadcast_to(vector[:, half], (8, 128)), out)
+        halves.append(out)
+    return halves
 
 
 def split_pairs(both):
@@ -265,7 +266,7 @@
 
 def middle_body(
     local, carry, x, cot, weight, table,
-    out_far, direct_far, gz, state, state_f, local_adj, send, small, out, direct, sems,
+    out_far, direct_far, gz, state, state_f, local_adj, send, skip, out, direct, sems,
 ):
     spot = Spot()
     d0, d1 = table[0:1, :], table[1:2, :]
@@ -303,50 +304,51 @@
                 put_chunks(send, h, half, d0[:, half] * v)
             local_adj[t, h, :, half] = v
     total = jnp.concatenate([jnp.sum(v, axis=0, keepdims=True) for v in totals], axis=1)
-    small[0], small[1] = spread(total, None)
+    skip[...] = total
     for copy in copies:
         copy.wait()
 
 
-def pack_grad(core, g, a, scale, mine, theirs):
+def pack_grad(g, a, scale, out):
     for b in range(3):
         tap = (3 * a + b) * 8
-        low = g[b * CHANS : (b + 1) * CHANS, 0:128] * scale
-        high = g[b * CHANS : (b + 1) * CHANS, 128:256] * scale
-        mine[:, tap : tap + 8, :] = (
-            jnp.where(core == 0, low, high).astype(BF).reshape(GROUPS, 8, 128)
-        )
-        theirs[:, tap : tap + 8, :] = (
-            jnp.where(core == 0, high, low).astype(BF).reshape(GROUPS, 8, 128)
-        )
-
-
-def pack_small(core, low, high, scale, mine, theirs):
-    blank = jnp.zeros((GROUPS, 8, 128), BF)
-    for ref, half in (
-        (mine, jnp.where(core == 0, low, high)),
-        (theirs, jnp.where(core == 0, high, low)),
-    ):
-        ref[:, TAPS:PACK, :] = blank
-        ref[0, TAPS:PACK, :] = split_pairs(half * scale).astype(BF)
-
-
-def out_grad_body(scale, state, gz, small, mine, theirs, flat):
-    spot = Spot()
+        for lg, half in enumerate(HALVES):
+            part = g[b * CHANS : (b + 1) * CHANS, half] * scale
+            out[:, lg, tap : tap + 8, :] = part.astype(BF).reshape(GROUPS, 8, 128)
+
+
+def out_grad_body(scale, state, gz, out, flat):
     transpose_rows(state, flat, WIDE, lambda t, h: t * WIDE + h)
     rhs = gz[...].reshape(FRAMES * HEIGHT * WIDTH, CHANS)
     for a in range(3):
         lhs = jnp.concatenate(
             [flat[:, pl.ds((t * WIDE + a) * WIDTH, HEIGHT * WIDTH)] for t in range(FRAMES)], axis=1
         )
-        g = jnp.dot(lhs, rhs, preferred_element_type=F32)
-        pack_grad(spot.core, g, a, scale, mine, theirs)
-    pack_small(spot.core, small[0], small[1], scale, mine, theirs)
-
-
-def in_grad_body(
-    scale, step_scale, local, incoming, state_f, carry, table, flat_mid, flat_edge, out_theirs,
-    mine, theirs, adj_far, to_core, to_chip, adj, sems,
+        pack_grad(jnp.dot(lhs, rhs, preferred_element_type=F32), a, scale, out)
+    out[:, :, TAPS:PACK, :] = jnp.zeros((GROUPS, 2, 8, 128), BF)
+
+
+def in_grad(scale, adj, small, flat_mid, flat_edge, out):
+    rhs = adj[...].reshape(FRAMES * WIDE * WIDTH, CHANS)
+    for a in range(3):
+        pieces = []
+        for t in range(FRAMES):
+            at = t * 4 * WIDTH
+            if a < 2:
+                pieces.append(flat_edge[:, at + a * WIDTH : at + 2 * WIDTH])
+            pieces.append(flat_mid[:, at : at + 4 * WIDTH])
+            if a > 0:
+                pieces.append(flat_edge[:, at + 2 * WIDTH : at + (2 + a) * WIDTH])
+        g = jnp.dot(jnp.concatenate(pieces, axis=1), rhs, preferred_element_type=F32)
+        pack_grad(g, a, scale, out)
+    out[:, :, TAPS:PACK, :] = jnp.zeros((GROUPS, 2, 8, 128), BF)
+    for lg in range(2):
+        out[0, lg, TAPS:PACK, :] = split_pairs(small[lg]).astype(BF)
+
+
+def odd_grad_body(
+    scale, step_scale, local, incoming, state_f, carry, table, skip, flat_mid, flat_edge, out_part,
+    payload, small, adj, adj_far, to_core, to_chip, sems,
 ):
     spot = Spot()
     d0, d1 = table[0:1, :], table[1:2, :]
@@ -362,6 +364,7 @@
         for t, (a, earlier) in enumerate(pairs):
             sums[t][k] = sums[t][k] + jnp.sum((a * earlier).reshape(WIDTH // 8, 8, 128), axis=0)
     up, down = adj.at[:, 0:2], adj.at[:, WIDE - 2 :]
+    (whole,) = fetch(sems.at[2:3], (adj, adj_far))
 
     @pl.when(spot.core == 0)
     def _():
@@ -371,19 +374,6 @@
     def _():
         fetch(sems, (down, to_chip), (up, to_core))
 
-    others = fetch(sems.at[2:4], (adj, adj_far), (out_theirs, theirs.at[0]))
-    rhs = adj[...].reshape(FRAMES * WIDE * WIDTH, CHANS)
-    for a in range(3):
-        pieces = []
-        for t in range(FRAMES):
-            at = t * 4 * WIDTH
-            if a < 2:
-                pieces.append(flat_edge[:, at + a * WIDTH : at + 2 * WIDTH])
-            pieces.append(flat_mid[:, at : at + 4 * WIDTH])
-            if a > 0:
-                pieces.append(flat_edge[:, at + 2 * WIDTH : at + (2 + a) * WIDTH])
-        g = jnp.dot(jnp.concatenate(pieces, axis=1), rhs, preferred_element_type=F32)
-        pack_grad(spot.core, g, a, scale, mine, theirs.at[1])
     k0, k1 = (
         jnp.concatenate([jnp.sum(v, axis=0, keepdims=True) for v in pair], axis=1) * d
         for pair, d in zip(sums, (d0, d1))
@@ -391,12 +381,34 @@
     rate_part = (k0 * table[2:3, :] + k1 * table[3:4, :]) * (-scale)
     s0 = jnp.sum(k0 * table[4:5, :], axis=1, keepdims=True) * (-step_scale)
     s1 = jnp.sum(k1 * table[4:5, :], axis=1, keepdims=True) * (-step_scale)
-    lane = lax.broadcasted_iota(jnp.int32, (8, 128), 1)
+    lane = lax.broadcasted_iota(jnp.int32, (1, CHANS), 1)
     at = spot.place * FRAMES
-    low, high = spread(rate_part, jnp.where(lane == at, s0, jnp.where(lane == at + 1, s1, 0.0)))
-    pack_small(spot.core, low, high, 1.0, mine, theirs.at[1])
+    steps = jnp.where(lane == at, s0, jnp.where(lane == at + 1, s1, 0.0))
+    small[0], small[1] = spread(rate_part, steps, skip[...] * scale)
+
+    @pl.when(spot.core == 0)
+    def _():
+        (copy,) = fetch(sems.at[3:4], (out_part, payload))
+        copy.wait()
+
+    @pl.when(spot.core == 1)
+    def _():
+        in_grad(scale, adj, small, flat_mid, flat_edge, payload)
+
     fetch_wait(sems, (up, to_chip), (down, to_core))
-    for copy in others:
+    whole.wait()
+
+
+def even_grad_body(scale, adj, small, flat_mid, flat_edge, out_part, mine, sems):
+    spot = Spot()
+
+    @pl.when(spot.core == 0)
+    def _():
+        in_grad(scale, adj, small, flat_mid, flat_edge, mine)
+
+    @pl.when(spot.core == 1)
+    def _():
+        (copy,) = fetch(sems, (out_part, mine))
         copy.wait()
 
 
@@ -428,20 +440,17 @@
     copy.wait()
 
 
-def pair_sum_body(out_own, in_own, both_got, send_far, send, sems):
+def pair_sum_body(mine, got, send_far, send, sems):
     copies = []
-    for g, own in enumerate((out_own, in_own)):
-        got = both_got.at[g]
-        for k in range(GROUPS):
-            send[g, k] = (own[k].astype(F32) + got[k].astype(F32)).astype(BF)
-            if k == 0:
-                pairs = own[0, TAPS:PACK, :].astype(F32) + got[0, TAPS:PACK, :].astype(F32)
-                send[g, 0, TAPS:PACK, :] = split_pairs(joined(pairs)).astype(BF)
-            if k % 8 == 7:
-                part = slice(k - 7, k + 1)
-                copies += fetch(
-                    sems.at[g, k // 8 : k // 8 + 1], (send.at[g, part], send_far.at[g, part])
-                )
+    for k in range(GROUPS):
+        send[k] = (mine[k].astype(F32) + got[k].astype(F32)).astype(BF)
+        if k == 0:
+            for lg in range(2):
+                pairs = mine[0, lg, TAPS:PACK, :].astype(F32) + got[0, lg, TAPS:PACK, :].astype(F32)
+                send[0, lg, TAPS:PACK, :] = split_pairs(joined(pairs)).astype(BF)
+        if k % 8 == 7:
+            part = slice(k - 7, k + 1)
+            copies += fetch(sems.at[k // 8 : k // 8 + 1], (send.at[part], send_far.at[part]))
     for copy in copies:
         copy.wait()
 
@@ -458,54 +467,55 @@
         copy.wait()
 
 
-def write_half(src, lane_half, grads, stage, sems):
-    lanes = pl.ds(pl.multiple_of(lane_half * 128, 128), 128)
+def write_grad(src, grad, stage, sems):
     copies = []
-    for g, grad in enumerate(grads):
-        for a in range(3):
-            for b in range(3):
-                tap = (3 * a + b) * 8
-                part = src[g, :, tap : tap + 8, :].astype(F32)
-                stage[g, a, b] = part.reshape(CHANS, 128)
-            copy = pltpu.make_async_copy(
-                stage.at[g, a], grad.at[a, :, :, lanes], sems.at[3 * g + a]
-            )
-            copy.start()
-            copies.append(copy)
-    return copies
+    for a in range(3):
+        for b in range(3):
+            tap = (3 * a + b) * 8
+            for lg, half in enumerate(HALVES):
+                part = src[:, lg, tap : tap + 8, :].astype(F32)
+                stage[a, b, :, half] = part.reshape(CHANS, 128)
+        copies += fetch(sems.at[a : a + 1], (stage.at[a], grad.at[a]))
+    for copy in copies:
+        copy.wait()
 
 
 def unpack_own_body(own, grad_out, grad_in, stage, sems):
-    for copy in write_half(own, Spot().core, (grad_out, grad_in), stage, sems):
-        copy.wait()
+    core = Spot().core
+
+    @pl.when(core == 0)
+    def _():
+        write_grad(own, grad_in, stage, sems)
+
+    @pl.when(core == 1)
+    def _():
+        write_grad(own, grad_out, stage, sems)
 
 
 def unpack_other_body(
-    own, got, out_half, in_half, grad_out, grad_in, skip, rate, step, stage, sems
+    own, got, out_half, in_half, grad_out, grad_in, rate, skip, step, stage, sems
 ):
     del out_half, in_half
     spot = Spot()
-    copies = write_half(got, 1 - spot.core, (grad_out, grad_in), stage, sems)
-
-    def smalls(low, high):
-        for g, vector in enumerate((skip, rate)):
-            for lg, src in enumerate((low, high)):
-                extras = joined(src[g, 0, TAPS:PACK, :].astype(F32))
-                vector[lg : lg + 1, :] = extras[0:1]
-                if g == 1 and lg == 0:
-                    turned = pltpu.roll(extras, (128 - spot.place * FRAMES) % 128, 1)
-                    step[...] = turned[1:2, 0:FRAMES]
+
+    def smalls(src):
+        for lg in range(2):
+            extras = joined(src[0, lg, TAPS:PACK, :].astype(F32))
+            rate[lg : lg + 1, :] = extras[0:1]
+            skip[lg : lg + 1, :] = extras[2:3]
+            if lg == 0:
+                turned = pltpu.roll(extras, (128 - spot.place * FRAMES) % 128, 1)
+                step[...] = turned[1:2, 0:FRAMES]
 
     @pl.when(spot.core == 0)
     def _():
-        smalls(own, got)
+        smalls(own)
+        write_grad(got, grad_out, stage, sems)
 
     @pl.when(spot.core == 1)
     def _():
-        smalls(got, own)
-
-    for copy in copies:
-        copy.wait()
+        smalls(got)
+        write_grad(got, grad_in, stage, sems)
 
 
 ROWS_AXES = ("z", "core")
@@ -541,7 +551,7 @@
     edge = (FRAMES, 2, WIDTH, CHANS)
     kernel = (3, 3, CHANS, CHANS)
     chunk = sds((BLOCKS, PLACES, CHANS), BF)
-    packed = sds((GROUPS, PACK, 128), BF)
+    packed = sds((GROUPS, 2, PACK, 128), BF)
     flat = sds((3 * CHANS, FRAMES * 4 * WIDTH), BF)
     params = jnp.concatenate([rates, skip_gain, jnp.pad(step_sizes, (0, CHANS - FRAMES))])
     params = params.reshape(3, CHANS)
@@ -566,7 +576,7 @@
     got = swap(send, TM_AXES)
     send, block_decays = call(forward_scan_body, [chunk, sds((BLOCKS, CHANS), F32)], [got, table])
     carry = swap(send, TM_AXES)
-    outputs, direct, gz, state, state_f, local_adj, send, small = call(
+    outputs, direct, gz, state, state_f, local_adj, send, skip = call(
         middle_body,
         [
             far(sds(field, BF)),
@@ -576,45 +586,47 @@
             sds(wide[1:], F32),
             sds(wide, F32),
             chunk,
-            sds((2, 8, 128), F32),
+            sds((1, CHANS), F32),
         ],
         [local, carry, x, cotangent, out_weight, table],
         (HEIGHT + WIDE) * ROW_FLOPS,
         [vmem(field), vmem(field), sems(FRAMES, 2)],
     )
-    out_mine, out_theirs = call(
+    (out_part,) = call(
         functools.partial(out_grad_body, scale),
-        [packed, packed],
-        [state, gz, small],
+        [packed],
+        [state, gz],
         HEIGHT * ROW_FLOPS,
         [vmem((3 * CHANS, FRAMES * WIDE * WIDTH))],
     )
-    send, out_mine, out_theirs = lax.optimization_barrier((send, out_mine, out_theirs))
+    send, out_part = lax.optimization_barrier((send, out_part))
     got = swap(send, TM_AXES)
     (send,) = call(backward_scan_body, [chunk], [got, block_decays])
     incoming = swap(send, TM_AXES)
-    in_mine, theirs, adj_far, to_core, to_chip = call(
-        functools.partial(in_grad_body, scale, step_scale),
+    payload, small, adj, adj_far, to_core, to_chip = call(
+        functools.partial(odd_grad_body, scale, step_scale),
         [
             packed,
-            sds((2, GROUPS, PACK, 128), BF),
+            sds((2, 8, 128), F32),
+            sds(wide, BF),
             far(sds(wide, BF)),
             far(sds(edge, BF)),
             far(sds(edge, BF)),
         ],
-        [local_adj, incoming, state_f, carry, table, flat_mid, flat_edge, out_theirs],
+        [local_adj, incoming, state_f, carry, table, skip, flat_mid, flat_edge, out_part],
         WIDE * ROW_FLOPS,
-        [vmem(wide), sems(4)],
-    )
-    both_got = lax.ppermute(theirs, ROWS_AXES, CORE_PAIRS)
+        [sems(4)],
+    )
+    got = lax.ppermute(payload, ROWS_AXES, CORE_PAIRS)
+    (mine,) = call(
+        functools.partial(even_grad_body, scale),
+        [packed],
+        [adj, small, flat_mid, flat_edge, out_part],
+        WIDE * ROW_FLOPS,
+        [sems(1)],
+    )
     from_core, from_chip = halos(to_core, to_chip)
-    (send,) = call(
-        pair_sum_body,
-        [far(sds((2, GROUPS, PACK, 128), BF))],
-        [out_mine, in_mine, both_got],
-        0,
-        [vmem((2, GROUPS, PACK, 128)), sems(2, 4)],
-    )
+    (send,) = call(pair_sum_body, [far(packed)], [mine, got], 0, [vmem(packed.shape), sems(4)])
     got = swap(send.reshape(CHIPS, PACK, 128), ("x", "y", "z"))
     (send,) = call(
         all_sum_body,
@@ -644,20 +656,20 @@
         {4: 0},
     )
     own, grad_inputs = lax.optimization_barrier((own, grad_inputs))
-    own = own.reshape(2, GROUPS, PACK, 128)
+    own = own.reshape(packed.shape)
     other = lax.ppermute(own, ROWS_AXES, CORE_PAIRS)
     weights = sds(kernel, F32)
     half = sds((2, 128), F32)
-    stage = vmem((2, 3, 3, CHANS, 128), F32)
+    stage = vmem(kernel, F32)
     grad_out_weight, grad_in_weight = call(
-        unpack_own_body, [far(weights), far(weights)], [own], 0, [stage, sems(6)]
-    )
-    grad_out_weight, grad_in_weight, grad_skip, grad_rates, grad_steps = call(
+        unpack_own_body, [far(weights), far(weights)], [own], 0, [stage, sems(3)]
+    )
+    grad_out_weight, grad_in_weight, grad_rates, grad_skip, grad_steps = call(
         unpack_other_body,
         [far(weights), far(weights), half, half, sds((1, FRAMES), F32)],
         [own, other, far(grad_out_weight), far(grad_in_weight)],
         0,
-        [stage, sems(6)],
+        [stage, sems(3)],
         {2: 0, 3: 1},
     )
     return (

time: 145 us -> 144 us (level)
    pallas_call x12 -> x13, Pallas kernels: 20.9 us -> 21 us  [call(): pl.pallas_call(body, out_shape=[o for o, _ in outs], in_specs=[s for _, s...]
where the time goes in v5:
time: 144 us; the launch traced here: 143 us
  blocking collectives  51.3 us (36%)
  waiting for transfers between devices  37.4 us (26%)
  starting transfers between devices  28.3 us (20%)
  Pallas kernels  21 us (15%)
  local copies, waits for them, and re-layouts  3.41 us (2%)
    all_to_all x4, blocking collectives, swap(): return lax.all_to_all(chunks, axes, 0, 0)  51.3 us
    all_to_all x2, waiting for transfers between devices, swap(): return lax.all_to_all(chunks, axes, 0, 0)  33.7 us
    pallas_call x13, Pallas kernels, call(): pl.pallas_call(body, out_shape=[o for o, _ in outs], in_specs=[s for _, s...  21 us
    all_to_all x2, starting transfers between devices, swap(): return lax.all_to_all(chunks, axes, 0, 0)  14.9 us
    ppermute x2, starting transfers between devices, halos(): from_chip = lax.ppermute(to_chip, ROWS_AXES, CHIP_PAIRS)  4.38 us
    ppermute x1, starting transfers between devices, on_device(): got = lax.ppermute(payload, ROWS_AXES, CORE_PAIRS)  3.64 us
  transfers between devices with their start and end apart: 8, of which 4 were waited for; matrix products, arithmetic and copies ran while one was open for 1% of the time, Pallas kernels for 5%

profile of v5, /device:TPU:1, one launch (start us, length us, event | category | flops | bytes accessed | tf_op | source)
XLA Modules:
  0.0 143.1 jit_solution(2708712809887484622)
XLA Ops:
  0.6 1.1 constant_dynamic-slice_fusion
  1.7 3.1 %collective-permute-start.1 = (bf16[2,2,128,256]{3,2,1,0:T(8,128)(2,1)S(1)}, bf16[2,2,128,256]{3,2,1,0:T(8,128)(2,1)S(1)}, u32[]{:S(2)}, u32[]{:S(2)}) collective-permute-start(bf16[2,2,128,256]{3,2,1,0:T(8,128)(2,1)S(1)} %get-tuple-element.81), channel_id=1, source_target_pairs={{0,7},{1,2},{2,1},{3,4},{4,3},{5,6},{6,5},{7,0},{8,15},{9,10},{10,... | collective-permute-start | bytes 786440 | tf_op jit(solution)/shard_map/ppermute | solution.py:528
  4.8 2.0 %collective-permute-start = (bf16[2,2,128,256]{3,2,1,0:T(8,128)(2,1)S(1)}, bf16[2,2,128,256]{3,2,1,0:T(8,128)(2,1)S(1)}, u32[]{:S(2)}, u32[]{:S(2)}) collective-permute-start(bf16[2,2,128,256]{3,2,1,0:T(8,128)(2,1)S(1)} %get-tuple-element.82), channel_id=1, source_target_pairs={{0,1},{1,0},{2,3},{3,2},{4,5},{5,4},{6,7},{7,6},{8,9},{9,8},{10,11... | collective-permute-start | bytes 786440 | tf_op jit(solution)/shard_map/ppermute | solution.py:529
  6.8 0.7 select_maximum_fusion
  7.5 0.0 copy-start
  7.5 1.0 copy-done
  8.5 0.0 copy-start.2
  8.6 1.3 copy-done.2
  9.8 0.9 shard_map.126
  10.7 0.0 collective-permute-done.1.from_chip
  10.7 0.0 collective-permute-done.from_core
  10.7 2.1 %shard_map.127 = (f32[2,6,128,256]{3,2,1,0:T(8,128)S(1)}, bf16[16,56,256]{2,1,0:T(8,128)(2,1)S(1)}, bf16[768,1024]{1,0:T(8,128)(2,1)S(1)}) custom-call(bf16[2,4,128,256]{3,2,1,0:T(8,128)(2,1)S(1)} %get-tuple-element.44.x, bf16[2,2,128,256]{3,2,1,0:T(8,128)(2,1)S(1)} %collective-permute-done.from_core, ...), custom_call_target="tpu_custom_call" | custom-call | flops 1811939328 | bytes 5840896 | tf_op jit(solution)/shard_map/pallas_call | solution.py:34
  12.9 0.0 copy-start.1
  12.9 0.0 copy-start.4
  12.9 16.3 %all_to_all.30.got = bf16[16,56,256]{2,1,0:T(8,128)(2,1)S(1)} all-to-all(bf16[16,56,256]{2,1,0:T(8,128)(2,1)S(1)} %get-tuple-element.48), channel_id=1, replica_groups=mesh['x'=4,'y'=4,'z'=4,'core'=2] {'x','y'}, dimensions={0} | all-to-all | bytes 917504 | tf_op jit(solution)/shard_map/all_to_all | solution.py:534
  29.2 0.1 shard_map.128
  29.4 12.0 %all_to_all.31.carry = bf16[16,48,256]{2,1,0:T(8,128)(2,1)S(1)} all-to-all(bf16[16,48,256]{2,1,0:T(8,128)(2,1)S(1)} %get-tuple-element.49), channel_id=1, replica_groups=mesh['x'=4,'y'=4,'z'=4,'core'=2] {'x','y'}, dimensions={0} | all-to-all | bytes 786432 | tf_op jit(solution)/shard_map/all_to_all | solution.py:534
  41.4 0.0 copy-done.1
  41.4 0.0 copy-done.4
  41.4 3.7 %shard_map.129 = (bf16[2,4,128,256]{3,2,1,0:T(8,128)(2,1)}, bf16[2,4,128,256]{3,2,1,0:T(8,128)(2,1)}, bf16[2,4,128,256]{3,2,1,0:T(8,128)(2,1)S(1)}, bf16[2,6,128...) custom-call(f32[2,6,128,256]{3,2,1,0:T(8,128)S(1)} %get-tuple-elemen, ...), custom_call_target="tpu_custom_call" | custom-call | flops 3019898880 | bytes 9315328 | tf_op jit(solution)/shard_map/pallas_call | solution.py:34
  45.1 1.7 %shard_map.130.out_part = bf16[32,2,80,128]{3,2,1,0:T(8,128)(2,1)S(1)} custom-call(bf16[2,6,128,256]{3,2,1,0:T(8,128)(2,1)S(1)} %get-tuple-element.53.state, bf16[2,4,128,256]{3,2,1,0:T(8,128)(2,1)S(1)} %get-tuple-element.54.gz), custom_call_target="tpu_custom_call" | custom-call | flops 1207959552 | bytes 2621440 | tf_op jit(solution)/shard_map/pallas_call | solution.py:34
  46.8 11.5 %all_to_all.32.got = bf16[16,48,256]{2,1,0:T(8,128)(2,1)S(1)} all-to-all(bf16[16,48,256]{2,1,0:T(8,128)(2,1)S(1)} %get-tuple-element.55), channel_id=1, replica_groups=mesh['x'=4,'y'=4,'z'=4,'core'=2] {'x','y'}, dimensions={0} | all-to-all | bytes 786432 | tf_op jit(solution)/shard_map/all_to_all | solution.py:534
  58.3 0.1 shard_map.131
  58.4 11.5 %all_to_all.33.incoming = bf16[16,48,256]{2,1,0:T(8,128)(2,1)S(1)} all-to-all(bf16[16,48,256]{2,1,0:T(8,128)(2,1)S(1)} %shard_map.131), channel_id=1, replica_groups=mesh['x'=4,'y'=4,'z'=4,'core'=2] {'x','y'}, dimensions={0} | all-to-all | bytes 786432 | tf_op jit(solution)/shard_map/all_to_all | solution.py:534
  69.9 2.6 %shard_map.132 = (bf16[32,2,80,128]{3,2,1,0:T(8,128)(2,1)S(1)}, f32[2,8,128]{2,1,0:T(8,128)S(1)}, bf16[2,6,128,256]{3,2,1,0:T(8,128)(2,1)S(1)}, bf16[2,6,128,256...) custom-call(f32[2,6,128,256]{3,2,1,0:T(8,128)S(1)} %get-tuple-element.51.local, ...), custom_call_target="tpu_custom_call" | custom-call | flops 1811939328 | bytes 11027456 | tf_op jit(solution)/shard_map/pallas_call | solution.py:34
  72.4 3.6 %collective-permute-start.2 = (bf16[32,2,80,128]{3,2,1,0:T(8,128)(2,1)S(1)}, bf16[32,2,80,128]{3,2,1,0:T(8,128)(2,1)S(1)}, u32[]{:S(2)}, u32[]{:S(2)}) collective-permute-start(bf16[32,2,80,128]{3,2,1,0:T(8,128)(2,1)S(1)} %get-tuple-element.64), channel_id=1, source_target_pairs={{0,1},{1,0},{2,3},{3,2},{4,5},{5,4},{6,7},{7,6},{8,9},{9,8},{10,11... | collective-permute-start | bytes 3932168 | tf_op jit(solution)/shard_map/ppermute | solution.py:620
  76.1 0.1 shard_map.133.mine
  76.2 2.6 %collective-permute-done.2.got = bf16[32,2,80,128]{3,2,1,0:T(8,128)(2,1)S(1)} collective-permute-done((bf16[32,2,80,128]{3,2,1,0:T(8,128)(2,1)S(1)}, bf16[32,2,80,128]{3,2,1,0:T(8,128)(2,1)S(1)}, u32[]{:S(2)}, u32[]{:S(2)}) %collective-permute-start.2) | collective-permute-done | bytes 1310752 | tf_op jit(solution)/shard_map/ppermute | solution.py:620
  78.7 1.2 shard_map.134
  79.9 7.3 %all-to-all-start.4 = ((bf16[64,80,128]{2,1,0:T(8,128)(2,1)}), bf16[64,80,128]{2,1,0:T(8,128)(2,1)S(1)}, u32[]{:S(2)}, u32[]{:S(2)}) async-start(bf16[64,80,128]{2,1,0:T(8,128)(2,1)} %bitcast), calls=%async_computation.4 | async-start | bytes 2621440 | tf_op jit(solution)/shard_map/all_to_all | solution.py:534
  87.2 0.7 collective-permute-start.3
  88.0 1.3 collective-permute-start.4
  89.2 17.6 %all-to-all-done.4.got = bf16[64,80,128]{2,1,0:T(8,128)(2,1)S(1)} async-done(((bf16[64,80,128]{2,1,0:T(8,128)(2,1)}), bf16[64,80,128]{2,1,0:T(8,128)(2,1)S(1)}, u32[]{:S(2)}, u32[]{:S(2)}) %all-to-all-start.4) | async-done | bytes 1310752 | tf_op jit(solution)/shard_map/all_to_all | solution.py:534
  106.8 1.3 shard_map.135
  108.2 0.0 copy-start.3
  108.2 0.0 collective-permute-done.3.core_far
  108.2 0.0 collective-permute-done.4.chip_far
  108.2 7.6 %all-to-all-start.5 = ((bf16[64,80,128]{2,1,0:T(8,128)(2,1)}), bf16[64,80,128]{2,1,0:T(8,128)(2,1)S(1)}, u32[]{:S(2)}, u32[]{:S(2)}) async-start(bf16[64,80,128]{2,1,0:T(8,128)(2,1)} %shard_map.135), calls=%async_computation.5 | async-start | bytes 2621440 | tf_op jit(solution)/shard_map/all_to_all | solution.py:534
  115.8 0.0 copy-done.3
  115.8 3.7 %shard_map.136 = bf16[2,4,128,256]{3,2,1,0:T(8,128)(2,1)} custom-call(bf16[2,6,128,256]{3,2,1,0:T(8,128)(2,1)S(1)} %get-tuple-element.68.adj_far, bf16[2,2,128,256]{3,2,1,0:T(8,128)(2,1)} %collective-permute-done.3.core_far, bf16[2,2,128,256]{3,2,1,0:T(8,128)(2,1)} %collective-permute-done.4.chip_far, ...), custom_call_target="tpu_custom_call", output_to_operand_aliasing={{}: (4, {})} | custom-call | flops 1207959552 | bytes 3538944 | tf_op jit(solution)/shard_map/pallas_call | solution.py:34
  119.5 16.1 %all-to-all-done.5 = bf16[64,80,128]{2,1,0:T(8,128)(2,1)S(1)} async-done(((bf16[64,80,128]{2,1,0:T(8,128)(2,1)}), bf16[64,80,128]{2,1,0:T(8,128)(2,1)S(1)}, u32[]{:S(2)}, u32[]{:S(2)}) %all-to-all-start.5) | async-done | bytes 1310752 | tf_op jit(solution)/shard_map/all_to_all | solution.py:534
  135.6 2.6 %collective-permute-start.5 = (bf16[32,2,80,128]{3,2,1,0:T(8,128)(2,1)S(1)}, bf16[32,2,80,128]{3,2,1,0:T(8,128)(2,1)S(1)}, u32[]{:S(2)}, u32[]{:S(2)}) collective-permute-start(bf16[32,2,80,128]{3,2,1,0:T(8,128)(2,1)S(1)} %bitcast.5), channel_id=1, source_target_pairs={{0,1},{1,0},{2,3},{3,2},{4,5},{5,4},{6,7},{7,6},{8,9},{9,8},{10,11... | collective-permute-start | bytes 3932168 | tf_op jit(solution)/shard_map/ppermute | solution.py:660
  138.2 1.5 %shard_map.137 = (f32[3,3,256,256]{3,2,1,0:T(8,128)}, f32[3,3,256,256]{3,2,1,0:T(8,128)}) custom-call(bf16[32,2,80,128]{3,2,1,0:T(8,128)(2,1)S(1)} %bitcast.6), custom_call_target="tpu_custom_call" | custom-call | bytes 6029312 | tf_op jit(solution)/shard_map/pallas_call | solution.py:34
  139.7 1.2 collective-permute-done.5.got
  140.9 2.0 %shard_map.138 = (f32[3,3,256,256]{3,2,1,0:T(8,128)}, f32[3,3,256,256]{3,2,1,0:T(8,128)}, f32[2,128]{1,0:T(2,128)}, f32[2,128]{1,0:T(2,128)}, f32[1,2]{1,0:T(1,128)}) custom-call(bf16[32,2,80,128]{3,2,1,0:T(8,128)(2,1)S(1)} %bitcast.7, bf16[32,2,80,128]{3,2,1,0:T(8,128)(2,1)S(1)} %collective-permute-done.5.got, ...), custom_call_target="tpu_custom_call", output_to_operand_aliasing={{0}: (2, {}), {1}: (3, {})} | custom-call | bytes 12060680 | tf_op jit(solution)/shard_map/pallas_call | solution.py:34
  (1 shorter events, 0.0 us)
Async XLA Ops:
  1.7 9.0 %collective-permute-start.1 = (bf16[2,2,128,256]{3,2,1,0:T(8,128)(2,1)S(1)}, bf16[2,2,128,256]{3,2,1,0:T(8,128)(2,1)S(1)}, u32[]{:S(2)}, u32[]{:S(2)}) collective-permute-start(bf16[2,2,128,256]{3,2,1,0:T(8,128)(2,1)S(1)} %get-tuple-element.81), channel_id=1, source_target_pairs={{0,7},{1,2},{2,1},{3,4},{4,3},{5,6},{6,5},{7,0},{8,15},{9,10},{10,... | collective-permute-start | bytes 786440 | tf_op jit(solution)/shard_map/ppermute | solution.py:528
  4.8 5.9 %collective-permute-start = (bf16[2,2,128,256]{3,2,1,0:T(8,128)(2,1)S(1)}, bf16[2,2,128,256]{3,2,1,0:T(8,128)(2,1)S(1)}, u32[]{:S(2)}, u32[]{:S(2)}) collective-permute-start(bf16[2,2,128,256]{3,2,1,0:T(8,128)(2,1)S(1)} %get-tuple-element.82), channel_id=1, source_target_pairs={{0,1},{1,0},{2,3},{3,2},{4,5},{5,4},{6,7},{7,6},{8,9},{9,8},{10,11... | collective-permute-start | bytes 786440 | tf_op jit(solution)/shard_map/ppermute | solution.py:529
  7.5 1.0 copy-start
  8.5 1.3 copy-start.2
  12.9 28.5 %copy-start.1 = (bf16[3,3,256,256]{3,2,1,0:T(8,128)(2,1)S(1)}, bf16[3,3,256,256]{3,2,1,0:T(8,128)(2,1)}, u32[]{:S(2)}) copy-start(bf16[3,3,256,256]{3,2,1,0:T(8,128)(2,1)} %weight.1) | copy-start | bytes 3538948
  12.9 28.5 %copy-start.4 = (bf16[2,4,128,256]{3,2,1,0:T(8,128)(2,1)S(1)}, bf16[2,4,128,256]{3,2,1,0:T(8,128)(2,1)}, u32[]{:S(2)}) copy-start(bf16[2,4,128,256]{3,2,1,0:T(8,128)(2,1)} %cot.1) | copy-start | bytes 1572868
  72.4 6.3 %collective-permute-start.2 = (bf16[32,2,80,128]{3,2,1,0:T(8,128)(2,1)S(1)}, bf16[32,2,80,128]{3,2,1,0:T(8,128)(2,1)S(1)}, u32[]{:S(2)}, u32[]{:S(2)}) collective-permute-start(bf16[32,2,80,128]{3,2,1,0:T(8,128)(2,1)S(1)} %get-tuple-element.64), channel_id=1, source_target_pairs={{0,1},{1,0},{2,3},{3,2},{4,5},{5,4},{6,7},{7,6},{8,9},{9,8},{10,11... | collective-permute-start | bytes 3932168 | tf_op jit(solution)/shard_map/ppermute | solution.py:620
  79.9 27.0 %all-to-all-start.4 = ((bf16[64,80,128]{2,1,0:T(8,128)(2,1)}), bf16[64,80,128]{2,1,0:T(8,128)(2,1)S(1)}, u32[]{:S(2)}, u32[]{:S(2)}) async-start(bf16[64,80,128]{2,1,0:T(8,128)(2,1)} %bitcast), calls=%async_computation.4 | async-start | bytes 2621440 | tf_op jit(solution)/shard_map/all_to_all | solution.py:534
  87.2 21.0 %collective-permute-start.3 = (bf16[2,2,128,256]{3,2,1,0:T(8,128)(2,1)}, bf16[2,2,128,256]{3,2,1,0:T(8,128)(2,1)}, u32[]{:S(2)}, u32[]{:S(2)}) collective-permute-start(bf16[2,2,128,256]{3,2,1,0:T(8,128)(2,1)} %get-tuple-element.65), channel_id=1, source_target_pairs={{0,1},{1,0},{2,3},{3,2},{4,5},{5,4},{6,7},{7,6},{8,9},{9,8},{10,11... | collective-permute-start | bytes 786440 | tf_op jit(solution)/shard_map/ppermute | solution.py:529
  88.0 20.2 %collective-permute-start.4 = (bf16[2,2,128,256]{3,2,1,0:T(8,128)(2,1)S(1)}, bf16[2,2,128,256]{3,2,1,0:T(8,128)(2,1)}, u32[]{:S(2)}, u32[]{:S(2)}) collective-permute-start(bf16[2,2,128,256]{3,2,1,0:T(8,128)(2,1)S(1)} %get-tuple-element.66), channel_id=1, source_target_pairs={{0,7},{1,2},{2,1},{3,4},{4,3},{5,6},{6,5},{7,0},{8,15},{9,10},{10,... | collective-permute-start | bytes 786440 | tf_op jit(solution)/shard_map/ppermute | solution.py:528
  108.2 7.6 %copy-start.3 = (bf16[3,3,256,256]{3,2,1,0:T(8,128)(2,1)S(1)}, bf16[3,3,256,256]{3,2,1,0:T(8,128)(2,1)}, u32[]{:S(2)}) copy-start(bf16[3,3,256,256]{3,2,1,0:T(8,128)(2,1)} %weight_far.1) | copy-start | bytes 3538948
  108.2 27.4 %all-to-all-start.5 = ((bf16[64,80,128]{2,1,0:T(8,128)(2,1)}), bf16[64,80,128]{2,1,0:T(8,128)(2,1)S(1)}, u32[]{:S(2)}, u32[]{:S(2)}) async-start(bf16[64,80,128]{2,1,0:T(8,128)(2,1)} %shard_map.135), calls=%async_computation.5 | async-start | bytes 2621440 | tf_op jit(solution)/shard_map/all_to_all | solution.py:534
  135.6 5.3 %collective-permute-start.5 = (bf16[32,2,80,128]{3,2,1,0:T(8,128)(2,1)S(1)}, bf16[32,2,80,128]{3,2,1,0:T(8,128)(2,1)S(1)}, u32[]{:S(2)}, u32[]{:S(2)}) collective-permute-start(bf16[32,2,80,128]{3,2,1,0:T(8,128)(2,1)S(1)} %bitcast.5), channel_id=1, source_target_pairs={{0,1},{1,0},{2,3},{3,2},{4,5},{5,4},{6,7},{7,6},{8,9},{9,8},{10,11... | collective-permute-start | bytes 3932168 | tf_op jit(solution)/shard_map/ppermute | solution.py:660

commit v6 on v5

--- a/solution.py
+++ b/solution.py
@@ -45,11 +45,6 @@
 
 def far(array):
     return array, HB
-
-
-def fetch_wait(sems, *pairs):
-    for i, (s, d) in enumerate(pairs):
-        pltpu.make_async_copy(s, d, sems.at[i]).wait()
 
 
 def fetch(sems, *pairs):
@@ -243,32 +238,23 @@
 GELU_A = math.sqrt(2 / math.pi)
 
 
-def spread(*vectors):
-    row = lax.broadcasted_iota(jnp.int32, (8, 128), 0) % 4
-    halves = []
-    for half in HALVES:
-        out = jnp.zeros((8, 128), F32)
-        for k, vector in enumerate(vectors):
-            out = jnp.where(row == k, jnp.broadcast_to(vector[:, half], (8, 128)), out)
-        halves.append(out)
-    return halves
-
-
-def split_pairs(both):
+def small_rows(rate, skip, steps):
     row = lax.broadcasted_iota(jnp.int32, (8, 128), 0)
-    top = both.astype(BF).astype(F32)
-    return jnp.where(row < 4, top, both - top)
-
-
-def joined(pairs):
-    return pairs + pltpu.roll(pairs, 4, 0)
+    halves = [v[:, half] for v in (rate, skip) for half in HALVES]
+    lines = halves + [steps, steps] + halves[0:2]
+    out = jnp.zeros((8, 128), F32)
+    for k, line in enumerate(lines):
+        out = jnp.where(row == k, jnp.broadcast_to(line, (8, 128)), out)
+    top = out.astype(BF).astype(F32)
+    return jnp.where(row < 5, top, out - top).astype(BF)
 
 
 def middle_body(
     local, carry, x, cot, weight, table,
-    out_far, direct_far, gz, state, state_f, local_adj, send, skip, out, direct, sems,
+    out_far, direct_far, message, state_f, local_adj, send, skip, out, direct, sems,
 ):
     spot = Spot()
+    state, gz = message.at[:, 0:WIDE], message.at[:, WIDE:]
     d0, d1 = table[0:1, :], table[1:2, :]
     for h, half in blocks(WIDE):
         c = take_chunks(carry, h, half)
@@ -312,23 +298,21 @@
 def pack_grad(g, a, scale, out):
     for b in range(3):
         tap = (3 * a + b) * 8
-        for lg, half in enumerate(HALVES):
-            part = g[b * CHANS : (b + 1) * CHANS, half] * scale
-            out[:, lg, tap : tap + 8, :] = part.astype(BF).reshape(GROUPS, 8, 128)
-
-
-def out_grad_body(scale, state, gz, out, flat):
+        part = (g[b * CHANS : (b + 1) * CHANS] * scale).astype(BF)
+        out[:, tap : tap + 8, :] = part.reshape(GROUPS, 8, CHANS)
+
+
+def out_grad(state, gz, flat):
     transpose_rows(state, flat, WIDE, lambda t, h: t * WIDE + h)
     rhs = gz[...].reshape(FRAMES * HEIGHT * WIDTH, CHANS)
     for a in range(3):
         lhs = jnp.concatenate(
             [flat[:, pl.ds((t * WIDE + a) * WIDTH, HEIGHT * WIDTH)] for t in range(FRAMES)], axis=1
         )
-        pack_grad(jnp.dot(lhs, rhs, preferred_element_type=F32), a, scale, out)
-    out[:, :, TAPS:PACK, :] = jnp.zeros((GROUPS, 2, 8, 128), BF)
-
-
-def in_grad(scale, adj, small, flat_mid, flat_edge, out):
+        yield a, jnp.dot(lhs, rhs, preferred_element_type=F32)
+
+
+def in_grad(adj, flat_mid, flat_edge):
     rhs = adj[...].reshape(FRAMES * WIDE * WIDTH, CHANS)
     for a in range(3):
         pieces = []
@@ -339,18 +323,11 @@
             pieces.append(flat_mid[:, at : at + 4 * WIDTH])
             if a > 0:
                 pieces.append(flat_edge[:, at + 2 * WIDTH : at + (2 + a) * WIDTH])
-        g = jnp.dot(jnp.concatenate(pieces, axis=1), rhs, preferred_element_type=F32)
-        pack_grad(g, a, scale, out)
-    out[:, :, TAPS:PACK, :] = jnp.zeros((GROUPS, 2, 8, 128), BF)
-    for lg in range(2):
-        out[0, lg, TAPS:PACK, :] = split_pairs(small[lg]).astype(BF)
-
-
-def odd_grad_body(
-    scale, step_scale, local, incoming, state_f, carry, table, skip, flat_mid, flat_edge, out_part,
-    payload, small, adj, adj_far, to_core, to_chip, sems,
-):
-    spot = Spot()
+        yield a, jnp.dot(jnp.concatenate(pieces, axis=1), rhs, preferred_element_type=F32)
+
+
+def adjoint_stage(scales, spot, sources, adj, small):
+    local, incoming, state_f, carry, table, skip = sources
     d0, d1 = table[0:1, :], table[1:2, :]
     sums = [[jnp.zeros((8, 128), F32) for _ in HALVES] for _ in range(FRAMES)]
     for h, half in blocks(WIDE):
@@ -363,53 +340,58 @@
         pairs = ((a0, take_chunks(carry, h, half)), (a1, state_f[h, :, half]))
         for t, (a, earlier) in enumerate(pairs):
             sums[t][k] = sums[t][k] + jnp.sum((a * earlier).reshape(WIDTH // 8, 8, 128), axis=0)
-    up, down = adj.at[:, 0:2], adj.at[:, WIDE - 2 :]
-    (whole,) = fetch(sems.at[2:3], (adj, adj_far))
-
-    @pl.when(spot.core == 0)
-    def _():
-        fetch(sems, (up, to_chip), (down, to_core))
-
-    @pl.when(spot.core == 1)
-    def _():
-        fetch(sems, (down, to_chip), (up, to_core))
-
     k0, k1 = (
         jnp.concatenate([jnp.sum(v, axis=0, keepdims=True) for v in pair], axis=1) * d
         for pair, d in zip(sums, (d0, d1))
     )
-    rate_part = (k0 * table[2:3, :] + k1 * table[3:4, :]) * (-scale)
-    s0 = jnp.sum(k0 * table[4:5, :], axis=1, keepdims=True) * (-step_scale)
-    s1 = jnp.sum(k1 * table[4:5, :], axis=1, keepdims=True) * (-step_scale)
-    lane = lax.broadcasted_iota(jnp.int32, (1, CHANS), 1)
+    rate = (k0 * table[2:3, :] + k1 * table[3:4, :]) * (-scales[0])
+    s0 = jnp.sum(k0 * table[4:5, :], axis=1, keepdims=True) * (-scales[1])
+    s1 = jnp.sum(k1 * table[4:5, :], axis=1, keepdims=True) * (-scales[1])
+    lane = lax.broadcasted_iota(jnp.int32, (1, 128), 1)
     at = spot.place * FRAMES
     steps = jnp.where(lane == at, s0, jnp.where(lane == at + 1, s1, 0.0))
-    small[0], small[1] = spread(rate_part, steps, skip[...] * scale)
+    small[...] = small_rows(rate, skip[...] * scales[0], steps)
+
+
+def odd_grad_body(
+    scales, local, incoming, state_f, carry, table, skip, flat_mid, flat_edge, message, flat_message,
+    payload, out_part, adj, small, flat,
+):
+    spot = Spot()
 
     @pl.when(spot.core == 0)
     def _():
-        (copy,) = fetch(sems.at[3:4], (out_part, payload))
-        copy.wait()
+        payload[...] = flat_message[...]
 
     @pl.when(spot.core == 1)
     def _():
-        in_grad(scale, adj, small, flat_mid, flat_edge, payload)
-
-    fetch_wait(sems, (up, to_chip), (down, to_core))
-    whole.wait()
-
-
-def even_grad_body(scale, adj, small, flat_mid, flat_edge, out_part, mine, sems):
+        adjoint_stage(scales, spot, (local, incoming, state_f, carry, table, skip), adj, small)
+        for a, g in in_grad(adj, flat_mid, flat_edge):
+            pack_grad(g, a, scales[0], payload)
+        for a, g in out_grad(message.at[:, 0:WIDE], message.at[:, WIDE:], flat):
+            pack_grad(g, a, scales[0], out_part)
+
+
+def even_grad_body(
+    scales, local, incoming, state_f, carry, table, skip, flat_mid, flat_edge, odd_adj, odd_small,
+    mine, adj, to_core, to_chip, small,
+):
     spot = Spot()
 
     @pl.when(spot.core == 0)
     def _():
-        in_grad(scale, adj, small, flat_mid, flat_edge, mine)
+        adjoint_stage(scales, spot, (local, incoming, state_f, carry, table, skip), adj, small)
+        to_chip[...] = adj[:, 0:2]
+        to_core[...] = adj[:, WIDE - 2 :]
+        for a, g in in_grad(adj, flat_mid, flat_edge):
+            pack_grad(g, a, scales[0], mine)
 
     @pl.when(spot.core == 1)
     def _():
-        (copy,) = fetch(sems, (out_part, mine))
-        copy.wait()
+        adj[...] = odd_adj[...]
+        small[...] = odd_small[...]
+        to_core[...] = odd_adj[:, 0:2]
+        to_chip[...] = odd_adj[:, WIDE - 2 :]
 
 
 def grad_inputs_body(
@@ -440,27 +422,43 @@
     copy.wait()
 
 
-def pair_sum_body(mine, got, send_far, send, sems):
-    copies = []
-    for k in range(GROUPS):
-        send[k] = (mine[k].astype(F32) + got[k].astype(F32)).astype(BF)
-        if k == 0:
-            for lg in range(2):
-                pairs = mine[0, lg, TAPS:PACK, :].astype(F32) + got[0, lg, TAPS:PACK, :].astype(F32)
-                send[0, lg, TAPS:PACK, :] = split_pairs(joined(pairs)).astype(BF)
-        if k % 8 == 7:
-            part = slice(k - 7, k + 1)
-            copies += fetch(sems.at[k // 8 : k // 8 + 1], (send.at[part], send_far.at[part]))
-    for copy in copies:
-        copy.wait()
-
-
-def all_sum_body(got, send_far, send, sems):
-    total = jnp.zeros((PACK, 128), F32)
+def pair_sum_body(scale, mine, out_part, got, message, send_far, send, flat, sems):
+    core = Spot().core
+
+    @pl.when(core == 0)
+    def _():
+        copies = []
+        for k in range(GROUPS):
+            total = mine[k].astype(F32) + got[k, 0:TAPS, :].astype(F32)
+            for lg, half in enumerate(HALVES):
+                send[k, lg] = total[:, half].astype(BF)
+            if k % 8 == 7:
+                part = slice(k - 7, k + 1)
+                copies += fetch(sems.at[k // 8 : k // 8 + 1], (send.at[part], send_far.at[part]))
+        for copy in copies:
+            copy.wait()
+
+    @pl.when(core == 1)
+    def _():
+        copies = []
+        for a, g in out_grad(message.at[:, 0:WIDE], message.at[:, WIDE:], flat):
+            for b in range(3):
+                tap = (3 * a + b) * 8
+                own = out_part[:, tap : tap + 8, :].astype(F32)
+                total = g[b * CHANS : (b + 1) * CHANS].reshape(GROUPS, 8, CHANS) * scale + own
+                for lg, half in enumerate(HALVES):
+                    send[:, lg, tap : tap + 8, :] = total[:, :, half].astype(BF)
+            part = slice(24 * a, 24 * a + 24)
+            copies += fetch(sems.at[a : a + 1], (send.at[:, :, part], send_far.at[:, :, part]))
+        for copy in copies:
+            copy.wait()
+
+
+def all_sum_body(got, small, send_far, send, sems):
+    total = jnp.zeros((TAPS, 128), F32)
     for k in range(CHIPS):
         total = total + got[k].astype(F32)
-    extras = split_pairs(joined(total[TAPS:PACK]))
-    total = jnp.concatenate([total[0:TAPS], extras], axis=0).astype(BF)
+    total = jnp.concatenate([total.astype(BF), small[...]], axis=0)
     send[...] = jnp.broadcast_to(total[None], send.shape)
     pairs = [(send, send_far.at[8 * k : 8 * k + 8]) for k in range(8)]
     for copy in fetch(sems, *pairs):
@@ -469,15 +467,13 @@
 
 def write_grad(src, grad, stage, sems):
     copies = []
-    for a in range(3):
-        for b in range(3):
-            tap = (3 * a + b) * 8
-            for lg, half in enumerate(HALVES):
-                part = src[:, lg, tap : tap + 8, :].astype(F32)
-                stage[a, b, :, half] = part.reshape(CHANS, 128)
-        copies += fetch(sems.at[a : a + 1], (stage.at[a], grad.at[a]))
-    for copy in copies:
-        copy.wait()
+    for tap in range(9):
+        a, b = tap // 3, tap % 3
+        for lg, half in enumerate(HALVES):
+            part = src[:, lg, tap * 8 : tap * 8 + 8, :].astype(F32)
+            stage[a, b, :, half] = part.reshape(CHANS, 128)
+        copies += fetch(sems.at[tap : tap + 1], (stage.at[a, b], grad.at[a, b]))
+    return copies
 
 
 def unpack_own_body(own, grad_out, grad_in, stage, sems):
@@ -485,11 +481,13 @@
 
     @pl.when(core == 0)
     def _():
-        write_grad(own, grad_in, stage, sems)
+        for copy in write_grad(own, grad_in, stage, sems):
+            copy.wait()
 
     @pl.when(core == 1)
     def _():
-        write_grad(own, grad_out, stage, sems)
+        for copy in write_grad(own, grad_out, stage, sems):
+            copy.wait()
 
 
 def unpack_other_body(
@@ -498,24 +496,30 @@
     del out_half, in_half
     spot = Spot()
 
-    def smalls(src):
-        for lg in range(2):
-            extras = joined(src[0, lg, TAPS:PACK, :].astype(F32))
-            rate[lg : lg + 1, :] = extras[0:1]
-            skip[lg : lg + 1, :] = extras[2:3]
-            if lg == 0:
-                turned = pltpu.roll(extras, (128 - spot.place * FRAMES) % 128, 1)
-                step[...] = turned[1:2, 0:FRAMES]
+    def smalls():
+        total = jnp.zeros((8, 128), F32)
+        for k in range(GROUPS):
+            for lg in range(2):
+                pair = own[k, lg, TAPS:PACK, :].astype(F32) + got[k, lg, TAPS:PACK, :].astype(F32)
+                total = total + pair
+        rate[...] = total[0:2] + total[6:8]
+        skip[...] = total[2:4]
+        steps = total + pltpu.roll(total, 7, 0)
+        step[...] = pltpu.roll(steps, (128 - spot.place * FRAMES) % 128, 1)[4:5, 0:FRAMES]
 
     @pl.when(spot.core == 0)
     def _():
-        smalls(own)
-        write_grad(got, grad_out, stage, sems)
+        copies = write_grad(got, grad_out, stage, sems)
+        smalls()
+        for copy in copies:
+            copy.wait()
 
     @pl.when(spot.core == 1)
     def _():
-        smalls(got)
-        write_grad(got, grad_in, stage, sems)
+        copies = write_grad(got, grad_in, stage, sems)
+        smalls()
+        for copy in copies:
+            copy.wait()
 
 
 ROWS_AXES = ("z", "core")
@@ -548,10 +552,13 @@
     core = lax.axis_index("core")
     field = (FRAMES, HEIGHT, WIDTH, CHANS)
     wide = (FRAMES, WIDE, WIDTH, CHANS)
+    message = (FRAMES, WIDE + HEIGHT, WIDTH, CHANS)
     edge = (FRAMES, 2, WIDTH, CHANS)
     kernel = (3, 3, CHANS, CHANS)
     chunk = sds((BLOCKS, PLACES, CHANS), BF)
     packed = sds((GROUPS, 2, PACK, 128), BF)
+    part = sds((GROUPS, TAPS, CHANS), BF)
+    scales = (scale, step_scale)
     flat = sds((3 * CHANS, FRAMES * 4 * WIDTH), BF)
     params = jnp.concatenate([rates, skip_gain, jnp.pad(step_sizes, (0, CHANS - FRAMES))])
     params = params.reshape(3, CHANS)
@@ -576,13 +583,12 @@
     got = swap(send, TM_AXES)
     send, block_decays = call(forward_scan_body, [chunk, sds((BLOCKS, CHANS), F32)], [got, table])
     carry = swap(send, TM_AXES)
-    outputs, direct, gz, state, state_f, local_adj, send, skip = call(
+    outputs, direct, sent, state_f, local_adj, send, skip = call(
         middle_body,
         [
             far(sds(field, BF)),
             far(sds(field, BF)),
-            sds(field, BF),
-            sds(wide, BF),
+            sds(message, BF),
             sds(wide[1:], F32),
             sds(wide, F32),
             chunk,
@@ -592,46 +598,42 @@
         (HEIGHT + WIDE) * ROW_FLOPS,
         [vmem(field), vmem(field), sems(FRAMES, 2)],
     )
-    (out_part,) = call(
-        functools.partial(out_grad_body, scale),
-        [packed],
-        [state, gz],
-        HEIGHT * ROW_FLOPS,
-        [vmem((3 * CHANS, FRAMES * WIDE * WIDTH))],
-    )
-    send, out_part = lax.optimization_barrier((send, out_part))
     got = swap(send, TM_AXES)
     (send,) = call(backward_scan_body, [chunk], [got, block_decays])
     incoming = swap(send, TM_AXES)
-    payload, small, adj, adj_far, to_core, to_chip = call(
-        functools.partial(odd_grad_body, scale, step_scale),
+    sources = [local_adj, incoming, state_f, carry, table, skip, flat_mid, flat_edge]
+    flat_sent = sent.reshape(GROUPS, PACK, CHANS)
+    payload, out_part, odd_adj, odd_small = call(
+        functools.partial(odd_grad_body, scales),
+        [sds(flat_sent.shape, BF), part, sds(wide, BF), sds((8, 128), BF)],
+        [*sources, sent, flat_sent],
+        WIDE * ROW_FLOPS,
+        [vmem((3 * CHANS, FRAMES * WIDE * WIDTH))],
+    )
+    got = lax.ppermute(payload, ROWS_AXES, CORE_PAIRS)
+    mine, adj, to_core, to_chip, small = call(
+        functools.partial(even_grad_body, scales),
+        [part, sds(wide, BF), sds(edge, BF), sds(edge, BF), sds((8, 128), BF)],
+        [*sources, odd_adj, odd_small],
+        WIDE * ROW_FLOPS,
+    )
+    from_core, from_chip = halos(to_core, to_chip)
+    (send,) = call(
+        functools.partial(pair_sum_body, scale),
+        [far(sds((GROUPS, 2, TAPS, 128), BF))],
+        [mine, out_part, got, got.reshape(message)],
+        HEIGHT * ROW_FLOPS,
         [
-            packed,
-            sds((2, 8, 128), F32),
-            sds(wide, BF),
-            far(sds(wide, BF)),
-            far(sds(edge, BF)),
-            far(sds(edge, BF)),
+            vmem((GROUPS, 2, TAPS, 128)),
+            vmem((3 * CHANS, FRAMES * WIDE * WIDTH)),
+            sems(4),
         ],
-        [local_adj, incoming, state_f, carry, table, skip, flat_mid, flat_edge, out_part],
-        WIDE * ROW_FLOPS,
-        [sems(4)],
-    )
-    got = lax.ppermute(payload, ROWS_AXES, CORE_PAIRS)
-    (mine,) = call(
-        functools.partial(even_grad_body, scale),
-        [packed],
-        [adj, small, flat_mid, flat_edge, out_part],
-        WIDE * ROW_FLOPS,
-        [sems(1)],
-    )
-    from_core, from_chip = halos(to_core, to_chip)
-    (send,) = call(pair_sum_body, [far(packed)], [mine, got], 0, [vmem(packed.shape), sems(4)])
-    got = swap(send.reshape(CHIPS, PACK, 128), ("x", "y", "z"))
+    )
+    got = swap(send.reshape(CHIPS, TAPS, 128), ("x", "y", "z"))
     (send,) = call(
         all_sum_body,
         [far(sds((CHIPS, PACK, 128), BF))],
-        [got],
+        [got, small],
         0,
         [vmem((8, PACK, 128)), sems(8)],
     )
@@ -640,7 +642,7 @@
     (grad_inputs,) = call(
         grad_inputs_body,
         [far(sds(field, BF))],
-        [far(a) for a in (adj_far, from_core, from_chip, in_weight, direct)],
+        [far(a) for a in (adj, from_core, from_chip, in_weight, direct)],
         HEIGHT * ROW_FLOPS,
         [
             vmem(wide),
@@ -662,14 +664,14 @@
     half = sds((2, 128), F32)
     stage = vmem(kernel, F32)
     grad_out_weight, grad_in_weight = call(
-        unpack_own_body, [far(weights), far(weights)], [own], 0, [stage, sems(3)]
+        unpack_own_body, [far(weights), far(weights)], [own], 0, [stage, sems(9)]
     )
     grad_out_weight, grad_in_weight, grad_rates, grad_skip, grad_steps = call(
         unpack_other_body,
         [far(weights), far(weights), half, half, sds((1, FRAMES), F32)],
         [own, other, far(grad_out_weight), far(grad_in_weight)],
         0,
-        [stage, sems(3)],
+        [stage, sems(9)],
         {2: 0, 3: 1},
     )
     return (

time: 144 us -> 141 us (0.979)
  starting transfers between devices: 28.3 us -> 23.7 us
  Pallas kernels: 21 us -> 22.5 us
    ppermute x1, starting transfers between devices: 3.64 us -> 1.57 us  [on_device(): got = lax.ppermute(payload, ROWS_AXES, CORE_PAIRS)]
    all_to_all x2, starting transfers between devices: 14.9 us -> 13.1 us  [swap(): return lax.all_to_all(chunks, axes, 0, 0)]
    pallas_call x13 -> x12, Pallas kernels: 21 us -> 22.5 us  [call(): pl.pallas_call(body, out_shape=[o for o, _ in outs], in_specs=[s for _, s...]
  transfers between devices with their start and end apart: 8 -> 8, of which waited for: 4 -> 4; matrix products, arithmetic and copies ran while one was open for 1% -> 1% of each run, Pallas kernels for 5% -> 6%
where the time goes in v6:
time: 141 us; the launch traced here: 140 us
  blocking collectives  51.3 us (36%)
  waiting for transfers between devices  37.7 us (27%)
  starting transfers between devices  23.7 us (17%)
  Pallas kernels  22.5 us (16%)
  local copies, waits for them, and re-layouts  3.41 us (2%)
    all_to_all x4, blocking collectives, swap(): return lax.all_to_all(chunks, axes, 0, 0)  51.3 us
    all_to_all x2, waiting for transfers between devices, swap(): return lax.all_to_all(chunks, axes, 0, 0)  34.7 us
    pallas_call x12, Pallas kernels, call(): pl.pallas_call(body, out_shape=[o for o, _ in outs], in_specs=[s for _, s...  22.5 us
    all_to_all x2, starting transfers between devices, swap(): return lax.all_to_all(chunks, axes, 0, 0)  13.1 us
    ppermute x2, starting transfers between devices, halos(): from_chip = lax.ppermute(to_chip, ROWS_AXES, CHIP_PAIRS)  4.5 us
  transfers between devices with their start and end apart: 8, of which 4 were waited for; matrix products, arithmetic and copies ran while one was open for 1% of the time, Pallas kernels for 6%

profile of v6, /device:TPU:1, one launch (start us, length us, event | category | flops | bytes accessed | tf_op | source)
XLA Modules:
  0.0 140.3 jit_solution(2391612242923380834)
XLA Ops:
  0.6 1.1 constant_dynamic-slice_fusion
  1.7 3.1 %collective-permute-start.1 = (bf16[2,2,128,256]{3,2,1,0:T(8,128)(2,1)S(1)}, bf16[2,2,128,256]{3,2,1,0:T(8,128)(2,1)S(1)}, u32[]{:S(2)}, u32[]{:S(2)}) collective-permute-start(bf16[2,2,128,256]{3,2,1,0:T(8,128)(2,1)S(1)} %get-tuple-element.81), channel_id=1, source_target_pairs={{0,7},{1,2},{2,1},{3,4},{4,3},{5,6},{6,5},{7,0},{8,15},{9,10},{10,... | collective-permute-start | bytes 786440 | tf_op jit(solution)/shard_map/ppermute | solution.py:532
  4.8 2.0 %collective-permute-start = (bf16[2,2,128,256]{3,2,1,0:T(8,128)(2,1)S(1)}, bf16[2,2,128,256]{3,2,1,0:T(8,128)(2,1)S(1)}, u32[]{:S(2)}, u32[]{:S(2)}) collective-permute-start(bf16[2,2,128,256]{3,2,1,0:T(8,128)(2,1)S(1)} %get-tuple-element.82), channel_id=1, source_target_pairs={{0,1},{1,0},{2,3},{3,2},{4,5},{5,4},{6,7},{7,6},{8,9},{9,8},{10,11... | collective-permute-start | bytes 786440 | tf_op jit(solution)/shard_map/ppermute | solution.py:533
  6.8 0.7 select_maximum_fusion
  7.5 0.0 copy-start
  7.5 1.0 copy-done
  8.5 0.0 copy-start.2
  8.6 1.3 copy-done.2
  9.8 0.9 shard_map.126
  10.7 0.0 collective-permute-done.1.from_chip
  10.7 0.0 collective-permute-done.from_core
  10.7 2.1 %shard_map.127 = (f32[2,6,128,256]{3,2,1,0:T(8,128)S(1)}, bf16[16,56,256]{2,1,0:T(8,128)(2,1)S(1)}, bf16[768,1024]{1,0:T(8,128)(2,1)S(1)}) custom-call(bf16[2,4,128,256]{3,2,1,0:T(8,128)(2,1)S(1)} %get-tuple-element.44.x, bf16[2,2,128,256]{3,2,1,0:T(8,128)(2,1)S(1)} %collective-permute-done.from_core, ...), custom_call_target="tpu_custom_call" | custom-call | flops 1811939328 | bytes 5840896 | tf_op jit(solution)/shard_map/pallas_call | solution.py:34
  12.9 0.0 copy-start.1
  12.9 0.0 copy-start.4
  12.9 16.3 %all_to_all.30.got = bf16[16,56,256]{2,1,0:T(8,128)(2,1)S(1)} all-to-all(bf16[16,56,256]{2,1,0:T(8,128)(2,1)S(1)} %get-tuple-element.48), channel_id=1, replica_groups=mesh['x'=4,'y'=4,'z'=4,'core'=2] {'x','y'}, dimensions={0} | all-to-all | bytes 917504 | tf_op jit(solution)/shard_map/all_to_all | solution.py:538
  29.2 0.1 shard_map.128
  29.4 12.0 %all_to_all.31.carry = bf16[16,48,256]{2,1,0:T(8,128)(2,1)S(1)} all-to-all(bf16[16,48,256]{2,1,0:T(8,128)(2,1)S(1)} %get-tuple-element.49), channel_id=1, replica_groups=mesh['x'=4,'y'=4,'z'=4,'core'=2] {'x','y'}, dimensions={0} | all-to-all | bytes 786432 | tf_op jit(solution)/shard_map/all_to_all | solution.py:538
  41.4 0.0 copy-done.1
  41.4 0.0 copy-done.4
  41.4 3.7 %shard_map.129 = (bf16[2,4,128,256]{3,2,1,0:T(8,128)(2,1)}, bf16[2,4,128,256]{3,2,1,0:T(8,128)(2,1)}, bf16[2,10,128,256]{3,2,1,0:T(8,128)(2,1)S(1)}, f32[6,128,2...) custom-call(f32[2,6,128,256]{3,2,1,0:T(8,128)S(1)} %get-tuple-element, ...), custom_call_target="tpu_custom_call" | custom-call | flops 3019898880 | bytes 9315328 | tf_op jit(solution)/shard_map/pallas_call | solution.py:34
  45.1 11.5 %all_to_all.32.got = bf16[16,48,256]{2,1,0:T(8,128)(2,1)S(1)} all-to-all(bf16[16,48,256]{2,1,0:T(8,128)(2,1)S(1)} %get-tuple-element.52), channel_id=1, replica_groups=mesh['x'=4,'y'=4,'z'=4,'core'=2] {'x','y'}, dimensions={0} | all-to-all | bytes 786432 | tf_op jit(solution)/shard_map/all_to_all | solution.py:538
  56.6 0.1 shard_map.130
  56.7 11.5 %all_to_all.33.incoming = bf16[16,48,256]{2,1,0:T(8,128)(2,1)S(1)} all-to-all(bf16[16,48,256]{2,1,0:T(8,128)(2,1)S(1)} %shard_map.130), channel_id=1, replica_groups=mesh['x'=4,'y'=4,'z'=4,'core'=2] {'x','y'}, dimensions={0} | all-to-all | bytes 786432 | tf_op jit(solution)/shard_map/all_to_all | solution.py:538
  68.2 3.6 %shard_map.131 = (bf16[32,80,256]{2,1,0:T(8,128)(2,1)S(1)}, bf16[32,72,256]{2,1,0:T(8,128)(2,1)S(1)}, bf16[2,6,128,256]{3,2,1,0:T(8,128)(2,1)S(1)}, bf16[8,128]{1,0:T(8,128)(2,1)S(1)}) custom-call(f32[2,6,128,256]{3,2,1,0:T(8,128)S(1)} %get-tuple-element.51.local, bf16[16,48,256]{2,1,0:T(8,128)(2,1)S(1)} %all_to_all.33.incoming, ...), custom_call_target="tpu_custom_call" | custom-call | flops 1811939328 | bytes 12200960 | tf_op jit(solution)/shard_map/pallas_call | solution.py:34
  71.7 1.6 %collective-permute-start.2 = (bf16[32,80,256]{2,1,0:T(8,128)(2,1)S(1)}, bf16[32,80,256]{2,1,0:T(8,128)(2,1)S(1)}, u32[]{:S(2)}, u32[]{:S(2)}) collective-permute-start(bf16[32,80,256]{2,1,0:T(8,128)(2,1)S(1)} %get-tuple-element.63), channel_id=1, source_target_pairs={{0,1},{1,0},{2,3},{3,2},{4,5},{5,4},{6,7},{7,6},{8,9},{9,8},{10,11... | collective-permute-start | bytes 3932168 | tf_op jit(solution)/shard_map/ppermute | solution.py:613
  73.3 0.8 shard_map.132
  74.1 1.9 %collective-permute-done.2.got = bf16[32,80,256]{2,1,0:T(8,128)(2,1)S(1)} collective-permute-done((bf16[32,80,256]{2,1,0:T(8,128)(2,1)S(1)}, bf16[32,80,256]{2,1,0:T(8,128)(2,1)S(1)}, u32[]{:S(2)}, u32[]{:S(2)}) %collective-permute-start.2) | collective-permute-done | bytes 1310752 | tf_op jit(solution)/shard_map/ppermute | solution.py:613
  76.0 2.6 %shard_map.133 = bf16[32,2,72,128]{3,2,1,0:T(8,128)(2,1)} custom-call(bf16[32,72,256]{2,1,0:T(8,128)(2,1)S(1)} %get-tuple-element.61.mine, bf16[32,72,256]{2,1,0:T(8,128)(2,1)S(1)} %get-tuple-element.62.out_part, bf16[32,80,256]{2,1,0:T(8,128)(2,1)S(1)} %collective-permute-done.2.got, bf16[2,10,128,256]{3,2,1,0:T(8,128)(2,1)S(1)} %bitcast.10), custom_call_target="tpu_custom_call" | custom-call | flops 1207959552 | bytes 6160384 | tf_op jit(solution)/shard_map/pallas_call | solution.py:34
  78.6 7.3 %all-to-all-start.4 = ((bf16[64,72,128]{2,1,0:T(8,128)(2,1)}), bf16[64,72,128]{2,1,0:T(8,128)(2,1)S(1)}, u32[]{:S(2)}, u32[]{:S(2)}) async-start(bf16[64,72,128]{2,1,0:T(8,128)(2,1)} %bitcast.2), calls=%async_computation.4 | async-start | bytes 2359296 | tf_op jit(solution)/shard_map/all_to_all | solution.py:538
  85.9 0.1 collective-permute-start.3
  86.0 1.4 collective-permute-start.4
  87.4 18.5 %all-to-all-done.4.got = bf16[64,72,128]{2,1,0:T(8,128)(2,1)S(1)} async-done(((bf16[64,72,128]{2,1,0:T(8,128)(2,1)}), bf16[64,72,128]{2,1,0:T(8,128)(2,1)S(1)}, u32[]{:S(2)}, u32[]{:S(2)}) %all-to-all-start.4) | async-done | bytes 1179680 | tf_op jit(solution)/shard_map/all_to_all | solution.py:538
  105.9 1.3 shard_map.134
  107.2 0.0 copy-start.3
  107.2 0.0 collective-permute-done.3.core_far
  107.2 0.0 collective-permute-done.4.chip_far
  107.2 5.8 %all-to-all-start.5 = ((bf16[64,80,128]{2,1,0:T(8,128)(2,1)}), bf16[64,80,128]{2,1,0:T(8,128)(2,1)S(1)}, u32[]{:S(2)}, u32[]{:S(2)}) async-start(bf16[64,80,128]{2,1,0:T(8,128)(2,1)} %shard_map.134), calls=%async_computation.5 | async-start | bytes 2621440 | tf_op jit(solution)/shard_map/all_to_all | solution.py:538
  113.0 0.0 copy-done.3
  113.0 3.7 %shard_map.135 = bf16[2,4,128,256]{3,2,1,0:T(8,128)(2,1)} custom-call(bf16[2,6,128,256]{3,2,1,0:T(8,128)(2,1)S(1)} %get-tuple-element.68.adj_far, bf16[2,2,128,256]{3,2,1,0:T(8,128)(2,1)} %collective-permute-done.3.core_far, bf16[2,2,128,256]{3,2,1,0:T(8,128)(2,1)} %collective-permute-done.4.chip_far, ...), custom_call_target="tpu_custom_call", output_to_operand_aliasing={{}: (4, {})} | custom-call | flops 1207959552 | bytes 3538944 | tf_op jit(solution)/shard_map/pallas_call | solution.py:34
  116.7 16.2 %all-to-all-done.5 = bf16[64,80,128]{2,1,0:T(8,128)(2,1)S(1)} async-done(((bf16[64,80,128]{2,1,0:T(8,128)(2,1)}), bf16[64,80,128]{2,1,0:T(8,128)(2,1)S(1)}, u32[]{:S(2)}, u32[]{:S(2)}) %all-to-all-start.5) | async-done | bytes 1310752 | tf_op jit(solution)/shard_map/all_to_all | solution.py:538
  133.0 2.5 %collective-permute-start.5 = (bf16[32,2,80,128]{3,2,1,0:T(8,128)(2,1)S(1)}, bf16[32,2,80,128]{3,2,1,0:T(8,128)(2,1)S(1)}, u32[]{:S(2)}, u32[]{:S(2)}) collective-permute-start(bf16[32,2,80,128]{3,2,1,0:T(8,128)(2,1)S(1)} %bitcast.7), channel_id=1, source_target_pairs={{0,1},{1,0},{2,3},{3,2},{4,5},{5,4},{6,7},{7,6},{8,9},{9,8},{10,11... | collective-permute-start | bytes 3932168 | tf_op jit(solution)/shard_map/ppermute | solution.py:662
  135.4 1.5 %shard_map.136 = (f32[3,3,256,256]{3,2,1,0:T(8,128)}, f32[3,3,256,256]{3,2,1,0:T(8,128)}) custom-call(bf16[32,2,80,128]{3,2,1,0:T(8,128)(2,1)S(1)} %bitcast.8), custom_call_target="tpu_custom_call" | custom-call | bytes 6029312 | tf_op jit(solution)/shard_map/pallas_call | solution.py:34
  136.9 1.2 collective-permute-done.5.got
  138.1 2.1 %shard_map.137 = (f32[3,3,256,256]{3,2,1,0:T(8,128)}, f32[3,3,256,256]{3,2,1,0:T(8,128)}, f32[2,128]{1,0:T(2,128)}, f32[2,128]{1,0:T(2,128)}, f32[1,2]{1,0:T(1,128)}) custom-call(bf16[32,2,80,128]{3,2,1,0:T(8,128)(2,1)S(1)} %bitcast.9, bf16[32,2,80,128]{3,2,1,0:T(8,128)(2,1)S(1)} %collective-permute-done.5.got, ...), custom_call_target="tpu_custom_call", output_to_operand_aliasing={{0}: (2, {}), {1}: (3, {})} | custom-call | bytes 12060680 | tf_op jit(solution)/shard_map/pallas_call | solution.py:34
  (1 shorter events, 0.0 us)
Async XLA Ops:
  1.7 9.0 %collective-permute-start.1 = (bf16[2,2,128,256]{3,2,1,0:T(8,128)(2,1)S(1)}, bf16[2,2,128,256]{3,2,1,0:T(8,128)(2,1)S(1)}, u32[]{:S(2)}, u32[]{:S(2)}) collective-permute-start(bf16[2,2,128,256]{3,2,1,0:T(8,128)(2,1)S(1)} %get-tuple-element.81), channel_id=1, source_target_pairs={{0,7},{1,2},{2,1},{3,4},{4,3},{5,6},{6,5},{7,0},{8,15},{9,10},{10,... | collective-permute-start | bytes 786440 | tf_op jit(solution)/shard_map/ppermute | solution.py:532
  4.8 5.9 %collective-permute-start = (bf16[2,2,128,256]{3,2,1,0:T(8,128)(2,1)S(1)}, bf16[2,2,128,256]{3,2,1,0:T(8,128)(2,1)S(1)}, u32[]{:S(2)}, u32[]{:S(2)}) collective-permute-start(bf16[2,2,128,256]{3,2,1,0:T(8,128)(2,1)S(1)} %get-tuple-element.82), channel_id=1, source_target_pairs={{0,1},{1,0},{2,3},{3,2},{4,5},{5,4},{6,7},{7,6},{8,9},{9,8},{10,11... | collective-permute-start | bytes 786440 | tf_op jit(solution)/shard_map/ppermute | solution.py:533
  7.5 1.0 copy-start
  8.5 1.3 copy-start.2
  12.9 28.5 %copy-start.1 = (bf16[3,3,256,256]{3,2,1,0:T(8,128)(2,1)S(1)}, bf16[3,3,256,256]{3,2,1,0:T(8,128)(2,1)}, u32[]{:S(2)}) copy-start(bf16[3,3,256,256]{3,2,1,0:T(8,128)(2,1)} %weight.1) | copy-start | bytes 3538948
  12.9 28.5 %copy-start.4 = (bf16[2,4,128,256]{3,2,1,0:T(8,128)(2,1)S(1)}, bf16[2,4,128,256]{3,2,1,0:T(8,128)(2,1)}, u32[]{:S(2)}) copy-start(bf16[2,4,128,256]{3,2,1,0:T(8,128)(2,1)} %cot.1) | copy-start | bytes 1572868
  71.7 4.2 %collective-permute-start.2 = (bf16[32,80,256]{2,1,0:T(8,128)(2,1)S(1)}, bf16[32,80,256]{2,1,0:T(8,128)(2,1)S(1)}, u32[]{:S(2)}, u32[]{:S(2)}) collective-permute-start(bf16[32,80,256]{2,1,0:T(8,128)(2,1)S(1)} %get-tuple-element.63), channel_id=1, source_target_pairs={{0,1},{1,0},{2,3},{3,2},{4,5},{5,4},{6,7},{7,6},{8,9},{9,8},{10,11... | collective-permute-start | bytes 3932168 | tf_op jit(solution)/shard_map/ppermute | solution.py:613
  78.6 27.3 %all-to-all-start.4 = ((bf16[64,72,128]{2,1,0:T(8,128)(2,1)}), bf16[64,72,128]{2,1,0:T(8,128)(2,1)S(1)}, u32[]{:S(2)}, u32[]{:S(2)}) async-start(bf16[64,72,128]{2,1,0:T(8,128)(2,1)} %bitcast.2), calls=%async_computation.4 | async-start | bytes 2359296 | tf_op jit(solution)/shard_map/all_to_all | solution.py:538
  85.9 21.3 %collective-permute-start.3 = (bf16[2,2,128,256]{3,2,1,0:T(8,128)(2,1)}, bf16[2,2,128,256]{3,2,1,0:T(8,128)(2,1)}, u32[]{:S(2)}, u32[]{:S(2)}) collective-permute-start(bf16[2,2,128,256]{3,2,1,0:T(8,128)(2,1)} %get-tuple-element.65), channel_id=1, source_target_pairs={{0,1},{1,0},{2,3},{3,2},{4,5},{5,4},{6,7},{7,6},{8,9},{9,8},{10,11... | collective-permute-start | bytes 786440 | tf_op jit(solution)/shard_map/ppermute | solution.py:533
  86.0 21.2 %collective-permute-start.4 = (bf16[2,2,128,256]{3,2,1,0:T(8,128)(2,1)S(1)}, bf16[2,2,128,256]{3,2,1,0:T(8,128)(2,1)}, u32[]{:S(2)}, u32[]{:S(2)}) collective-permute-start(bf16[2,2,128,256]{3,2,1,0:T(8,128)(2,1)S(1)} %get-tuple-element.66), channel_id=1, source_target_pairs={{0,7},{1,2},{2,1},{3,4},{4,3},{5,6},{6,5},{7,0},{8,15},{9,10},{10,... | collective-permute-start | bytes 786440 | tf_op jit(solution)/shard_map/ppermute | solution.py:532
  107.2 5.8 %copy-start.3 = (bf16[3,3,256,256]{3,2,1,0:T(8,128)(2,1)S(1)}, bf16[3,3,256,256]{3,2,1,0:T(8,128)(2,1)}, u32[]{:S(2)}) copy-start(bf16[3,3,256,256]{3,2,1,0:T(8,128)(2,1)} %weight_far.1) | copy-start | bytes 3538948
  107.2 25.7 %all-to-all-start.5 = ((bf16[64,80,128]{2,1,0:T(8,128)(2,1)}), bf16[64,80,128]{2,1,0:T(8,128)(2,1)S(1)}, u32[]{:S(2)}, u32[]{:S(2)}) async-start(bf16[64,80,128]{2,1,0:T(8,128)(2,1)} %shard_map.134), calls=%async_computation.5 | async-start | bytes 2621440 | tf_op jit(solution)/shard_map/all_to_all | solution.py:538
  133.0 5.1 %collective-permute-start.5 = (bf16[32,2,80,128]{3,2,1,0:T(8,128)(2,1)S(1)}, bf16[32,2,80,128]{3,2,1,0:T(8,128)(2,1)S(1)}, u32[]{:S(2)}, u32[]{:S(2)}) collective-permute-start(bf16[32,2,80,128]{3,2,1,0:T(8,128)(2,1)S(1)} %bitcast.7), channel_id=1, source_target_pairs={{0,1},{1,0},{2,3},{3,2},{4,5},{5,4},{6,7},{7,6},{8,9},{9,8},{10,11... | collective-permute-start | bytes 3932168 | tf_op jit(solution)/shard_map/ppermute | solution.py:662

commit v7 on v6

--- a/solution.py
+++ b/solution.py
@@ -192,7 +192,7 @@
 
 
 def drive_body(
-    x, from_core, from_chip, weight, table, local, send, flat_edge, above, below, edges
+    x, from_core, from_chip, weight, table, local, send, edges, above, below
 ):
     spot = Spot()
     place_halos(spot, from_core, from_chip, above, below)
@@ -215,7 +215,6 @@
     ).astype(BF)
     edges[:, 0:2] = above[...]
     edges[:, 2:4] = below[...]
-    transpose_rows(edges, flat_edge, 4, lambda t, h: t * 4 + h)
 
 
 def forward_scan_body(got, table, send, block_decays):
@@ -264,7 +263,6 @@
         s1 = local[1, h, :, half] + (d0 * d1)[:, half] * c
         state[1, h, :, half] = s1.astype(BF)
     totals = [jnp.zeros((8, 128), F32) for _ in HALVES]
-    copies = []
     for t in (1, 0):
         pre_act = conv(state[t], weight, False)
         for h, half in blocks(HEIGHT):
@@ -280,7 +278,7 @@
             direct[t, h, :, half] = (table[5:6, half] * g).astype(BF)
             k = HALVES.index(half)
             totals[k] = totals[k] + jnp.sum((g * xt).reshape(WIDTH // 8, 8, 128), axis=0)
-        copies += fetch(sems.at[t], (out.at[t], out_far.at[t]), (direct.at[t], direct_far.at[t]))
+    copies = fetch(sems, (out, out_far), (direct, direct_far))
     grad = spread_conv(gz, weight)
     for t in (1, 0):
         for h, half in blocks(WIDE):
@@ -312,7 +310,8 @@
         yield a, jnp.dot(lhs, rhs, preferred_element_type=F32)
 
 
-def in_grad(adj, flat_mid, flat_edge):
+def in_grad(adj, flat_mid, edges, flat_edge):
+    transpose_rows(edges, flat_edge, 4, lambda t, h: t * 4 + h)
     rhs = adj[...].reshape(FRAMES * WIDE * WIDTH, CHANS)
     for a in range(3):
         pieces = []
@@ -354,8 +353,8 @@
 
 
 def odd_grad_body(
-    scales, local, incoming, state_f, carry, table, skip, flat_mid, flat_edge, message, flat_message,
-    payload, out_part, adj, small, flat,
+    scales, local, incoming, state_f, carry, table, skip, flat_mid, edges, message, flat_message,
+    payload, out_part, adj, small, flat, flat_edge,
 ):
     spot = Spot()
 
@@ -366,15 +365,15 @@
     @pl.when(spot.core == 1)
     def _():
         adjoint_stage(scales, spot, (local, incoming, state_f, carry, table, skip), adj, small)
-        for a, g in in_grad(adj, flat_mid, flat_edge):
+        for a, g in in_grad(adj, flat_mid, edges, flat_edge):
             pack_grad(g, a, scales[0], payload)
         for a, g in out_grad(message.at[:, 0:WIDE], message.at[:, WIDE:], flat):
             pack_grad(g, a, scales[0], out_part)
 
 
 def even_grad_body(
-    scales, local, incoming, state_f, carry, table, skip, flat_mid, flat_edge, odd_adj, odd_small,
-    mine, adj, to_core, to_chip, small,
+    scales, local, incoming, state_f, carry, table, skip, flat_mid, edges, odd_adj, odd_small,
+    mine, adj, to_core, to_chip, small, flat_edge,
 ):
     spot = Spot()
 
@@ -383,7 +382,7 @@
         adjoint_stage(scales, spot, (local, incoming, state_f, carry, table, skip), adj, small)
         to_chip[...] = adj[:, 0:2]
         to_core[...] = adj[:, WIDE - 2 :]
-        for a, g in in_grad(adj, flat_mid, flat_edge):
+        for a, g in in_grad(adj, flat_mid, edges, flat_edge):
             pack_grad(g, a, scales[0], mine)
 
     @pl.when(spot.core == 1)
@@ -491,35 +490,34 @@
 
 
 def unpack_other_body(
-    own, got, out_half, in_half, grad_out, grad_in, rate, skip, step, stage, sems
+    own, got, out_half, in_half, grad_out, grad_in, rate_far, skip_far, step_far,
+    stage, rate, skip, step, sems,
 ):
     del out_half, in_half
     spot = Spot()
-
-    def smalls():
-        total = jnp.zeros((8, 128), F32)
-        for k in range(GROUPS):
-            for lg in range(2):
-                pair = own[k, lg, TAPS:PACK, :].astype(F32) + got[k, lg, TAPS:PACK, :].astype(F32)
-                total = total + pair
-        rate[...] = total[0:2] + total[6:8]
-        skip[...] = total[2:4]
-        steps = total + pltpu.roll(total, 7, 0)
-        step[...] = pltpu.roll(steps, (128 - spot.place * FRAMES) % 128, 1)[4:5, 0:FRAMES]
+    total = jnp.zeros((8, 128), F32)
+    for k in range(GROUPS):
+        for lg in range(2):
+            pair = own[k, lg, TAPS:PACK, :].astype(F32) + got[k, lg, TAPS:PACK, :].astype(F32)
+            total = total + pair
+    rate[...] = total[0:2] + total[6:8]
+    skip[...] = total[2:4]
+    steps = total + pltpu.roll(total, 7, 0)
+    step[...] = pltpu.roll(steps, (128 - spot.place * FRAMES) % 128, 1)[4:5, 0:FRAMES]
+    smalls = fetch(sems.at[9:12], (rate, rate_far), (skip, skip_far), (step, step_far))
 
     @pl.when(spot.core == 0)
     def _():
-        copies = write_grad(got, grad_out, stage, sems)
-        smalls()
-        for copy in copies:
+        for copy in write_grad(got, grad_out, stage, sems):
             copy.wait()
 
     @pl.when(spot.core == 1)
     def _():
-        copies = write_grad(got, grad_in, stage, sems)
-        smalls()
-        for copy in copies:
+        for copy in write_grad(got, grad_in, stage, sems):
             copy.wait()
+
+    for copy in smalls:
+        copy.wait()
 
 
 ROWS_AXES = ("z", "core")
@@ -573,12 +571,12 @@
         2 * ROW_FLOPS,
         [sems(2)],
     )
-    local, send, flat_edge = call(
+    local, send, edges = call(
         drive_body,
-        [sds(wide, F32), sds((BLOCKS, PLACES + NOTE, CHANS), BF), flat],
+        [sds(wide, F32), sds((BLOCKS, PLACES + NOTE, CHANS), BF), sds(field, BF)],
         [x, from_core, from_chip, in_w, table],
         WIDE * ROW_FLOPS,
-        [vmem(edge), vmem(edge), vmem(field)],
+        [vmem(edge), vmem(edge)],
     )
     got = swap(send, TM_AXES)
     send, block_decays = call(forward_scan_body, [chunk, sds((BLOCKS, CHANS), F32)], [got, table])
@@ -596,19 +594,19 @@
         ],
         [local, carry, x, cotangent, out_weight, table],
         (HEIGHT + WIDE) * ROW_FLOPS,
-        [vmem(field), vmem(field), sems(FRAMES, 2)],
+        [vmem(field), vmem(field), sems(2)],
     )
     got = swap(send, TM_AXES)
     (send,) = call(backward_scan_body, [chunk], [got, block_decays])
     incoming = swap(send, TM_AXES)
-    sources = [local_adj, incoming, state_f, carry, table, skip, flat_mid, flat_edge]
+    sources = [local_adj, incoming, state_f, carry, table, skip, flat_mid, edges]
     flat_sent = sent.reshape(GROUPS, PACK, CHANS)
     payload, out_part, odd_adj, odd_small = call(
         functools.partial(odd_grad_body, scales),
         [sds(flat_sent.shape, BF), part, sds(wide, BF), sds((8, 128), BF)],
         [*sources, sent, flat_sent],
         WIDE * ROW_FLOPS,
-        [vmem((3 * CHANS, FRAMES * WIDE * WIDTH))],
+        [vmem((3 * CHANS, FRAMES * WIDE * WIDTH)), vmem(flat.shape)],
     )
     got = lax.ppermute(payload, ROWS_AXES, CORE_PAIRS)
     mine, adj, to_core, to_chip, small = call(
@@ -616,6 +614,7 @@
         [part, sds(wide, BF), sds(edge, BF), sds(edge, BF), sds((8, 128), BF)],
         [*sources, odd_adj, odd_small],
         WIDE * ROW_FLOPS,
+        [vmem(flat.shape)],
     )
     from_core, from_chip = halos(to_core, to_chip)
     (send,) = call(
@@ -668,10 +667,10 @@
     )
     grad_out_weight, grad_in_weight, grad_rates, grad_skip, grad_steps = call(
         unpack_other_body,
-        [far(weights), far(weights), half, half, sds((1, FRAMES), F32)],
+        [far(a) for a in (weights, weights, half, half, sds((1, FRAMES), F32))],
         [own, other, far(grad_out_weight), far(grad_in_weight)],
         0,
-        [stage, sems(9)],
+        [stage, vmem((2, 128), F32), vmem((2, 128), F32), vmem((1, FRAMES), F32), sems(12)],
         {2: 0, 3: 1},
     )
     return (

time: 141 us -> 140 us (level)
    unnamed x10 -> x14, local copies, waits for them, and re-layouts: 2.33 us -> 3.46 us
  transfers between devices with their start and end apart: 8 -> 8, of which waited for: 4 -> 4; matrix products, arithmetic and copies ran while one was open for 1% -> 1% of each run, Pallas kernels for 6% -> 5%
where the time goes in v7:
time: 140 us
  blocking collectives  51.3 us (37%)
  waiting for transfers between devices  37.2 us (27%)
  starting transfers between devices  23.4 us (17%)
  Pallas kernels  21.4 us (15%)
  local copies, waits for them, and re-layouts  4.55 us (3%)
    all_to_all x4, blocking collectives, swap(): return lax.all_to_all(chunks, axes, 0, 0)  51.3 us
    all_to_all x2, waiting for transfers between devices, swap(): return lax.all_to_all(chunks, axes, 0, 0)  33.5 us
    pallas_call x12, Pallas kernels, call(): pl.pallas_call(body, out_shape=[o for o, _ in outs], in_specs=[s for _, s...  21.4 us
    all_to_all x2, starting transfers between devices, swap(): return lax.all_to_all(chunks, axes, 0, 0)  13 us
    ppermute x2, starting transfers between devices, halos(): from_chip = lax.ppermute(to_chip, ROWS_AXES, CHIP_PAIRS)  4.5 us
    unnamed x14, local copies, waits for them, and re-layouts  3.46 us
  transfers between devices with their start and end apart: 8, of which 4 were waited for; matrix products, arithmetic and copies ran while one was open for 1% of the time, Pallas kernels for 5%

profile of v7, /device:TPU:1, one launch (start us, length us, event | category | flops | bytes accessed | tf_op | source)
XLA Modules:
  0.0 139.6 jit_solution(7591497268489800107)
XLA Ops:
  0.6 1.1 constant_dynamic-slice_fusion
  1.7 3.1 %collective-permute-start.1 = (bf16[2,2,128,256]{3,2,1,0:T(8,128)(2,1)S(1)}, bf16[2,2,128,256]{3,2,1,0:T(8,128)(2,1)S(1)}, u32[]{:S(2)}, u32[]{:S(2)}) collective-permute-start(bf16[2,2,128,256]{3,2,1,0:T(8,128)(2,1)S(1)} %get-tuple-element.81), channel_id=1, source_target_pairs={{0,7},{1,2},{2,1},{3,4},{4,3},{5,6},{6,5},{7,0},{8,15},{9,10},{10,... | collective-permute-start | bytes 786440 | tf_op jit(solution)/shard_map/ppermute | solution.py:530
  4.8 2.0 %collective-permute-start = (bf16[2,2,128,256]{3,2,1,0:T(8,128)(2,1)S(1)}, bf16[2,2,128,256]{3,2,1,0:T(8,128)(2,1)S(1)}, u32[]{:S(2)}, u32[]{:S(2)}) collective-permute-start(bf16[2,2,128,256]{3,2,1,0:T(8,128)(2,1)S(1)} %get-tuple-element.82), channel_id=1, source_target_pairs={{0,1},{1,0},{2,3},{3,2},{4,5},{5,4},{6,7},{7,6},{8,9},{9,8},{10,11... | collective-permute-start | bytes 786440 | tf_op jit(solution)/shard_map/ppermute | solution.py:531
  6.8 0.7 select_maximum_fusion
  7.5 0.0 copy-start
  7.5 1.0 copy-done
  8.5 0.0 copy-start.2
  8.6 1.3 copy-done.2
  9.8 0.9 shard_map.126
  10.7 0.0 collective-permute-done.1.from_chip
  10.7 0.0 collective-permute-done.from_core
  10.7 2.1 %shard_map.127 = (f32[2,6,128,256]{3,2,1,0:T(8,128)S(1)}, bf16[16,56,256]{2,1,0:T(8,128)(2,1)S(1)}, bf16[2,4,128,256]{3,2,1,0:T(8,128)(2,1)S(1)}) custom-call(bf16[2,4,128,256]{3,2,1,0:T(8,128)(2,1)S(1)} %get-tuple-element.44.x, bf16[2,2,128,256]{3,2,1,0:T(8,128)(2,1)S(1)} %collective-permute-done.from_core, ...), custom_call_target="tpu_custom_call" | custom-call | flops 1811939328 | bytes 4792320 | tf_op jit(solution)/shard_map/pallas_call | solution.py:34
  12.8 0.0 copy-start.1
  12.8 0.0 copy-start.4
  12.9 16.3 %all_to_all.30.got = bf16[16,56,256]{2,1,0:T(8,128)(2,1)S(1)} all-to-all(bf16[16,56,256]{2,1,0:T(8,128)(2,1)S(1)} %get-tuple-element.48), channel_id=1, replica_groups=mesh['x'=4,'y'=4,'z'=4,'core'=2] {'x','y'}, dimensions={0} | all-to-all | bytes 917504 | tf_op jit(solution)/shard_map/all_to_all | solution.py:536
  29.2 0.1 shard_map.128
  29.3 12.0 %all_to_all.31.carry = bf16[16,48,256]{2,1,0:T(8,128)(2,1)S(1)} all-to-all(bf16[16,48,256]{2,1,0:T(8,128)(2,1)S(1)} %get-tuple-element.49), channel_id=1, replica_groups=mesh['x'=4,'y'=4,'z'=4,'core'=2] {'x','y'}, dimensions={0} | all-to-all | bytes 786432 | tf_op jit(solution)/shard_map/all_to_all | solution.py:536
  41.4 0.0 copy-done.1
  41.4 0.0 copy-done.4
  41.4 3.6 %shard_map.129 = (bf16[2,4,128,256]{3,2,1,0:T(8,128)(2,1)}, bf16[2,4,128,256]{3,2,1,0:T(8,128)(2,1)}, bf16[2,10,128,256]{3,2,1,0:T(8,128)(2,1)S(1)}, f32[6,128,2...) custom-call(f32[2,6,128,256]{3,2,1,0:T(8,128)S(1)} %get-tuple-element, ...), custom_call_target="tpu_custom_call" | custom-call | flops 3019898880 | bytes 9315328 | tf_op jit(solution)/shard_map/pallas_call | solution.py:34
  45.0 11.5 %all_to_all.32.got = bf16[16,48,256]{2,1,0:T(8,128)(2,1)S(1)} all-to-all(bf16[16,48,256]{2,1,0:T(8,128)(2,1)S(1)} %get-tuple-element.52), channel_id=1, replica_groups=mesh['x'=4,'y'=4,'z'=4,'core'=2] {'x','y'}, dimensions={0} | all-to-all | bytes 786432 | tf_op jit(solution)/shard_map/all_to_all | solution.py:536
  56.5 0.1 shard_map.130
  56.6 11.5 %all_to_all.33.incoming = bf16[16,48,256]{2,1,0:T(8,128)(2,1)S(1)} all-to-all(bf16[16,48,256]{2,1,0:T(8,128)(2,1)S(1)} %shard_map.130), channel_id=1, replica_groups=mesh['x'=4,'y'=4,'z'=4,'core'=2] {'x','y'}, dimensions={0} | all-to-all | bytes 786432 | tf_op jit(solution)/shard_map/all_to_all | solution.py:536
  68.0 3.7 %shard_map.131 = (bf16[32,80,256]{2,1,0:T(8,128)(2,1)S(1)}, bf16[32,72,256]{2,1,0:T(8,128)(2,1)S(1)}, bf16[2,6,128,256]{3,2,1,0:T(8,128)(2,1)S(1)}, bf16[8,128]{1,0:T(8,128)(2,1)S(1)}) custom-call(f32[2,6,128,256]{3,2,1,0:T(8,128)S(1)} %get-tuple-element.51.local, bf16[16,48,256]{2,1,0:T(8,128)(2,1)S(1)} %all_to_all.33.incoming, ...), custom_call_target="tpu_custom_call" | custom-call | flops 1811939328 | bytes 11152384 | tf_op jit(solution)/shard_map/pallas_call | solution.py:34
  71.7 1.4 %collective-permute-start.2 = (bf16[32,80,256]{2,1,0:T(8,128)(2,1)S(1)}, bf16[32,80,256]{2,1,0:T(8,128)(2,1)S(1)}, u32[]{:S(2)}, u32[]{:S(2)}) collective-permute-start(bf16[32,80,256]{2,1,0:T(8,128)(2,1)S(1)} %get-tuple-element.63), channel_id=1, source_target_pairs={{0,1},{1,0},{2,3},{3,2},{4,5},{5,4},{6,7},{7,6},{8,9},{9,8},{10,11... | collective-permute-start | bytes 3932168 | tf_op jit(solution)/shard_map/ppermute | solution.py:611
  73.2 0.1 shard_map.132
  73.3 0.0 copy-start.5
  73.3 2.6 %collective-permute-done.2.got = bf16[32,80,256]{2,1,0:T(8,128)(2,1)S(1)} collective-permute-done((bf16[32,80,256]{2,1,0:T(8,128)(2,1)S(1)}, bf16[32,80,256]{2,1,0:T(8,128)(2,1)S(1)}, u32[]{:S(2)}, u32[]{:S(2)}) %collective-permute-start.2) | collective-permute-done | bytes 1310752 | tf_op jit(solution)/shard_map/ppermute | solution.py:611
  75.8 2.6 %shard_map.133 = bf16[32,2,72,128]{3,2,1,0:T(8,128)(2,1)} custom-call(bf16[32,72,256]{2,1,0:T(8,128)(2,1)S(1)} %get-tuple-element.61.mine, bf16[32,72,256]{2,1,0:T(8,128)(2,1)S(1)} %get-tuple-element.62.out_part, bf16[32,80,256]{2,1,0:T(8,128)(2,1)S(1)} %collective-permute-done.2.got, bf16[2,10,128,256]{3,2,1,0:T(8,128)(2,1)S(1)} %bitcast.11), custom_call_target="tpu_custom_call" | custom-call | flops 1207959552 | bytes 6160384 | tf_op jit(solution)/shard_map/pallas_call | solution.py:34
  78.5 0.0 copy-done.5
  78.5 7.3 %all-to-all-start.4 = ((bf16[64,72,128]{2,1,0:T(8,128)(2,1)}), bf16[64,72,128]{2,1,0:T(8,128)(2,1)S(1)}, u32[]{:S(2)}, u32[]{:S(2)}) async-start(bf16[64,72,128]{2,1,0:T(8,128)(2,1)} %bitcast.2), calls=%async_computation.4 | async-start | bytes 2359296 | tf_op jit(solution)/shard_map/all_to_all | solution.py:536
  85.8 0.1 collective-permute-start.3
  85.9 1.4 collective-permute-start.4
  87.3 18.3 %all-to-all-done.4.got = bf16[64,72,128]{2,1,0:T(8,128)(2,1)S(1)} async-done(((bf16[64,72,128]{2,1,0:T(8,128)(2,1)}), bf16[64,72,128]{2,1,0:T(8,128)(2,1)S(1)}, u32[]{:S(2)}, u32[]{:S(2)}) %all-to-all-start.4) | async-done | bytes 1179680 | tf_op jit(solution)/shard_map/all_to_all | solution.py:536
  105.6 1.3 shard_map.134
  107.0 0.0 copy-start.3
  107.0 0.0 collective-permute-done.3.core_far
  107.0 0.0 collective-permute-done.4.chip_far
  107.0 5.7 %all-to-all-start.5 = ((bf16[64,80,128]{2,1,0:T(8,128)(2,1)}), bf16[64,80,128]{2,1,0:T(8,128)(2,1)S(1)}, u32[]{:S(2)}, u32[]{:S(2)}) async-start(bf16[64,80,128]{2,1,0:T(8,128)(2,1)} %shard_map.134), calls=%async_computation.5 | async-start | bytes 2621440 | tf_op jit(solution)/shard_map/all_to_all | solution.py:536
  112.7 0.0 copy-done.3
  112.7 0.0 copy-start.6
  112.7 1.1 copy-done.6
  113.8 3.7 %shard_map.135 = bf16[2,4,128,256]{3,2,1,0:T(8,128)(2,1)} custom-call(bf16[2,6,128,256]{3,2,1,0:T(8,128)(2,1)S(1)} %copy-done.6, bf16[2,2,128,256]{3,2,1,0:T(8,128)(2,1)S(1)} %collective-permute-done.3.core_far, bf16[2,2,128,256]{3,2,1,0:T(8,128)(2,1)S(1)} %collective-permute-done.4.chip_far, ...), custom_call_target="tpu_custom_call", output_to_operand_aliasing={{}: (4, {})} | custom-call | flops 1207959552 | bytes 3538944 | tf_op jit(solution)/shard_map/pallas_call | solution.py:34
  117.5 15.2 %all-to-all-done.5 = bf16[64,80,128]{2,1,0:T(8,128)(2,1)S(1)} async-done(((bf16[64,80,128]{2,1,0:T(8,128)(2,1)}), bf16[64,80,128]{2,1,0:T(8,128)(2,1)S(1)}, u32[]{:S(2)}, u32[]{:S(2)}) %all-to-all-start.5) | async-done | bytes 1310752 | tf_op jit(solution)/shard_map/all_to_all | solution.py:536
  132.7 2.4 %collective-permute-start.5 = (bf16[32,2,80,128]{3,2,1,0:T(8,128)(2,1)S(1)}, bf16[32,2,80,128]{3,2,1,0:T(8,128)(2,1)S(1)}, u32[]{:S(2)}, u32[]{:S(2)}) collective-permute-start(bf16[32,2,80,128]{3,2,1,0:T(8,128)(2,1)S(1)} %bitcast.7), channel_id=1, source_target_pairs={{0,1},{1,0},{2,3},{3,2},{4,5},{5,4},{6,7},{7,6},{8,9},{9,8},{10,11... | collective-permute-start | bytes 3932168 | tf_op jit(solution)/shard_map/ppermute | solution.py:661
  135.1 1.5 %shard_map.136 = (f32[3,3,256,256]{3,2,1,0:T(8,128)}, f32[3,3,256,256]{3,2,1,0:T(8,128)}) custom-call(bf16[32,2,80,128]{3,2,1,0:T(8,128)(2,1)S(1)} %bitcast.8), custom_call_target="tpu_custom_call" | custom-call | bytes 6029312 | tf_op jit(solution)/shard_map/pallas_call | solution.py:34
  136.6 1.2 collective-permute-done.5.got
  137.7 1.7 %shard_map.137 = (f32[3,3,256,256]{3,2,1,0:T(8,128)}, f32[3,3,256,256]{3,2,1,0:T(8,128)}, f32[2,128]{1,0:T(2,128)}, f32[2,128]{1,0:T(2,128)}, f32[1,2]{1,0:T(1,128)}) custom-call(bf16[32,2,80,128]{3,2,1,0:T(8,128)(2,1)S(1)} %bitcast.9, bf16[32,2,80,128]{3,2,1,0:T(8,128)(2,1)S(1)} %collective-permute-done.5.got, ...), custom_call_target="tpu_custom_call", output_to_operand_aliasing={{0}: (2, {}), {1}: (3, {})} | custom-call | bytes 12060680 | tf_op jit(solution)/shard_map/pallas_call | solution.py:34
  (1 shorter events, 0.0 us)
Async XLA Ops:
  1.7 9.0 %collective-permute-start.1 = (bf16[2,2,128,256]{3,2,1,0:T(8,128)(2,1)S(1)}, bf16[2,2,128,256]{3,2,1,0:T(8,128)(2,1)S(1)}, u32[]{:S(2)}, u32[]{:S(2)}) collective-permute-start(bf16[2,2,128,256]{3,2,1,0:T(8,128)(2,1)S(1)} %get-tuple-element.81), channel_id=1, source_target_pairs={{0,7},{1,2},{2,1},{3,4},{4,3},{5,6},{6,5},{7,0},{8,15},{9,10},{10,... | collective-permute-start | bytes 786440 | tf_op jit(solution)/shard_map/ppermute | solution.py:530
  4.8 5.9 %collective-permute-start = (bf16[2,2,128,256]{3,2,1,0:T(8,128)(2,1)S(1)}, bf16[2,2,128,256]{3,2,1,0:T(8,128)(2,1)S(1)}, u32[]{:S(2)}, u32[]{:S(2)}) collective-permute-start(bf16[2,2,128,256]{3,2,1,0:T(8,128)(2,1)S(1)} %get-tuple-element.82), channel_id=1, source_target_pairs={{0,1},{1,0},{2,3},{3,2},{4,5},{5,4},{6,7},{7,6},{8,9},{9,8},{10,11... | collective-permute-start | bytes 786440 | tf_op jit(solution)/shard_map/ppermute | solution.py:531
  7.5 1.0 copy-start
  8.5 1.3 copy-start.2
  12.8 28.5 %copy-start.1 = (bf16[3,3,256,256]{3,2,1,0:T(8,128)(2,1)S(1)}, bf16[3,3,256,256]{3,2,1,0:T(8,128)(2,1)}, u32[]{:S(2)}) copy-start(bf16[3,3,256,256]{3,2,1,0:T(8,128)(2,1)} %weight.1) | copy-start | bytes 3538948
  12.8 28.5 %copy-start.4 = (bf16[2,4,128,256]{3,2,1,0:T(8,128)(2,1)S(1)}, bf16[2,4,128,256]{3,2,1,0:T(8,128)(2,1)}, u32[]{:S(2)}) copy-start(bf16[2,4,128,256]{3,2,1,0:T(8,128)(2,1)} %cot.1) | copy-start | bytes 1572868
  71.7 4.1 %collective-permute-start.2 = (bf16[32,80,256]{2,1,0:T(8,128)(2,1)S(1)}, bf16[32,80,256]{2,1,0:T(8,128)(2,1)S(1)}, u32[]{:S(2)}, u32[]{:S(2)}) collective-permute-start(bf16[32,80,256]{2,1,0:T(8,128)(2,1)S(1)} %get-tuple-element.63), channel_id=1, source_target_pairs={{0,1},{1,0},{2,3},{3,2},{4,5},{5,4},{6,7},{7,6},{8,9},{9,8},{10,11... | collective-permute-start | bytes 3932168 | tf_op jit(solution)/shard_map/ppermute | solution.py:611
  73.3 5.2 %copy-start.5 = (bf16[2,6,128,256]{3,2,1,0:T(8,128)(2,1)}, bf16[2,6,128,256]{3,2,1,0:T(8,128)(2,1)S(1)}, u32[]{:S(2)}) copy-start(bf16[2,6,128,256]{3,2,1,0:T(8,128)(2,1)S(1)} %get-tuple-element.68.adj_far) | copy-start | bytes 2359300
  78.5 27.2 %all-to-all-start.4 = ((bf16[64,72,128]{2,1,0:T(8,128)(2,1)}), bf16[64,72,128]{2,1,0:T(8,128)(2,1)S(1)}, u32[]{:S(2)}, u32[]{:S(2)}) async-start(bf16[64,72,128]{2,1,0:T(8,128)(2,1)} %bitcast.2), calls=%async_computation.4 | async-start | bytes 2359296 | tf_op jit(solution)/shard_map/all_to_all | solution.py:536
  85.8 21.2 %collective-permute-start.3 = (bf16[2,2,128,256]{3,2,1,0:T(8,128)(2,1)S(1)}, bf16[2,2,128,256]{3,2,1,0:T(8,128)(2,1)S(1)}, u32[]{:S(2)}, u32[]{:S(2)}) collective-permute-start(bf16[2,2,128,256]{3,2,1,0:T(8,128)(2,1)S(1)} %get-tuple-element.65), channel_id=1, source_target_pairs={{0,1},{1,0},{2,3},{3,2},{4,5},{5,4},{6,7},{7,6},{8,9},{9,8},{10,11... | collective-permute-start | bytes 786440 | tf_op jit(solution)/shard_map/ppermute | solution.py:531
  85.9 21.1 %collective-permute-start.4 = (bf16[2,2,128,256]{3,2,1,0:T(8,128)(2,1)S(1)}, bf16[2,2,128,256]{3,2,1,0:T(8,128)(2,1)S(1)}, u32[]{:S(2)}, u32[]{:S(2)}) collective-permute-start(bf16[2,2,128,256]{3,2,1,0:T(8,128)(2,1)S(1)} %get-tuple-element.66), channel_id=1, source_target_pairs={{0,7},{1,2},{2,1},{3,4},{4,3},{5,6},{6,5},{7,0},{8,15},{9,10},{10,... | collective-permute-start | bytes 786440 | tf_op jit(solution)/shard_map/ppermute | solution.py:530
  107.0 5.7 %copy-start.3 = (bf16[3,3,256,256]{3,2,1,0:T(8,128)(2,1)S(1)}, bf16[3,3,256,256]{3,2,1,0:T(8,128)(2,1)}, u32[]{:S(2)}) copy-start(bf16[3,3,256,256]{3,2,1,0:T(8,128)(2,1)} %weight_far.1) | copy-start | bytes 3538948
  107.0 25.7 %all-to-all-start.5 = ((bf16[64,80,128]{2,1,0:T(8,128)(2,1)}), bf16[64,80,128]{2,1,0:T(8,128)(2,1)S(1)}, u32[]{:S(2)}, u32[]{:S(2)}) async-start(bf16[64,80,128]{2,1,0:T(8,128)(2,1)} %shard_map.134), calls=%async_computation.5 | async-start | bytes 2621440 | tf_op jit(solution)/shard_map/all_to_all | solution.py:536
  112.7 1.1 copy-start.6
  132.7 5.1 %collective-permute-start.5 = (bf16[32,2,80,128]{3,2,1,0:T(8,128)(2,1)S(1)}, bf16[32,2,80,128]{3,2,1,0:T(8,128)(2,1)S(1)}, u32[]{:S(2)}, u32[]{:S(2)}) collective-permute-start(bf16[32,2,80,128]{3,2,1,0:T(8,128)(2,1)S(1)} %bitcast.7), channel_id=1, source_target_pairs={{0,1},{1,0},{2,3},{3,2},{4,5},{5,4},{6,7},{7,6},{8,9},{9,8},{10,11... | collective-permute-start | bytes 3932168 | tf_op jit(solution)/shard_map/ppermute | solution.py:661

commit v8 on v7

--- a/solution.py
+++ b/solution.py
@@ -27,7 +27,7 @@
     return jax.ShapeDtypeStruct(shape, dtype)
 
 
-def call(body, outs, ins, flops=0, scratch=(), aliases=None):
+def call(body, outs, ins, flops=0, scratch=(), aliases=None, light=False):
     ins = [i if isinstance(i, tuple) else (i, VM) for i in ins]
     outs = [o if isinstance(o, tuple) else (o, VM) for o in outs]
     nbytes = sum(math.prod(a.shape) * a.dtype.itemsize for a, _ in ins + outs)
@@ -39,7 +39,7 @@
         scratch_shapes=list(scratch),
         input_output_aliases=aliases or {},
         compiler_params=pltpu.CompilerParams(vmem_limit_bytes=GRANT),
-        cost_estimate=pl.CostEstimate(flops=flops, bytes_accessed=nbytes, transcendentals=0),
+        cost_estimate=pl.CostEstimate(flops=flops, bytes_accessed=0 if light else nbytes, transcendentals=0),
     )(*[i for i, _ in ins])
 
 
@@ -371,9 +371,9 @@
             pack_grad(g, a, scales[0], out_part)
 
 
-def even_grad_body(
-    scales, local, incoming, state_f, carry, table, skip, flat_mid, edges, odd_adj, odd_small,
-    mine, adj, to_core, to_chip, small, flat_edge,
+def adjoint_body(
+    scales, local, incoming, state_f, carry, table, skip, odd_adj, odd_small,
+    adj, to_core, to_chip, small,
 ):
     spot = Spot()
 
@@ -382,15 +382,20 @@
         adjoint_stage(scales, spot, (local, incoming, state_f, carry, table, skip), adj, small)
         to_chip[...] = adj[:, 0:2]
         to_core[...] = adj[:, WIDE - 2 :]
-        for a, g in in_grad(adj, flat_mid, edges, flat_edge):
-            pack_grad(g, a, scales[0], mine)
 
     @pl.when(spot.core == 1)
     def _():
+        to_core[...] = odd_adj[:, 0:2]
+        to_chip[...] = odd_adj[:, WIDE - 2 :]
         adj[...] = odd_adj[...]
         small[...] = odd_small[...]
-        to_core[...] = odd_adj[:, 0:2]
-        to_chip[...] = odd_adj[:, WIDE - 2 :]
+
+
+def even_grad_body(scale, adj, flat_mid, edges, mine, flat_edge):
+    @pl.when(Spot().core == 0)
+    def _():
+        for a, g in in_grad(adj, flat_mid, edges, flat_edge):
+            pack_grad(g, a, scale, mine)
 
 
 def grad_inputs_body(
@@ -453,15 +458,12 @@
             copy.wait()
 
 
-def all_sum_body(got, small, send_far, send, sems):
+def all_sum_body(got, small, send):
     total = jnp.zeros((TAPS, 128), F32)
     for k in range(CHIPS):
         total = total + got[k].astype(F32)
     total = jnp.concatenate([total.astype(BF), small[...]], axis=0)
     send[...] = jnp.broadcast_to(total[None], send.shape)
-    pairs = [(send, send_far.at[8 * k : 8 * k + 8]) for k in range(8)]
-    for copy in fetch(sems, *pairs):
-        copy.wait()
 
 
 def write_grad(src, grad, stage, sems):
@@ -609,40 +611,38 @@
         [vmem((3 * CHANS, FRAMES * WIDE * WIDTH)), vmem(flat.shape)],
     )
     got = lax.ppermute(payload, ROWS_AXES, CORE_PAIRS)
-    mine, adj, to_core, to_chip, small = call(
-        functools.partial(even_grad_body, scales),
-        [part, sds(wide, BF), sds(edge, BF), sds(edge, BF), sds((8, 128), BF)],
-        [*sources, odd_adj, odd_small],
-        WIDE * ROW_FLOPS,
+    adj, to_core, to_chip, small = call(
+        functools.partial(adjoint_body, scales),
+        [sds(wide, BF), sds(edge, BF), sds(edge, BF), sds((8, 128), BF)],
+        [*sources[:6], odd_adj, odd_small],
+    )
+    from_core, from_chip = halos(to_core, to_chip)
+    (mine,) = call(
+        functools.partial(even_grad_body, scale),
+        [part],
+        [adj, flat_mid, edges],
+        0,
         [vmem(flat.shape)],
-    )
-    from_core, from_chip = halos(to_core, to_chip)
+        light=True,
+    )
     (send,) = call(
         functools.partial(pair_sum_body, scale),
         [far(sds((GROUPS, 2, TAPS, 128), BF))],
         [mine, out_part, got, got.reshape(message)],
-        HEIGHT * ROW_FLOPS,
+        0,
         [
             vmem((GROUPS, 2, TAPS, 128)),
             vmem((3 * CHANS, FRAMES * WIDE * WIDTH)),
             sems(4),
         ],
+        light=True,
     )
     got = swap(send.reshape(CHIPS, TAPS, 128), ("x", "y", "z"))
-    (send,) = call(
-        all_sum_body,
-        [far(sds((CHIPS, PACK, 128), BF))],
-        [got, small],
-        0,
-        [vmem((8, PACK, 128)), sems(8)],
-    )
-    send, from_core, from_chip = lax.optimization_barrier((send, from_core, from_chip))
-    own = swap(send, ("x", "y", "z"))
     (grad_inputs,) = call(
         grad_inputs_body,
         [far(sds(field, BF))],
         [far(a) for a in (adj, from_core, from_chip, in_weight, direct)],
-        HEIGHT * ROW_FLOPS,
+        4000 * ROW_FLOPS,
         [
             vmem(wide),
             vmem(edge),
@@ -656,7 +656,9 @@
         ],
         {4: 0},
     )
-    own, grad_inputs = lax.optimization_barrier((own, grad_inputs))
+    small, grad_inputs = lax.optimization_barrier((small, grad_inputs))
+    (send,) = call(all_sum_body, [sds((CHIPS, PACK, 128), BF)], [got, small])
+    own = swap(send, ("x", "y", "z"))
     own = own.reshape(packed.shape)
     other = lax.ppermute(own, ROWS_AXES, CORE_PAIRS)
     weights = sds(kernel, F32)

time: 140 us -> 139 us (level)
  blocking collectives: 51.3 us -> 75.4 us
  waiting for transfers between devices: 37.2 us -> 18.2 us
  starting transfers between devices: 23.4 us -> 18.2 us
    all_to_all x4 -> x5, blocking collectives: 51.3 us -> 75.4 us  [swap(): return lax.all_to_all(chunks, axes, 0, 0)]
    all_to_all x2 -> x1, waiting for transfers between devices: 33.5 us -> 14.9 us  [swap(): return lax.all_to_all(chunks, axes, 0, 0)]
    all_to_all x2 -> x1, starting transfers between devices: 13 us -> 7.71 us  [swap(): return lax.all_to_all(chunks, axes, 0, 0)]
    unnamed x14 -> x10, local copies, waits for them, and re-layouts: 3.46 us -> 2.33 us
    pallas_call x12 -> x13, Pallas kernels: 21.4 us -> 21.7 us  [call(): pl.pallas_call(body, out_shape=[o for o, _ in outs], in_specs=[s for _, s...]
  transfers between devices with their start and end apart: 8 -> 7, of which waited for: 4 -> 3; matrix products, arithmetic and copies ran while one was open for 1% -> 1% of each run, Pallas kernels for 5% -> 6%
where the time goes in v8:
time: 139 us
  blocking collectives  75.4 us (54%)
  Pallas kernels  21.7 us (16%)
  starting transfers between devices  18.2 us (13%)
  waiting for transfers between devices  18.2 us (13%)
  local copies, waits for them, and re-layouts  3.41 us (2%)
    all_to_all x5, blocking collectives, swap(): return lax.all_to_all(chunks, axes, 0, 0)  75.4 us
    pallas_call x13, Pallas kernels, call(): pl.pallas_call(body, out_shape=[o for o, _ in outs], in_specs=[s for _, s...  21.7 us
    all_to_all x1, waiting for transfers between devices, swap(): return lax.all_to_all(chunks, axes, 0, 0)  14.9 us
    all_to_all x1, starting transfers between devices, swap(): return lax.all_to_all(chunks, axes, 0, 0)  7.71 us
    ppermute x1, starting transfers between devices, on_device(): other = lax.ppermute(own, ROWS_AXES, CORE_PAIRS)  3.55 us
    ppermute x2, starting transfers between devices, halos(): from_chip = lax.ppermute(to_chip, ROWS_AXES, CHIP_PAIRS)  3.11 us
  transfers between devices with their start and end apart: 7, of which 3 were waited for; matrix products, arithmetic and copies ran while one was open for 1% of the time, Pallas kernels for 6%

profile of v8, /device:TPU:1, one launch (start us, length us, event | category | flops | bytes accessed | tf_op | source)
XLA Modules:
  0.0 138.6 jit_solution(10165670078553035070)
XLA Ops:
  0.6 1.1 constant_dynamic-slice_fusion
  1.7 3.1 %collective-permute-start.1 = (bf16[2,2,128,256]{3,2,1,0:T(8,128)(2,1)S(1)}, bf16[2,2,128,256]{3,2,1,0:T(8,128)(2,1)S(1)}, u32[]{:S(2)}, u32[]{:S(2)}) collective-permute-start(bf16[2,2,128,256]{3,2,1,0:T(8,128)(2,1)S(1)} %get-tuple-element.73), channel_id=1, source_target_pairs={{0,7},{1,2},{2,1},{3,4},{4,3},{5,6},{6,5},{7,0},{8,15},{9,10},{10,... | collective-permute-start | bytes 786440 | tf_op jit(solution)/shard_map/ppermute | solution.py:532
  4.8 2.0 %collective-permute-start = (bf16[2,2,128,256]{3,2,1,0:T(8,128)(2,1)S(1)}, bf16[2,2,128,256]{3,2,1,0:T(8,128)(2,1)S(1)}, u32[]{:S(2)}, u32[]{:S(2)}) collective-permute-start(bf16[2,2,128,256]{3,2,1,0:T(8,128)(2,1)S(1)} %get-tuple-element.74), channel_id=1, source_target_pairs={{0,1},{1,0},{2,3},{3,2},{4,5},{5,4},{6,7},{7,6},{8,9},{9,8},{10,11... | collective-permute-start | bytes 786440 | tf_op jit(solution)/shard_map/ppermute | solution.py:533
  6.8 0.7 select_maximum_fusion
  7.5 0.0 copy-start
  7.5 1.0 copy-done
  8.5 0.0 copy-start.2
  8.6 1.3 copy-done.2
  9.8 0.9 shard_map.126
  10.7 0.0 collective-permute-done.1.from_chip
  10.7 0.0 collective-permute-done.from_core
  10.7 2.1 %shard_map.127 = (f32[2,6,128,256]{3,2,1,0:T(8,128)S(1)}, bf16[16,56,256]{2,1,0:T(8,128)(2,1)S(1)}, bf16[2,4,128,256]{3,2,1,0:T(8,128)(2,1)S(1)}) custom-call(bf16[2,4,128,256]{3,2,1,0:T(8,128)(2,1)S(1)} %get-tuple-element.40.x, bf16[2,2,128,256]{3,2,1,0:T(8,128)(2,1)S(1)} %collective-permute-done.from_core, ...), custom_call_target="tpu_custom_call" | custom-call | flops 1811939328 | bytes 4792320 | tf_op jit(solution)/shard_map/pallas_call | solution.py:34
  12.8 0.0 copy-start.1
  12.9 0.0 copy-start.4
  12.9 16.3 %all_to_all.30.got = bf16[16,56,256]{2,1,0:T(8,128)(2,1)S(1)} all-to-all(bf16[16,56,256]{2,1,0:T(8,128)(2,1)S(1)} %get-tuple-element.44), channel_id=1, replica_groups=mesh['x'=4,'y'=4,'z'=4,'core'=2] {'x','y'}, dimensions={0} | all-to-all | bytes 917504 | tf_op jit(solution)/shard_map/all_to_all | solution.py:538
  29.2 0.1 shard_map.128
  29.3 12.0 %all_to_all.31.carry = bf16[16,48,256]{2,1,0:T(8,128)(2,1)S(1)} all-to-all(bf16[16,48,256]{2,1,0:T(8,128)(2,1)S(1)} %get-tuple-element.45), channel_id=1, replica_groups=mesh['x'=4,'y'=4,'z'=4,'core'=2] {'x','y'}, dimensions={0} | all-to-all | bytes 786432 | tf_op jit(solution)/shard_map/all_to_all | solution.py:538
  41.4 0.0 copy-done.1
  41.4 0.0 copy-done.4
  41.4 3.7 %shard_map.129 = (bf16[2,4,128,256]{3,2,1,0:T(8,128)(2,1)}, bf16[2,4,128,256]{3,2,1,0:T(8,128)(2,1)}, bf16[2,10,128,256]{3,2,1,0:T(8,128)(2,1)S(1)}, f32[6,128,2...) custom-call(f32[2,6,128,256]{3,2,1,0:T(8,128)S(1)} %get-tuple-element, ...), custom_call_target="tpu_custom_call" | custom-call | flops 3019898880 | bytes 9315328 | tf_op jit(solution)/shard_map/pallas_call | solution.py:34
  45.1 11.5 %all_to_all.32.got = bf16[16,48,256]{2,1,0:T(8,128)(2,1)S(1)} all-to-all(bf16[16,48,256]{2,1,0:T(8,128)(2,1)S(1)} %get-tuple-element.48), channel_id=1, replica_groups=mesh['x'=4,'y'=4,'z'=4,'core'=2] {'x','y'}, dimensions={0} | all-to-all | bytes 786432 | tf_op jit(solution)/shard_map/all_to_all | solution.py:538
  56.6 0.1 shard_map.130
  56.7 11.5 %all_to_all.33.incoming = bf16[16,48,256]{2,1,0:T(8,128)(2,1)S(1)} all-to-all(bf16[16,48,256]{2,1,0:T(8,128)(2,1)S(1)} %shard_map.130), channel_id=1, replica_groups=mesh['x'=4,'y'=4,'z'=4,'core'=2] {'x','y'}, dimensions={0} | all-to-all | bytes 786432 | tf_op jit(solution)/shard_map/all_to_all | solution.py:538
  68.1 3.7 %shard_map.131 = (bf16[32,80,256]{2,1,0:T(8,128)(2,1)S(1)}, bf16[32,72,256]{2,1,0:T(8,128)(2,1)S(1)}, bf16[2,6,128,256]{3,2,1,0:T(8,128)(2,1)S(1)}, bf16[8,128]{1,0:T(8,128)(2,1)S(1)}) custom-call(f32[2,6,128,256]{3,2,1,0:T(8,128)S(1)} %get-tuple-element.47.local, bf16[16,48,256]{2,1,0:T(8,128)(2,1)S(1)} %all_to_all.33.incoming, ...), custom_call_target="tpu_custom_call" | custom-call | flops 1811939328 | bytes 11152384 | tf_op jit(solution)/shard_map/pallas_call | solution.py:34
  71.8 1.4 %collective-permute-start.4 = (bf16[32,80,256]{2,1,0:T(8,128)(2,1)S(1)}, bf16[32,80,256]{2,1,0:T(8,128)(2,1)S(1)}, u32[]{:S(2)}, u32[]{:S(2)}) collective-permute-start(bf16[32,80,256]{2,1,0:T(8,128)(2,1)S(1)} %get-tuple-element.64), channel_id=1, source_target_pairs={{0,1},{1,0},{2,3},{3,2},{4,5},{5,4},{6,7},{7,6},{8,9},{9,8},{10,11... | collective-permute-start | bytes 3932168 | tf_op jit(solution)/shard_map/ppermute | solution.py:613
  73.3 0.1 shard_map.132
  73.4 0.5 collective-permute-start.2
  73.8 0.0 collective-permute-start.3
  73.8 2.1 %collective-permute-done.4.got = bf16[32,80,256]{2,1,0:T(8,128)(2,1)S(1)} collective-permute-done((bf16[32,80,256]{2,1,0:T(8,128)(2,1)S(1)}, bf16[32,80,256]{2,1,0:T(8,128)(2,1)S(1)}, u32[]{:S(2)}, u32[]{:S(2)}) %collective-permute-start.4) | collective-permute-done | bytes 1310752 | tf_op jit(solution)/shard_map/ppermute | solution.py:613
  75.9 2.6 %shard_map.135 = bf16[32,2,72,128]{3,2,1,0:T(8,128)(2,1)} custom-call(bf16[32,72,256]{2,1,0:T(8,128)(2,1)S(1)} %shard_map.134.mine, bf16[32,72,256]{2,1,0:T(8,128)(2,1)S(1)} %get-tuple-element.63.out_part, bf16[32,80,256]{2,1,0:T(8,128)(2,1)S(1)} %collective-permute-done.4.got, bf16[2,10,128,256]{3,2,1,0:T(8,128)(2,1)S(1)} %bitcast.11), custom_call_target="tpu_custom_call" | custom-call | tf_op jit(solution)/shard_map/pallas_call | solution.py:34
  78.6 0.0 copy-start.3
  78.6 7.7 %all-to-all-start.4 = ((bf16[64,72,128]{2,1,0:T(8,128)(2,1)}), bf16[64,72,128]{2,1,0:T(8,128)(2,1)}, u32[]{:S(2)}, u32[]{:S(2)}) async-start(bf16[64,72,128]{2,1,0:T(8,128)(2,1)} %bitcast.2), calls=%async_computation.4 | async-start | bytes 2359296 | tf_op jit(solution)/shard_map/all_to_all | solution.py:538
  86.3 0.0 collective-permute-done.2.core_far
  86.3 0.0 collective-permute-done.3.chip_far
  86.3 0.0 copy-done.3
  86.3 3.7 %shard_map.133 = bf16[2,4,128,256]{3,2,1,0:T(8,128)(2,1)} custom-call(bf16[2,6,128,256]{3,2,1,0:T(8,128)(2,1)S(1)} %get-tuple-element.58.adj_far.adj, bf16[2,2,128,256]{3,2,1,0:T(8,128)(2,1)S(1)} %collective-permute-done.2.core_far, bf16[2,2,128,256]{3,2,1,0:T(8,128)(2,1)S(1)} %collective-permute-done.3.chip_far, ...), custom_call_target="tpu_custom_call", output_to_operand_aliasing={{}: (4, {})} | custom-call | flops 1207959552000 | bytes 3538944 | tf_op jit(solution)/shard_map/pallas_call | solution.py:34
  90.1 14.9 %all-to-all-done.4.got = bf16[64,72,128]{2,1,0:T(8,128)(2,1)} async-done(((bf16[64,72,128]{2,1,0:T(8,128)(2,1)}), bf16[64,72,128]{2,1,0:T(8,128)(2,1)}, u32[]{:S(2)}, u32[]{:S(2)}) %all-to-all-start.4) | async-done | bytes 1179680 | tf_op jit(solution)/shard_map/all_to_all | solution.py:538
  105.0 1.5 %shard_map.136 = bf16[64,80,128]{2,1,0:T(8,128)(2,1)S(1)} custom-call(bf16[64,72,128]{2,1,0:T(8,128)(2,1)} %all-to-all-done.4.got, bf16[8,128]{1,0:T(8,128)(2,1)S(1)} %get-tuple-element.65.small), custom_call_target="tpu_custom_call" | custom-call | bytes 2492416 | tf_op jit(solution)/shard_map/pallas_call | solution.py:34
  106.5 24.1 %all_to_all.34 = bf16[64,80,128]{2,1,0:T(8,128)(2,1)S(1)} all-to-all(bf16[64,80,128]{2,1,0:T(8,128)(2,1)S(1)} %shard_map.136), channel_id=1, replica_groups=mesh['x'=4,'y'=4,'z'=4,'core'=2] {'x','y','z'}, dimensions={0} | all-to-all | bytes 2621440 | tf_op jit(solution)/shard_map/all_to_all | solution.py:538
  130.6 3.6 %collective-permute-start.5 = (bf16[32,2,80,128]{3,2,1,0:T(8,128)(2,1)S(1)}, bf16[32,2,80,128]{3,2,1,0:T(8,128)(2,1)S(1)}, u32[]{:S(2)}, u32[]{:S(2)}) collective-permute-start(bf16[32,2,80,128]{3,2,1,0:T(8,128)(2,1)S(1)} %bitcast.7), channel_id=1, source_target_pairs={{0,1},{1,0},{2,3},{3,2},{4,5},{5,4},{6,7},{7,6},{8,9},{9,8},{10,11... | collective-permute-start | bytes 3932168 | tf_op jit(solution)/shard_map/ppermute | solution.py:663
  134.2 1.5 %shard_map.137 = (f32[3,3,256,256]{3,2,1,0:T(8,128)}, f32[3,3,256,256]{3,2,1,0:T(8,128)}) custom-call(bf16[32,2,80,128]{3,2,1,0:T(8,128)(2,1)S(1)} %bitcast.8), custom_call_target="tpu_custom_call" | custom-call | bytes 6029312 | tf_op jit(solution)/shard_map/pallas_call | solution.py:34
  135.7 1.2 collective-permute-done.5.got
  136.8 1.7 %shard_map.138 = (f32[3,3,256,256]{3,2,1,0:T(8,128)}, f32[3,3,256,256]{3,2,1,0:T(8,128)}, f32[2,128]{1,0:T(2,128)}, f32[2,128]{1,0:T(2,128)}, f32[1,2]{1,0:T(1,128)}) custom-call(bf16[32,2,80,128]{3,2,1,0:T(8,128)(2,1)S(1)} %bitcast.9, bf16[32,2,80,128]{3,2,1,0:T(8,128)(2,1)S(1)} %collective-permute-done.5.got, ...), custom_call_target="tpu_custom_call", output_to_operand_aliasing={{0}: (2, {}), {1}: (3, {})} | custom-call | bytes 12060680 | tf_op jit(solution)/shard_map/pallas_call | solution.py:34
  (2 shorter events, 0.0 us)
Async XLA Ops:
  1.7 9.0 %collective-permute-start.1 = (bf16[2,2,128,256]{3,2,1,0:T(8,128)(2,1)S(1)}, bf16[2,2,128,256]{3,2,1,0:T(8,128)(2,1)S(1)}, u32[]{:S(2)}, u32[]{:S(2)}) collective-permute-start(bf16[2,2,128,256]{3,2,1,0:T(8,128)(2,1)S(1)} %get-tuple-element.73), channel_id=1, source_target_pairs={{0,7},{1,2},{2,1},{3,4},{4,3},{5,6},{6,5},{7,0},{8,15},{9,10},{10,... | collective-permute-start | bytes 786440 | tf_op jit(solution)/shard_map/ppermute | solution.py:532
  4.8 5.9 %collective-permute-start = (bf16[2,2,128,256]{3,2,1,0:T(8,128)(2,1)S(1)}, bf16[2,2,128,256]{3,2,1,0:T(8,128)(2,1)S(1)}, u32[]{:S(2)}, u32[]{:S(2)}) collective-permute-start(bf16[2,2,128,256]{3,2,1,0:T(8,128)(2,1)S(1)} %get-tuple-element.74), channel_id=1, source_target_pairs={{0,1},{1,0},{2,3},{3,2},{4,5},{5,4},{6,7},{7,6},{8,9},{9,8},{10,11... | collective-permute-start | bytes 786440 | tf_op jit(solution)/shard_map/ppermute | solution.py:533
  7.5 1.0 copy-start
  8.5 1.3 copy-start.2
  12.8 28.5 %copy-start.1 = (bf16[3,3,256,256]{3,2,1,0:T(8,128)(2,1)S(1)}, bf16[3,3,256,256]{3,2,1,0:T(8,128)(2,1)}, u32[]{:S(2)}) copy-start(bf16[3,3,256,256]{3,2,1,0:T(8,128)(2,1)} %weight.1) | copy-start | bytes 3538948
  12.9 28.5 %copy-start.4 = (bf16[2,4,128,256]{3,2,1,0:T(8,128)(2,1)S(1)}, bf16[2,4,128,256]{3,2,1,0:T(8,128)(2,1)}, u32[]{:S(2)}) copy-start(bf16[2,4,128,256]{3,2,1,0:T(8,128)(2,1)} %cot.1) | copy-start | bytes 1572868
  71.8 4.1 %collective-permute-start.4 = (bf16[32,80,256]{2,1,0:T(8,128)(2,1)S(1)}, bf16[32,80,256]{2,1,0:T(8,128)(2,1)S(1)}, u32[]{:S(2)}, u32[]{:S(2)}) collective-permute-start(bf16[32,80,256]{2,1,0:T(8,128)(2,1)S(1)} %get-tuple-element.64), channel_id=1, source_target_pairs={{0,1},{1,0},{2,3},{3,2},{4,5},{5,4},{6,7},{7,6},{8,9},{9,8},{10,11... | collective-permute-start | bytes 3932168 | tf_op jit(solution)/shard_map/ppermute | solution.py:613
  73.4 13.0 %collective-permute-start.2 = (bf16[2,2,128,256]{3,2,1,0:T(8,128)(2,1)S(1)}, bf16[2,2,128,256]{3,2,1,0:T(8,128)(2,1)S(1)}, u32[]{:S(2)}, u32[]{:S(2)}) collective-permute-start(bf16[2,2,128,256]{3,2,1,0:T(8,128)(2,1)S(1)} %get-tuple-element.59), channel_id=1, source_target_pairs={{0,1},{1,0},{2,3},{3,2},{4,5},{5,4},{6,7},{7,6},{8,9},{9,8},{10,11... | collective-permute-start | bytes 786440 | tf_op jit(solution)/shard_map/ppermute | solution.py:533
  73.8 12.5 %collective-permute-start.3 = (bf16[2,2,128,256]{3,2,1,0:T(8,128)(2,1)S(1)}, bf16[2,2,128,256]{3,2,1,0:T(8,128)(2,1)S(1)}, u32[]{:S(2)}, u32[]{:S(2)}) collective-permute-start(bf16[2,2,128,256]{3,2,1,0:T(8,128)(2,1)S(1)} %get-tuple-element.60), channel_id=1, source_target_pairs={{0,7},{1,2},{2,1},{3,4},{4,3},{5,6},{6,5},{7,0},{8,15},{9,10},{10,... | collective-permute-start | bytes 786440 | tf_op jit(solution)/shard_map/ppermute | solution.py:532
  78.6 7.7 %copy-start.3 = (bf16[3,3,256,256]{3,2,1,0:T(8,128)(2,1)S(1)}, bf16[3,3,256,256]{3,2,1,0:T(8,128)(2,1)}, u32[]{:S(2)}) copy-start(bf16[3,3,256,256]{3,2,1,0:T(8,128)(2,1)} %weight_far.1) | copy-start | bytes 3538948
  78.6 26.4 %all-to-all-start.4 = ((bf16[64,72,128]{2,1,0:T(8,128)(2,1)}), bf16[64,72,128]{2,1,0:T(8,128)(2,1)}, u32[]{:S(2)}, u32[]{:S(2)}) async-start(bf16[64,72,128]{2,1,0:T(8,128)(2,1)} %bitcast.2), calls=%async_computation.4 | async-start | bytes 2359296 | tf_op jit(solution)/shard_map/all_to_all | solution.py:538
  130.6 6.2 %collective-permute-start.5 = (bf16[32,2,80,128]{3,2,1,0:T(8,128)(2,1)S(1)}, bf16[32,2,80,128]{3,2,1,0:T(8,128)(2,1)S(1)}, u32[]{:S(2)}, u32[]{:S(2)}) collective-permute-start(bf16[32,2,80,128]{3,2,1,0:T(8,128)(2,1)S(1)} %bitcast.7), channel_id=1, source_target_pairs={{0,1},{1,0},{2,3},{3,2},{4,5},{5,4},{6,7},{7,6},{8,9},{9,8},{10,11... | collective-permute-start | bytes 3932168 | tf_op jit(solution)/shard_map/ppermute | solution.py:663

commit v9 on v8

--- a/solution.py
+++ b/solution.py
@@ -642,7 +642,7 @@
         grad_inputs_body,
         [far(sds(field, BF))],
         [far(a) for a in (adj, from_core, from_chip, in_weight, direct)],
-        4000 * ROW_FLOPS,
+        100 * ROW_FLOPS,
         [
             vmem(wide),
             vmem(edge),

time: 139 us -> 138 us (level)
  transfers between devices with their start and end apart: 7 -> 7, of which waited for: 3 -> 3; matrix products, arithmetic and copies ran while one was open for 1% -> 1% of each run, Pallas kernels for 6% -> 7%
where the time goes in v9:
time: 138 us; the launch traced here: 137 us
  blocking collectives  75.4 us (55%)
  Pallas kernels  21.1 us (15%)
  starting transfers between devices  17.9 us (13%)
  waiting for transfers between devices  17.7 us (13%)
  local copies, waits for them, and re-layouts  3.41 us (2%)
    all_to_all x5, blocking collectives, swap(): return lax.all_to_all(chunks, axes, 0, 0)  75.4 us
    pallas_call x13, Pallas kernels, call(): pl.pallas_call(body, out_shape=[o for o, _ in outs], in_specs=[s for _, s...  21.1 us
    all_to_all x1, waiting for transfers between devices, swap(): return lax.all_to_all(chunks, axes, 0, 0)  15.1 us
    all_to_all x1, starting transfers between devices, swap(): return lax.all_to_all(chunks, axes, 0, 0)  7.48 us
    ppermute x1, starting transfers between devices, on_device(): other = lax.ppermute(own, ROWS_AXES, CORE_PAIRS)  3.55 us
    ppermute x2, starting transfers between devices, halos(): from_chip = lax.ppermute(to_chip, ROWS_AXES, CHIP_PAIRS)  3.11 us
  transfers between devices with their start and end apart: 7, of which 3 were waited for; matrix products, arithmetic and copies ran while one was open for 1% of the time, Pallas kernels for 7%

profile of v9, /device:TPU:1, one launch (start us, length us, event | category | flops | bytes accessed | tf_op | source)
XLA Modules:
  0.0 137.3 jit_solution(10697907255072436863)
XLA Ops:
  0.6 1.1 constant_dynamic-slice_fusion
  1.7 3.1 %collective-permute-start.1 = (bf16[2,2,128,256]{3,2,1,0:T(8,128)(2,1)S(1)}, bf16[2,2,128,256]{3,2,1,0:T(8,128)(2,1)S(1)}, u32[]{:S(2)}, u32[]{:S(2)}) collective-permute-start(bf16[2,2,128,256]{3,2,1,0:T(8,128)(2,1)S(1)} %get-tuple-element.73), channel_id=1, source_target_pairs={{0,7},{1,2},{2,1},{3,4},{4,3},{5,6},{6,5},{7,0},{8,15},{9,10},{10,... | collective-permute-start | bytes 786440 | tf_op jit(solution)/shard_map/ppermute | solution.py:532
  4.8 2.0 %collective-permute-start = (bf16[2,2,128,256]{3,2,1,0:T(8,128)(2,1)S(1)}, bf16[2,2,128,256]{3,2,1,0:T(8,128)(2,1)S(1)}, u32[]{:S(2)}, u32[]{:S(2)}) collective-permute-start(bf16[2,2,128,256]{3,2,1,0:T(8,128)(2,1)S(1)} %get-tuple-element.74), channel_id=1, source_target_pairs={{0,1},{1,0},{2,3},{3,2},{4,5},{5,4},{6,7},{7,6},{8,9},{9,8},{10,11... | collective-permute-start | bytes 786440 | tf_op jit(solution)/shard_map/ppermute | solution.py:533
  6.8 0.7 select_maximum_fusion
  7.5 0.0 copy-start
  7.5 1.0 copy-done
  8.5 0.0 copy-start.2
  8.6 1.3 copy-done.2
  9.8 0.9 shard_map.126
  10.7 0.0 collective-permute-done.1.from_chip
  10.7 0.0 collective-permute-done.from_core
  10.7 2.1 %shard_map.127 = (f32[2,6,128,256]{3,2,1,0:T(8,128)S(1)}, bf16[16,56,256]{2,1,0:T(8,128)(2,1)S(1)}, bf16[2,4,128,256]{3,2,1,0:T(8,128)(2,1)S(1)}) custom-call(bf16[2,4,128,256]{3,2,1,0:T(8,128)(2,1)S(1)} %get-tuple-element.40.x, bf16[2,2,128,256]{3,2,1,0:T(8,128)(2,1)S(1)} %collective-permute-done.from_core, ...), custom_call_target="tpu_custom_call" | custom-call | flops 1811939328 | bytes 4792320 | tf_op jit(solution)/shard_map/pallas_call | solution.py:34
  12.8 0.0 copy-start.1
  12.9 0.0 copy-start.4
  12.9 16.3 %all_to_all.30.got = bf16[16,56,256]{2,1,0:T(8,128)(2,1)S(1)} all-to-all(bf16[16,56,256]{2,1,0:T(8,128)(2,1)S(1)} %get-tuple-element.44), channel_id=1, replica_groups=mesh['x'=4,'y'=4,'z'=4,'core'=2] {'x','y'}, dimensions={0} | all-to-all | bytes 917504 | tf_op jit(solution)/shard_map/all_to_all | solution.py:538
  29.2 0.1 shard_map.128
  29.3 12.0 %all_to_all.31.carry = bf16[16,48,256]{2,1,0:T(8,128)(2,1)S(1)} all-to-all(bf16[16,48,256]{2,1,0:T(8,128)(2,1)S(1)} %get-tuple-element.45), channel_id=1, replica_groups=mesh['x'=4,'y'=4,'z'=4,'core'=2] {'x','y'}, dimensions={0} | all-to-all | bytes 786432 | tf_op jit(solution)/shard_map/all_to_all | solution.py:538
  41.4 0.0 copy-done.1
  41.4 0.0 copy-done.4
  41.4 3.7 %shard_map.129 = (bf16[2,4,128,256]{3,2,1,0:T(8,128)(2,1)}, bf16[2,4,128,256]{3,2,1,0:T(8,128)(2,1)}, bf16[2,10,128,256]{3,2,1,0:T(8,128)(2,1)S(1)}, f32[6,128,2...) custom-call(f32[2,6,128,256]{3,2,1,0:T(8,128)S(1)} %get-tuple-element, ...), custom_call_target="tpu_custom_call" | custom-call | flops 3019898880 | bytes 9315328 | tf_op jit(solution)/shard_map/pallas_call | solution.py:34
  45.1 11.5 %all_to_all.32.got = bf16[16,48,256]{2,1,0:T(8,128)(2,1)S(1)} all-to-all(bf16[16,48,256]{2,1,0:T(8,128)(2,1)S(1)} %get-tuple-element.48), channel_id=1, replica_groups=mesh['x'=4,'y'=4,'z'=4,'core'=2] {'x','y'}, dimensions={0} | all-to-all | bytes 786432 | tf_op jit(solution)/shard_map/all_to_all | solution.py:538
  56.6 0.1 shard_map.130
  56.7 11.5 %all_to_all.33.incoming = bf16[16,48,256]{2,1,0:T(8,128)(2,1)S(1)} all-to-all(bf16[16,48,256]{2,1,0:T(8,128)(2,1)S(1)} %shard_map.130), channel_id=1, replica_groups=mesh['x'=4,'y'=4,'z'=4,'core'=2] {'x','y'}, dimensions={0} | all-to-all | bytes 786432 | tf_op jit(solution)/shard_map/all_to_all | solution.py:538
  68.1 3.7 %shard_map.131 = (bf16[32,80,256]{2,1,0:T(8,128)(2,1)S(1)}, bf16[32,72,256]{2,1,0:T(8,128)(2,1)S(1)}, bf16[2,6,128,256]{3,2,1,0:T(8,128)(2,1)S(1)}, bf16[8,128]{1,0:T(8,128)(2,1)S(1)}) custom-call(f32[2,6,128,256]{3,2,1,0:T(8,128)S(1)} %get-tuple-element.47.local, bf16[16,48,256]{2,1,0:T(8,128)(2,1)S(1)} %all_to_all.33.incoming, ...), custom_call_target="tpu_custom_call" | custom-call | flops 1811939328 | bytes 11152384 | tf_op jit(solution)/shard_map/pallas_call | solution.py:34
  71.8 1.4 %collective-permute-start.4 = (bf16[32,80,256]{2,1,0:T(8,128)(2,1)S(1)}, bf16[32,80,256]{2,1,0:T(8,128)(2,1)S(1)}, u32[]{:S(2)}, u32[]{:S(2)}) collective-permute-start(bf16[32,80,256]{2,1,0:T(8,128)(2,1)S(1)} %get-tuple-element.64), channel_id=1, source_target_pairs={{0,1},{1,0},{2,3},{3,2},{4,5},{5,4},{6,7},{7,6},{8,9},{9,8},{10,11... | collective-permute-start | bytes 3932168 | tf_op jit(solution)/shard_map/ppermute | solution.py:613
  73.3 0.8 shard_map.132
  74.1 0.4 collective-permute-start.2
  74.4 0.0 collective-permute-start.3
  74.4 1.5 %collective-permute-done.4.got = bf16[32,80,256]{2,1,0:T(8,128)(2,1)S(1)} collective-permute-done((bf16[32,80,256]{2,1,0:T(8,128)(2,1)S(1)}, bf16[32,80,256]{2,1,0:T(8,128)(2,1)S(1)}, u32[]{:S(2)}, u32[]{:S(2)}) %collective-permute-start.4) | collective-permute-done | bytes 1310752 | tf_op jit(solution)/shard_map/ppermute | solution.py:613
  75.9 2.6 %shard_map.135 = bf16[32,2,72,128]{3,2,1,0:T(8,128)(2,1)} custom-call(bf16[32,72,256]{2,1,0:T(8,128)(2,1)S(1)} %shard_map.134.mine, bf16[32,72,256]{2,1,0:T(8,128)(2,1)S(1)} %get-tuple-element.63.out_part, bf16[32,80,256]{2,1,0:T(8,128)(2,1)S(1)} %collective-permute-done.4.got, bf16[2,10,128,256]{3,2,1,0:T(8,128)(2,1)S(1)} %bitcast.11), custom_call_target="tpu_custom_call" | custom-call | tf_op jit(solution)/shard_map/pallas_call | solution.py:34
  78.6 0.0 copy-start.3
  78.6 7.5 %all-to-all-start.4 = ((bf16[64,72,128]{2,1,0:T(8,128)(2,1)}), bf16[64,72,128]{2,1,0:T(8,128)(2,1)S(1)}, u32[]{:S(2)}, u32[]{:S(2)}) async-start(bf16[64,72,128]{2,1,0:T(8,128)(2,1)} %bitcast.2), calls=%async_computation.4 | async-start | bytes 2359296 | tf_op jit(solution)/shard_map/all_to_all | solution.py:538
  86.1 0.0 collective-permute-done.2.core_far
  86.1 0.0 collective-permute-done.3.chip_far
  86.1 0.0 copy-done.3
  86.1 3.7 %shard_map.133 = bf16[2,4,128,256]{3,2,1,0:T(8,128)(2,1)} custom-call(bf16[2,6,128,256]{3,2,1,0:T(8,128)(2,1)S(1)} %get-tuple-element.58.adj_far.adj, bf16[2,2,128,256]{3,2,1,0:T(8,128)(2,1)} %collective-permute-done.2.core_far, bf16[2,2,128,256]{3,2,1,0:T(8,128)(2,1)} %collective-permute-done.3.chip_far, ...), custom_call_target="tpu_custom_call", output_to_operand_aliasing={{}: (4, {})} | custom-call | flops 30198988800 | bytes 3538944 | tf_op jit(solution)/shard_map/pallas_call | solution.py:34
  89.8 15.1 %all-to-all-done.4.got = bf16[64,72,128]{2,1,0:T(8,128)(2,1)S(1)} async-done(((bf16[64,72,128]{2,1,0:T(8,128)(2,1)}), bf16[64,72,128]{2,1,0:T(8,128)(2,1)S(1)}, u32[]{:S(2)}, u32[]{:S(2)}) %all-to-all-start.4) | async-done | bytes 1179680 | tf_op jit(solution)/shard_map/all_to_all | solution.py:538
  104.9 0.3 shard_map.136
  105.2 24.1 %all_to_all.34 = bf16[64,80,128]{2,1,0:T(8,128)(2,1)S(1)} all-to-all(bf16[64,80,128]{2,1,0:T(8,128)(2,1)S(1)} %shard_map.136), channel_id=1, replica_groups=mesh['x'=4,'y'=4,'z'=4,'core'=2] {'x','y','z'}, dimensions={0} | all-to-all | bytes 2621440 | tf_op jit(solution)/shard_map/all_to_all | solution.py:538
  129.2 3.5 %collective-permute-start.5 = (bf16[32,2,80,128]{3,2,1,0:T(8,128)(2,1)S(1)}, bf16[32,2,80,128]{3,2,1,0:T(8,128)(2,1)S(1)}, u32[]{:S(2)}, u32[]{:S(2)}) collective-permute-start(bf16[32,2,80,128]{3,2,1,0:T(8,128)(2,1)S(1)} %bitcast.7), channel_id=1, source_target_pairs={{0,1},{1,0},{2,3},{3,2},{4,5},{5,4},{6,7},{7,6},{8,9},{9,8},{10,11... | collective-permute-start | bytes 3932168 | tf_op jit(solution)/shard_map/ppermute | solution.py:663
  132.8 1.5 %shard_map.137 = (f32[3,3,256,256]{3,2,1,0:T(8,128)}, f32[3,3,256,256]{3,2,1,0:T(8,128)}) custom-call(bf16[32,2,80,128]{3,2,1,0:T(8,128)(2,1)S(1)} %bitcast.8), custom_call_target="tpu_custom_call" | custom-call | bytes 6029312 | tf_op jit(solution)/shard_map/pallas_call | solution.py:34
  134.3 1.2 collective-permute-done.5.got
  135.4 1.7 %shard_map.138 = (f32[3,3,256,256]{3,2,1,0:T(8,128)}, f32[3,3,256,256]{3,2,1,0:T(8,128)}, f32[2,128]{1,0:T(2,128)}, f32[2,128]{1,0:T(2,128)}, f32[1,2]{1,0:T(1,128)}) custom-call(bf16[32,2,80,128]{3,2,1,0:T(8,128)(2,1)S(1)} %bitcast.9, bf16[32,2,80,128]{3,2,1,0:T(8,128)(2,1)S(1)} %collective-permute-done.5.got, ...), custom_call_target="tpu_custom_call", output_to_operand_aliasing={{0}: (2, {}), {1}: (3, {})} | custom-call | bytes 12060680 | tf_op jit(solution)/shard_map/pallas_call | solution.py:34
  (2 shorter events, 0.0 us)
Async XLA Ops:
  1.7 9.0 %collective-permute-start.1 = (bf16[2,2,128,256]{3,2,1,0:T(8,128)(2,1)S(1)}, bf16[2,2,128,256]{3,2,1,0:T(8,128)(2,1)S(1)}, u32[]{:S(2)}, u32[]{:S(2)}) collective-permute-start(bf16[2,2,128,256]{3,2,1,0:T(8,128)(2,1)S(1)} %get-tuple-element.73), channel_id=1, source_target_pairs={{0,7},{1,2},{2,1},{3,4},{4,3},{5,6},{6,5},{7,0},{8,15},{9,10},{10,... | collective-permute-start | bytes 786440 | tf_op jit(solution)/shard_map/ppermute | solution.py:532
  4.8 5.9 %collective-permute-start = (bf16[2,2,128,256]{3,2,1,0:T(8,128)(2,1)S(1)}, bf16[2,2,128,256]{3,2,1,0:T(8,128)(2,1)S(1)}, u32[]{:S(2)}, u32[]{:S(2)}) collective-permute-start(bf16[2,2,128,256]{3,2,1,0:T(8,128)(2,1)S(1)} %get-tuple-element.74), channel_id=1, source_target_pairs={{0,1},{1,0},{2,3},{3,2},{4,5},{5,4},{6,7},{7,6},{8,9},{9,8},{10,11... | collective-permute-start | bytes 786440 | tf_op jit(solution)/shard_map/ppermute | solution.py:533
  7.5 1.0 copy-start
  8.5 1.3 copy-start.2
  12.8 28.5 %copy-start.1 = (bf16[3,3,256,256]{3,2,1,0:T(8,128)(2,1)S(1)}, bf16[3,3,256,256]{3,2,1,0:T(8,128)(2,1)}, u32[]{:S(2)}) copy-start(bf16[3,3,256,256]{3,2,1,0:T(8,128)(2,1)} %weight.1) | copy-start | bytes 3538948
  12.9 28.5 %copy-start.4 = (bf16[2,4,128,256]{3,2,1,0:T(8,128)(2,1)S(1)}, bf16[2,4,128,256]{3,2,1,0:T(8,128)(2,1)}, u32[]{:S(2)}) copy-start(bf16[2,4,128,256]{3,2,1,0:T(8,128)(2,1)} %cot.1) | copy-start | bytes 1572868
  71.8 4.1 %collective-permute-start.4 = (bf16[32,80,256]{2,1,0:T(8,128)(2,1)S(1)}, bf16[32,80,256]{2,1,0:T(8,128)(2,1)S(1)}, u32[]{:S(2)}, u32[]{:S(2)}) collective-permute-start(bf16[32,80,256]{2,1,0:T(8,128)(2,1)S(1)} %get-tuple-element.64), channel_id=1, source_target_pairs={{0,1},{1,0},{2,3},{3,2},{4,5},{5,4},{6,7},{7,6},{8,9},{9,8},{10,11... | collective-permute-start | bytes 3932168 | tf_op jit(solution)/shard_map/ppermute | solution.py:613
  74.1 12.0 %collective-permute-start.2 = (bf16[2,2,128,256]{3,2,1,0:T(8,128)(2,1)}, bf16[2,2,128,256]{3,2,1,0:T(8,128)(2,1)}, u32[]{:S(2)}, u32[]{:S(2)}) collective-permute-start(bf16[2,2,128,256]{3,2,1,0:T(8,128)(2,1)} %get-tuple-element.59), channel_id=1, source_target_pairs={{0,1},{1,0},{2,3},{3,2},{4,5},{5,4},{6,7},{7,6},{8,9},{9,8},{10,11... | collective-permute-start | bytes 786440 | tf_op jit(solution)/shard_map/ppermute | solution.py:533
  74.4 11.6 %collective-permute-start.3 = (bf16[2,2,128,256]{3,2,1,0:T(8,128)(2,1)S(1)}, bf16[2,2,128,256]{3,2,1,0:T(8,128)(2,1)}, u32[]{:S(2)}, u32[]{:S(2)}) collective-permute-start(bf16[2,2,128,256]{3,2,1,0:T(8,128)(2,1)S(1)} %get-tuple-element.60), channel_id=1, source_target_pairs={{0,7},{1,2},{2,1},{3,4},{4,3},{5,6},{6,5},{7,0},{8,15},{9,10},{10,... | collective-permute-start | bytes 786440 | tf_op jit(solution)/shard_map/ppermute | solution.py:532
  78.6 7.5 %copy-start.3 = (bf16[3,3,256,256]{3,2,1,0:T(8,128)(2,1)S(1)}, bf16[3,3,256,256]{3,2,1,0:T(8,128)(2,1)}, u32[]{:S(2)}) copy-start(bf16[3,3,256,256]{3,2,1,0:T(8,128)(2,1)} %weight_far.1) | copy-start | bytes 3538948
  78.6 26.3 %all-to-all-start.4 = ((bf16[64,72,128]{2,1,0:T(8,128)(2,1)}), bf16[64,72,128]{2,1,0:T(8,128)(2,1)S(1)}, u32[]{:S(2)}, u32[]{:S(2)}) async-start(bf16[64,72,128]{2,1,0:T(8,128)(2,1)} %bitcast.2), calls=%async_computation.4 | async-start | bytes 2359296 | tf_op jit(solution)/shard_map/all_to_all | solution.py:538
  129.2 6.2 %collective-permute-start.5 = (bf16[32,2,80,128]{3,2,1,0:T(8,128)(2,1)S(1)}, bf16[32,2,80,128]{3,2,1,0:T(8,128)(2,1)S(1)}, u32[]{:S(2)}, u32[]{:S(2)}) collective-permute-start(bf16[32,2,80,128]{3,2,1,0:T(8,128)(2,1)S(1)} %bitcast.7), channel_id=1, source_target_pairs={{0,1},{1,0},{2,3},{3,2},{4,5},{5,4},{6,7},{7,6},{8,9},{9,8},{10,11... | collective-permute-start | bytes 3932168 | tf_op jit(solution)/shard_map/ppermute | solution.py:663

commit v10 on v9

--- a/solution.py
+++ b/solution.py
@@ -11,7 +11,7 @@
 BF, F32 = jnp.bfloat16, jnp.float32
 VM = pl.BlockSpec(memory_space=pltpu.VMEM)
 HB = pl.BlockSpec(memory_space=pltpu.HBM)
-GRANT = 24 << 20
+GRANT = 16 << 20
 FRAMES, HEIGHT, WIDTH, CHANS = 2, 4, 128, 256
 WIDE, WIDER = HEIGHT + 2, HEIGHT + 4
 BLOCKS = 16

time: 138 us -> 138 us (level)
  no operation moved by 1% of the time
where the time goes in v10:
time: 138 us; the launch traced here: 137 us
  blocking collectives  75.4 us (55%)
  Pallas kernels  21.1 us (15%)
  starting transfers between devices  17.9 us (13%)
  waiting for transfers between devices  17.7 us (13%)
  local copies, waits for them, and re-layouts  3.41 us (2%)
    all_to_all x5, blocking collectives, swap(): return lax.all_to_all(chunks, axes, 0, 0)  75.4 us
    pallas_call x13, Pallas kernels, call(): pl.pallas_call(body, out_shape=[o for o, _ in outs], in_specs=[s for _, s...  21.1 us
    all_to_all x1, waiting for transfers between devices, swap(): return lax.all_to_all(chunks, axes, 0, 0)  15.1 us
    all_to_all x1, starting transfers between devices, swap(): return lax.all_to_all(chunks, axes, 0, 0)  7.48 us
    ppermute x1, starting transfers between devices, on_device(): other = lax.ppermute(own, ROWS_AXES, CORE_PAIRS)  3.55 us
    ppermute x2, starting transfers between devices, halos(): from_chip = lax.ppermute(to_chip, ROWS_AXES, CHIP_PAIRS)  3.11 us
  transfers between devices with their start and end apart: 7, of which 3 were waited for; matrix products, arithmetic and copies ran while one was open for 1% of the time, Pallas kernels for 7%

profile of v10, /device:TPU:1, one launch (start us, length us, event | category | flops | bytes accessed | tf_op | source)
XLA Modules:
  0.0 137.3 jit_solution(15136701164085541550)
XLA Ops:
  0.6 1.1 constant_dynamic-slice_fusion
  1.7 3.1 %collective-permute-start.1 = (bf16[2,2,128,256]{3,2,1,0:T(8,128)(2,1)S(1)}, bf16[2,2,128,256]{3,2,1,0:T(8,128)(2,1)S(1)}, u32[]{:S(2)}, u32[]{:S(2)}) collective-permute-start(bf16[2,2,128,256]{3,2,1,0:T(8,128)(2,1)S(1)} %get-tuple-element.73), channel_id=1, source_target_pairs={{0,7},{1,2},{2,1},{3,4},{4,3},{5,6},{6,5},{7,0},{8,15},{9,10},{10,... | collective-permute-start | bytes 786440 | tf_op jit(solution)/shard_map/ppermute | solution.py:532
  4.8 2.0 %collective-permute-start = (bf16[2,2,128,256]{3,2,1,0:T(8,128)(2,1)S(1)}, bf16[2,2,128,256]{3,2,1,0:T(8,128)(2,1)S(1)}, u32[]{:S(2)}, u32[]{:S(2)}) collective-permute-start(bf16[2,2,128,256]{3,2,1,0:T(8,128)(2,1)S(1)} %get-tuple-element.74), channel_id=1, source_target_pairs={{0,1},{1,0},{2,3},{3,2},{4,5},{5,4},{6,7},{7,6},{8,9},{9,8},{10,11... | collective-permute-start | bytes 786440 | tf_op jit(solution)/shard_map/ppermute | solution.py:533
  6.8 0.7 select_maximum_fusion
  7.5 0.0 copy-start
  7.5 1.0 copy-done
  8.5 0.0 copy-start.2
  8.6 1.3 copy-done.2
  9.8 0.9 shard_map.126
  10.7 0.0 collective-permute-done.1.from_chip
  10.7 0.0 collective-permute-done.from_core
  10.7 2.1 %shard_map.127 = (f32[2,6,128,256]{3,2,1,0:T(8,128)S(1)}, bf16[16,56,256]{2,1,0:T(8,128)(2,1)S(1)}, bf16[2,4,128,256]{3,2,1,0:T(8,128)(2,1)S(1)}) custom-call(bf16[2,4,128,256]{3,2,1,0:T(8,128)(2,1)S(1)} %get-tuple-element.40.x, bf16[2,2,128,256]{3,2,1,0:T(8,128)(2,1)S(1)} %collective-permute-done.from_core, ...), custom_call_target="tpu_custom_call" | custom-call | flops 1811939328 | bytes 4792320 | tf_op jit(solution)/shard_map/pallas_call | solution.py:34
  12.8 0.0 copy-start.1
  12.9 0.0 copy-start.4
  12.9 16.3 %all_to_all.30.got = bf16[16,56,256]{2,1,0:T(8,128)(2,1)S(1)} all-to-all(bf16[16,56,256]{2,1,0:T(8,128)(2,1)S(1)} %get-tuple-element.44), channel_id=1, replica_groups=mesh['x'=4,'y'=4,'z'=4,'core'=2] {'x','y'}, dimensions={0} | all-to-all | bytes 917504 | tf_op jit(solution)/shard_map/all_to_all | solution.py:538
  29.2 0.1 shard_map.128
  29.3 12.0 %all_to_all.31.carry = bf16[16,48,256]{2,1,0:T(8,128)(2,1)S(1)} all-to-all(bf16[16,48,256]{2,1,0:T(8,128)(2,1)S(1)} %get-tuple-element.45), channel_id=1, replica_groups=mesh['x'=4,'y'=4,'z'=4,'core'=2] {'x','y'}, dimensions={0} | all-to-all | bytes 786432 | tf_op jit(solution)/shard_map/all_to_all | solution.py:538
  41.4 0.0 copy-done.1
  41.4 0.0 copy-done.4
  41.4 3.7 %shard_map.129 = (bf16[2,4,128,256]{3,2,1,0:T(8,128)(2,1)}, bf16[2,4,128,256]{3,2,1,0:T(8,128)(2,1)}, bf16[2,10,128,256]{3,2,1,0:T(8,128)(2,1)S(1)}, f32[6,128,2...) custom-call(f32[2,6,128,256]{3,2,1,0:T(8,128)S(1)} %get-tuple-element, ...), custom_call_target="tpu_custom_call" | custom-call | flops 3019898880 | bytes 9315328 | tf_op jit(solution)/shard_map/pallas_call | solution.py:34
  45.1 11.5 %all_to_all.32.got = bf16[16,48,256]{2,1,0:T(8,128)(2,1)S(1)} all-to-all(bf16[16,48,256]{2,1,0:T(8,128)(2,1)S(1)} %get-tuple-element.48), channel_id=1, replica_groups=mesh['x'=4,'y'=4,'z'=4,'core'=2] {'x','y'}, dimensions={0} | all-to-all | bytes 786432 | tf_op jit(solution)/shard_map/all_to_all | solution.py:538
  56.6 0.1 shard_map.130
  56.7 11.5 %all_to_all.33.incoming = bf16[16,48,256]{2,1,0:T(8,128)(2,1)S(1)} all-to-all(bf16[16,48,256]{2,1,0:T(8,128)(2,1)S(1)} %shard_map.130), channel_id=1, replica_groups=mesh['x'=4,'y'=4,'z'=4,'core'=2] {'x','y'}, dimensions={0} | all-to-all | bytes 786432 | tf_op jit(solution)/shard_map/all_to_all | solution.py:538
  68.1 3.7 %shard_map.131 = (bf16[32,80,256]{2,1,0:T(8,128)(2,1)S(1)}, bf16[32,72,256]{2,1,0:T(8,128)(2,1)S(1)}, bf16[2,6,128,256]{3,2,1,0:T(8,128)(2,1)S(1)}, bf16[8,128]{1,0:T(8,128)(2,1)S(1)}) custom-call(f32[2,6,128,256]{3,2,1,0:T(8,128)S(1)} %get-tuple-element.47.local, bf16[16,48,256]{2,1,0:T(8,128)(2,1)S(1)} %all_to_all.33.incoming, ...), custom_call_target="tpu_custom_call" | custom-call | flops 1811939328 | bytes 11152384 | tf_op jit(solution)/shard_map/pallas_call | solution.py:34
  71.8 1.4 %collective-permute-start.4 = (bf16[32,80,256]{2,1,0:T(8,128)(2,1)S(1)}, bf16[32,80,256]{2,1,0:T(8,128)(2,1)S(1)}, u32[]{:S(2)}, u32[]{:S(2)}) collective-permute-start(bf16[32,80,256]{2,1,0:T(8,128)(2,1)S(1)} %get-tuple-element.64), channel_id=1, source_target_pairs={{0,1},{1,0},{2,3},{3,2},{4,5},{5,4},{6,7},{7,6},{8,9},{9,8},{10,11... | collective-permute-start | bytes 3932168 | tf_op jit(solution)/shard_map/ppermute | solution.py:613
  73.3 0.8 shard_map.132
  74.1 0.4 collective-permute-start.2
  74.4 0.0 collective-permute-start.3
  74.4 1.5 %collective-permute-done.4.got = bf16[32,80,256]{2,1,0:T(8,128)(2,1)S(1)} collective-permute-done((bf16[32,80,256]{2,1,0:T(8,128)(2,1)S(1)}, bf16[32,80,256]{2,1,0:T(8,128)(2,1)S(1)}, u32[]{:S(2)}, u32[]{:S(2)}) %collective-permute-start.4) | collective-permute-done | bytes 1310752 | tf_op jit(solution)/shard_map/ppermute | solution.py:613
  75.9 2.6 %shard_map.135 = bf16[32,2,72,128]{3,2,1,0:T(8,128)(2,1)} custom-call(bf16[32,72,256]{2,1,0:T(8,128)(2,1)S(1)} %shard_map.134.mine, bf16[32,72,256]{2,1,0:T(8,128)(2,1)S(1)} %get-tuple-element.63.out_part, bf16[32,80,256]{2,1,0:T(8,128)(2,1)S(1)} %collective-permute-done.4.got, bf16[2,10,128,256]{3,2,1,0:T(8,128)(2,1)S(1)} %bitcast.11), custom_call_target="tpu_custom_call" | custom-call | tf_op jit(solution)/shard_map/pallas_call | solution.py:34
  78.6 0.0 copy-start.3
  78.6 7.5 %all-to-all-start.4 = ((bf16[64,72,128]{2,1,0:T(8,128)(2,1)}), bf16[64,72,128]{2,1,0:T(8,128)(2,1)S(1)}, u32[]{:S(2)}, u32[]{:S(2)}) async-start(bf16[64,72,128]{2,1,0:T(8,128)(2,1)} %bitcast.2), calls=%async_computation.4 | async-start | bytes 2359296 | tf_op jit(solution)/shard_map/all_to_all | solution.py:538
  86.1 0.0 collective-permute-done.2.core_far
  86.1 0.0 collective-permute-done.3.chip_far
  86.1 0.0 copy-done.3
  86.1 3.7 %shard_map.133 = bf16[2,4,128,256]{3,2,1,0:T(8,128)(2,1)} custom-call(bf16[2,6,128,256]{3,2,1,0:T(8,128)(2,1)S(1)} %get-tuple-element.58.adj_far.adj, bf16[2,2,128,256]{3,2,1,0:T(8,128)(2,1)} %collective-permute-done.2.core_far, bf16[2,2,128,256]{3,2,1,0:T(8,128)(2,1)} %collective-permute-done.3.chip_far, ...), custom_call_target="tpu_custom_call", output_to_operand_aliasing={{}: (4, {})} | custom-call | flops 30198988800 | bytes 3538944 | tf_op jit(solution)/shard_map/pallas_call | solution.py:34
  89.8 15.1 %all-to-all-done.4.got = bf16[64,72,128]{2,1,0:T(8,128)(2,1)S(1)} async-done(((bf16[64,72,128]{2,1,0:T(8,128)(2,1)}), bf16[64,72,128]{2,1,0:T(8,128)(2,1)S(1)}, u32[]{:S(2)}, u32[]{:S(2)}) %all-to-all-start.4) | async-done | bytes 1179680 | tf_op jit(solution)/shard_map/all_to_all | solution.py:538
  104.9 0.3 shard_map.136
  105.2 24.1 %all_to_all.34 = bf16[64,80,128]{2,1,0:T(8,128)(2,1)S(1)} all-to-all(bf16[64,80,128]{2,1,0:T(8,128)(2,1)S(1)} %shard_map.136), channel_id=1, replica_groups=mesh['x'=4,'y'=4,'z'=4,'core'=2] {'x','y','z'}, dimensions={0} | all-to-all | bytes 2621440 | tf_op jit(solution)/shard_map/all_to_all | solution.py:538
  129.2 3.5 %collective-permute-start.5 = (bf16[32,2,80,128]{3,2,1,0:T(8,128)(2,1)S(1)}, bf16[32,2,80,128]{3,2,1,0:T(8,128)(2,1)S(1)}, u32[]{:S(2)}, u32[]{:S(2)}) collective-permute-start(bf16[32,2,80,128]{3,2,1,0:T(8,128)(2,1)S(1)} %bitcast.7), channel_id=1, source_target_pairs={{0,1},{1,0},{2,3},{3,2},{4,5},{5,4},{6,7},{7,6},{8,9},{9,8},{10,11... | collective-permute-start | bytes 3932168 | tf_op jit(solution)/shard_map/ppermute | solution.py:663
  132.8 1.5 %shard_map.137 = (f32[3,3,256,256]{3,2,1,0:T(8,128)}, f32[3,3,256,256]{3,2,1,0:T(8,128)}) custom-call(bf16[32,2,80,128]{3,2,1,0:T(8,128)(2,1)S(1)} %bitcast.8), custom_call_target="tpu_custom_call" | custom-call | bytes 6029312 | tf_op jit(solution)/shard_map/pallas_call | solution.py:34
  134.3 1.2 collective-permute-done.5.got
  135.4 1.7 %shard_map.138 = (f32[3,3,256,256]{3,2,1,0:T(8,128)}, f32[3,3,256,256]{3,2,1,0:T(8,128)}, f32[2,128]{1,0:T(2,128)}, f32[2,128]{1,0:T(2,128)}, f32[1,2]{1,0:T(1,128)}) custom-call(bf16[32,2,80,128]{3,2,1,0:T(8,128)(2,1)S(1)} %bitcast.9, bf16[32,2,80,128]{3,2,1,0:T(8,128)(2,1)S(1)} %collective-permute-done.5.got, ...), custom_call_target="tpu_custom_call", output_to_operand_aliasing={{0}: (2, {}), {1}: (3, {})} | custom-call | bytes 12060680 | tf_op jit(solution)/shard_map/pallas_call | solution.py:34
  (2 shorter events, 0.0 us)
Async XLA Ops:
  1.7 9.0 %collective-permute-start.1 = (bf16[2,2,128,256]{3,2,1,0:T(8,128)(2,1)S(1)}, bf16[2,2,128,256]{3,2,1,0:T(8,128)(2,1)S(1)}, u32[]{:S(2)}, u32[]{:S(2)}) collective-permute-start(bf16[2,2,128,256]{3,2,1,0:T(8,128)(2,1)S(1)} %get-tuple-element.73), channel_id=1, source_target_pairs={{0,7},{1,2},{2,1},{3,4},{4,3},{5,6},{6,5},{7,0},{8,15},{9,10},{10,... | collective-permute-start | bytes 786440 | tf_op jit(solution)/shard_map/ppermute | solution.py:532
  4.8 5.9 %collective-permute-start = (bf16[2,2,128,256]{3,2,1,0:T(8,128)(2,1)S(1)}, bf16[2,2,128,256]{3,2,1,0:T(8,128)(2,1)S(1)}, u32[]{:S(2)}, u32[]{:S(2)}) collective-permute-start(bf16[2,2,128,256]{3,2,1,0:T(8,128)(2,1)S(1)} %get-tuple-element.74), channel_id=1, source_target_pairs={{0,1},{1,0},{2,3},{3,2},{4,5},{5,4},{6,7},{7,6},{8,9},{9,8},{10,11... | collective-permute-start | bytes 786440 | tf_op jit(solution)/shard_map/ppermute | solution.py:533
  7.5 1.0 copy-start
  8.5 1.3 copy-start.2
  12.8 28.5 %copy-start.1 = (bf16[3,3,256,256]{3,2,1,0:T(8,128)(2,1)S(1)}, bf16[3,3,256,256]{3,2,1,0:T(8,128)(2,1)}, u32[]{:S(2)}) copy-start(bf16[3,3,256,256]{3,2,1,0:T(8,128)(2,1)} %weight.1) | copy-start | bytes 3538948
  12.9 28.5 %copy-start.4 = (bf16[2,4,128,256]{3,2,1,0:T(8,128)(2,1)S(1)}, bf16[2,4,128,256]{3,2,1,0:T(8,128)(2,1)}, u32[]{:S(2)}) copy-start(bf16[2,4,128,256]{3,2,1,0:T(8,128)(2,1)} %cot.1) | copy-start | bytes 1572868
  71.8 4.1 %collective-permute-start.4 = (bf16[32,80,256]{2,1,0:T(8,128)(2,1)S(1)}, bf16[32,80,256]{2,1,0:T(8,128)(2,1)S(1)}, u32[]{:S(2)}, u32[]{:S(2)}) collective-permute-start(bf16[32,80,256]{2,1,0:T(8,128)(2,1)S(1)} %get-tuple-element.64), channel_id=1, source_target_pairs={{0,1},{1,0},{2,3},{3,2},{4,5},{5,4},{6,7},{7,6},{8,9},{9,8},{10,11... | collective-permute-start | bytes 3932168 | tf_op jit(solution)/shard_map/ppermute | solution.py:613
  74.1 12.0 %collective-permute-start.2 = (bf16[2,2,128,256]{3,2,1,0:T(8,128)(2,1)}, bf16[2,2,128,256]{3,2,1,0:T(8,128)(2,1)}, u32[]{:S(2)}, u32[]{:S(2)}) collective-permute-start(bf16[2,2,128,256]{3,2,1,0:T(8,128)(2,1)} %get-tuple-element.59), channel_id=1, source_target_pairs={{0,1},{1,0},{2,3},{3,2},{4,5},{5,4},{6,7},{7,6},{8,9},{9,8},{10,11... | collective-permute-start | bytes 786440 | tf_op jit(solution)/shard_map/ppermute | solution.py:533
  74.4 11.6 %collective-permute-start.3 = (bf16[2,2,128,256]{3,2,1,0:T(8,128)(2,1)S(1)}, bf16[2,2,128,256]{3,2,1,0:T(8,128)(2,1)}, u32[]{:S(2)}, u32[]{:S(2)}) collective-permute-start(bf16[2,2,128,256]{3,2,1,0:T(8,128)(2,1)S(1)} %get-tuple-element.60), channel_id=1, source_target_pairs={{0,7},{1,2},{2,1},{3,4},{4,3},{5,6},{6,5},{7,0},{8,15},{9,10},{10,... | collective-permute-start | bytes 786440 | tf_op jit(solution)/shard_map/ppermute | solution.py:532
  78.6 7.5 %copy-start.3 = (bf16[3,3,256,256]{3,2,1,0:T(8,128)(2,1)S(1)}, bf16[3,3,256,256]{3,2,1,0:T(8,128)(2,1)}, u32[]{:S(2)}) copy-start(bf16[3,3,256,256]{3,2,1,0:T(8,128)(2,1)} %weight_far.1) | copy-start | bytes 3538948
  78.6 26.3 %all-to-all-start.4 = ((bf16[64,72,128]{2,1,0:T(8,128)(2,1)}), bf16[64,72,128]{2,1,0:T(8,128)(2,1)S(1)}, u32[]{:S(2)}, u32[]{:S(2)}) async-start(bf16[64,72,128]{2,1,0:T(8,128)(2,1)} %bitcast.2), calls=%async_computation.4 | async-start | bytes 2359296 | tf_op jit(solution)/shard_map/all_to_all | solution.py:538
  129.2 6.2 %collective-permute-start.5 = (bf16[32,2,80,128]{3,2,1,0:T(8,128)(2,1)S(1)}, bf16[32,2,80,128]{3,2,1,0:T(8,128)(2,1)S(1)}, u32[]{:S(2)}, u32[]{:S(2)}) collective-permute-start(bf16[32,2,80,128]{3,2,1,0:T(8,128)(2,1)S(1)} %bitcast.7), channel_id=1, source_target_pairs={{0,1},{1,0},{2,3},{3,2},{4,5},{5,4},{6,7},{7,6},{8,9},{9,8},{10,11... | collective-permute-start | bytes 3932168 | tf_op jit(solution)/shard_map/ppermute | solution.py:663
